TPU v7x, 32 devices: a whole 2x2x4 slice. The times are simulated.
32 devices in a mesh: depth: 4 (over z), tile: 8 (over y, x, core).
Axes of the slice: x: 2, y: 2, z: 4, core: 2. Of those that a mesh axis runs over, the one named last changes fastest.
Arguments:
- volume: bfloat16 [512, 64, 1024], P(None, 'depth', 'tile'), may hold values from -6 to 6
- active: int32 [4, 8], P('depth', 'tile'), may hold values 0 or 1
- depth_order: int32 [2, 4], replicated, may hold values from 0 to 3, each once within a row
- light_vector: float32 [2, 3], replicated, may hold values from -4 to 4
- class_gain: float32 [4], replicated, may hold values from 0.5 to 2
- class_bias: float32 [4], replicated, may hold values from -1 to 1
Outputs:
- image: float32 [2, 4, 512, 1024], P(None, None, ('depth', 'tile'))
Inputs may be any that keep to these rules, and one draw needn't show every extreme that they name: Each row of depth_order lists every slab group exactly once; depth_order[v, r] is the group at the r-th place from the eye in view v. `active`: A 0 marks a brick whose voxels are empty.
All inputs are finite; a program needn't handle non-finite values. No bound on the sum of `active` on one device may be relied on, other than what follows from the above.
Results may differ from a plain program's by a relative error of at most 0.0013.
Values may be sent and summed in bfloat16 or wider, within the bound.
No kernel may reach another device: no remote copies, remote signals or barrier semaphores. Data moves between devices by JAX's collectives and lax.ppermute only.
A program may use at most 64 MiB of HBM per device.

v0:
```python
import jax
import jax.numpy as jnp
from jax import lax
from jax.sharding import PartitionSpec as P

row_block = 16


def with_halo(block, sides, width):
    for axis, dim in sides:
        count = lax.axis_size(axis)
        forward = [(i, i + 1) for i in range(count - 1)]
        backward = [(target, source) for source, target in forward]
        low = lax.ppermute(
            lax.slice_in_dim(block, block.shape[dim] - width, None, axis=dim), axis, forward
        )
        high = lax.ppermute(lax.slice_in_dim(block, 0, width, axis=dim), axis, backward)
        block = jnp.concatenate([low, block, high], axis=dim)
    return block


def as_sent(x):

    def short(part):
        return part.astype(jnp.bfloat16) if part.dtype == jnp.float32 else part

    return jax.tree.map(short, x)


def passed_along(x, axis, by):
    devices = lax.axis_size(axis)
    pairs = [(i, i + by) for i in range(devices) if 0 <= i + by < devices]
    return lax.ppermute(x, axis, pairs)


def shear_rows(stacked, offset_step):
    leading = stacked.shape[:-2]
    slices, columns = stacked.shape[-2:]
    period = 2 * columns + offset_step
    widths = [(0, 0)] * (len(leading) + 1) + [(0, period - columns)]
    padded = jnp.pad(stacked, widths)
    flattened = padded.reshape(leading + (slices * period,))
    trimmed = flattened[..., : slices * 2 * columns]
    return trimmed.reshape(leading + (slices, 2 * columns))


def shade_block(block, weight_on, light_vector, class_gain, class_bias, total_z, views):
    field = block.astype(jnp.float32)
    center = field[1:-1, :, 1:-1]
    grad_x = 0.5 * (field[1:-1, :, 2:] - field[1:-1, :, :-2])
    grad_y = 0.5 * (field[2:, :, 1:-1] - field[:-2, :, 1:-1])
    zpadded = jnp.pad(center, ((0, 0), (1, 1), (0, 0)))
    grad_z = 0.5 * (zpadded[:, 2:] - zpadded[:, :-2])
    grad_sq = grad_x * grad_x + grad_y * grad_y + grad_z * grad_z
    sigma = weight_on * 2.0 * jax.nn.softplus(class_gain[3] * center + class_bias[3]) / total_z
    tints = [
        jax.nn.sigmoid(class_gain[channel] * center + class_bias[channel]) for channel in range(3)
    ]
    slices = center.shape[1]
    columns = center.shape[2]
    results = []
    for view_index in range(views):
        light_x = light_vector[view_index, 0]
        light_y = light_vector[view_index, 1]
        light_z = light_vector[view_index, 2]
        length_sq = light_x * light_x + light_y * light_y + light_z * light_z
        facing = grad_x * light_x + grad_y * light_y + grad_z * light_z
        shade = 0.3 + 0.7 * jnp.abs(facing) / jnp.sqrt(grad_sq * length_sq + 1.0)
        stacked = jnp.stack(
            [sigma * tints[0] * shade, sigma * tints[1] * shade, sigma * tints[2] * shade, sigma]
        )
        sheared = shear_rows(stacked, (view_index + 1) * columns // (2 * slices))
        optical = sheared[3]
        before = jnp.cumsum(optical, axis=1) - optical
        through = jnp.exp(-before)
        colour = jnp.sum(sheared[:3] * through[None], axis=2)
        depth_sum = jnp.sum(optical, axis=1)
        results.append(jnp.concatenate([colour, depth_sum[None]], axis=0))
    return jnp.stack(results)


def footprint(padded_x, weight_on, light_vector, class_gain, class_bias, total_z):
    rows = padded_x.shape[0]
    blocks = rows // row_block
    views = light_vector.shape[0]
    ypadded = jnp.pad(padded_x, ((1, 1), (0, 0), (0, 0)))

    def one_block(block_index):
        block = lax.dynamic_slice_in_dim(ypadded, block_index * row_block, row_block + 2, 0)
        return shade_block(block, weight_on, light_vector, class_gain, class_bias, total_z, views)

    stacked = lax.map(one_block, jnp.arange(blocks, dtype=jnp.int32))
    return jnp.transpose(stacked, (1, 2, 0, 3, 4)).reshape(views, 4, rows, stacked.shape[-1])


def over(front, back, axis):
    front_color = lax.slice_in_dim(front, 0, 3, axis=axis)
    front_depth = lax.slice_in_dim(front, 3, 4, axis=axis)
    back_color = lax.slice_in_dim(back, 0, 3, axis=axis)
    back_depth = lax.slice_in_dim(back, 3, 4, axis=axis)
    return jnp.concatenate(
        [front_color + jnp.exp(-front_depth) * back_color, front_depth + back_depth], axis=axis
    )


def composite(layers, depth_order):
    groups = layers.shape[0]
    group_ids = jnp.arange(groups, dtype=jnp.int32)
    places = jnp.sum(
        jnp.where(depth_order[:, :, None] == group_ids[None, None, :], group_ids[None, :, None], 0),
        axis=1,
    )
    ahead = (places[:, None, :] < places[:, :, None]).astype(jnp.float32)
    depths = layers[:, :, 3]
    front = jnp.einsum("vgh,hvrc->gvrc", ahead, depths, precision=lax.Precision.HIGHEST)
    colour = jnp.sum(layers[:, :, :3] * jnp.exp(-front)[:, :, None], axis=0)
    total = jnp.sum(depths, axis=0)
    return jnp.concatenate([colour, (1.0 - jnp.exp(-total))[:, None]], axis=1)


def local(volume, active, depth_order, light_vector, class_gain, class_bias):
    depth_count = lax.axis_size("depth")
    tile_count = lax.axis_size("tile")
    total_z = volume.shape[1] * depth_count
    width = volume.shape[2]
    rows = volume.shape[0]
    share = rows // (depth_count * tile_count)
    padded_x = with_halo(volume, (("tile", 2),), 1)
    weight_on = active[0, 0].astype(jnp.float32)
    prints = footprint(padded_x, weight_on, light_vector, class_gain, class_bias, total_z)
    views = prints.shape[0]
    channels = prints.shape[1]
    own = prints[..., :width]
    overhang = prints[..., width:]
    arrived = passed_along(as_sent(overhang), "tile", 1).astype(overhang.dtype)
    merged = over(own, arrived, 1)
    received = lax.all_to_all(merged, ("depth", "tile"), split_axis=2, concat_axis=3, tiled=True)
    every = received.reshape(views, channels, share, depth_count, tile_count * width)
    every = jnp.transpose(every, (3, 0, 1, 2, 4))
    return composite(every, depth_order)


def solution(mesh):
    placed = (P(None, "depth", "tile"), P("depth", "tile"), P(), P(), P(), P())
    return jax.shard_map(
        local,
        mesh=mesh,
        in_specs=placed,
        out_specs=P(None, None, ("depth", "tile"), None),
        check_vma=False,
    )
```

profile of v0, /device:TPU:0, one launch (start us, length us, event | category | flops | bytes accessed | tf_op | source)
XLA Modules:
  0.0 667.1 jit_solution(9203687148996721023)
XLA Ops:
  0.0 4.5 fusion.31
  31.0 5.6 fusion.18
  36.7 540.2 %while.12 = (s32[]{:T(128)}, f32[32,2,4,16,256]{4,3,0,2,1:T(8,128)}, f32[]{:T(128)}, f32[4]{0:T(128)S(1)}, s32[32]{0:T(128)S(1)}, /*index=5*/bf16[514,16,130]{2,...) while((s32[]{:T(128)}, ...), condition=%wide.region_7.8_spmd, body=%wide.region_0.7_spmd.sunk | while | flops 7410246 | bytes 26849568 | solution.py:92
  45.2 4.0 multiply_bitcast_fusion.11
  62.1 4.0 multiply_bitcast_fusion.11
  78.9 4.0 multiply_bitcast_fusion.11
  95.8 4.0 multiply_bitcast_fusion.11
  112.7 4.0 multiply_bitcast_fusion.11
  129.6 4.0 multiply_bitcast_fusion.11
  146.4 4.0 multiply_bitcast_fusion.11
  163.3 4.0 multiply_bitcast_fusion.11
  180.2 4.0 multiply_bitcast_fusion.11
  197.1 4.0 multiply_bitcast_fusion.11
  214.0 4.0 multiply_bitcast_fusion.11
  230.8 4.0 multiply_bitcast_fusion.11
  264.6 4.0 multiply_bitcast_fusion.11
  281.5 4.0 multiply_bitcast_fusion.11
  315.3 4.0 multiply_bitcast_fusion.11
  332.2 4.0 multiply_bitcast_fusion.11
  450.4 4.0 multiply_bitcast_fusion.11
  484.1 4.0 multiply_bitcast_fusion.11
  578.7 5.4 collective-permute-start.2
  592.0 18.8 %all-to-all-start = ((f32[2,4,512,128]{3,1,0,2:T(4,128)}), f32[2,4,512,128]{3,1,0,2:T(4,128)S(1)}, u32[]{:S(2)}, u32[]{:S(2)}) async-start(f32[2,4,512,128]{3,1,0,2:T(4,128)} %copy.43), calls=%async_computation | async-start | bytes 4194304 | tf_op jit(solution)/shard_map/all_to_all | solution.py:137
  610.9 48.8 %all-to-all-done = f32[2,4,512,128]{3,1,0,2:T(4,128)S(1)} async-done(((f32[2,4,512,128]{3,1,0,2:T(4,128)}), f32[2,4,512,128]{3,1,0,2:T(4,128)S(1)}, u32[]{:S(2)}, u32[]{:S(2)}) %all-to-all-start) | async-done | bytes 2097184 | tf_op jit(solution)/shard_map/all_to_all | solution.py:137
  (1012 shorter events, 474.0 us)
Async XLA Ops:
  4.5 8.1 %copy-start.3 = (f32[2,3]{1,0:T(2,128)S(1)}, f32[2,3]{1,0:T(2,128)}, u32[]{:S(2)}) copy-start(f32[2,3]{1,0:T(2,128)} %param.11) | copy-start | bytes 76
  7.3 18.0 %collective-permute-start = (bf16[512,16,1]{0,1,2:T(8,128)(2,1)S(1)}, bf16[512,16,1]{0,1,2:T(8,128)(2,1)S(1)}, u32[]{:S(2)}, u32[]{:S(2)}) collective-permute-start(bf16[512,16,1]{0,1,2:T(8,128)(2,1)S(1)} %copy.50), channel_id=1, source_target_pairs={{0,1},{1,2},{2,3},{3,4},{4,5},{5,6},{6,7},{8,9},{9,10},{10,11},{11... | collective-permute-start | bytes 49160 | tf_op jit(solution)/shard_map/ppermute | solution.py:14
  11.3 16.9 %collective-permute-start.1 = (bf16[512,16,1]{0,1,2:T(8,128)(2,1)S(1)}, bf16[512,16,1]{0,1,2:T(8,128)(2,1)S(1)}, u32[]{:S(2)}, u32[]{:S(2)}) collective-permute-start(bf16[512,16,1]{0,1,2:T(8,128)(2,1)S(1)} %copy.51), channel_id=1, source_target_pairs={{1,0},{2,1},{3,2},{4,3},{5,4},{6,5},{7,6},{9,8},{10,9},{11,10},{12... | collective-permute-start | bytes 49160 | tf_op jit(solution)/shard_map/ppermute | solution.py:17
  25.2 5.8 copy-start
  31.0 5.7 copy-start.1
  31.0 5.7 copy-start.2
  578.7 7.4 %collective-permute-start.2 = (bf16[2,4,512,128]{3,2,1,0:T(8,128)(2,1)S(1)}, bf16[2,4,512,128]{3,2,1,0:T(8,128)(2,1)S(1)}, u32[]{:S(2)}, u32[]{:S(2)}) collective-permute-start(bf16[2,4,512,128]{3,2,1,0:T(8,128)(2,1)S(1)} %slice.286), channel_id=1, source_target_pairs={{0,1},{1,2},{2,3},{3,4},{4,5},{5,6},{6,7},{8,9},{9,10},{10,11},{11... | collective-permute-start | bytes 3145736 | tf_op jit(solution)/shard_map/ppermute | solution.py:33
  592.0 18.8 %copy-start.4 = (s32[2,4]{1,0:T(2,128)S(1)}, s32[2,4]{1,0:T(2,128)}, u32[]{:S(2)}) copy-start(s32[2,4]{1,0:T(2,128)} %param.10) | copy-start | bytes 100
  592.0 67.7 %all-to-all-start = ((f32[2,4,512,128]{3,1,0,2:T(4,128)}), f32[2,4,512,128]{3,1,0,2:T(4,128)S(1)}, u32[]{:S(2)}, u32[]{:S(2)}) async-start(f32[2,4,512,128]{3,1,0,2:T(4,128)} %copy.43), calls=%async_computation | async-start | bytes 4194304 | tf_op jit(solution)/shard_map/all_to_all | solution.py:137
where the time goes:
time: 672 us; the launch traced here: 667 us
  other arithmetic  398 us (59%)
  local copies, waits for them, and re-layouts  151 us (22%)
  waiting for transfers between devices  50.8 us (8%)
  starting transfers between devices  27.8 us (4%)
  loops' own time  26.6 us (4%)
  between operations  12.1 us (2%)
    another operation x128, other arithmetic, shade_block(): jnp.stack([sigma * tints[0] * shade, sigma * tints[1] * shade, sigma * ti...  306 us
    all_to_all x1, waiting for transfers between devices, local(): lax.all_to_all(merged, ('depth', 'tile'), split_axis=2, concat_axis=3, ti...  48.8 us
    reshape x64, local copies, waits for them, and re-layouts, shear_rows(): flattened = padded.reshape(leading + (slices * period,))  38.3 us
    convert_element_type x32, other arithmetic, shade_block(): field = block.astype(jnp.float32)  29.9 us
    another operation x1, loops' own time, footprint(): stacked = lax.map(one_block, jnp.arange(blocks, dtype=jnp.int32))  26.6 us
    dynamic_update_slice x32, other arithmetic, footprint(): stacked = lax.map(one_block, jnp.arange(blocks, dtype=jnp.int32))  21.9 us
    slice x32, local copies, waits for them, and re-layouts, shade_block(): class_gain[channel] * center + class_bias[channel]  21.6 us
    while x128, local copies, waits for them, and re-layouts  21.2 us
  transfers between devices with their start and end apart: 4, of which 2 were waited for; matrix products, arithmetic and copies ran while one was open for 1% of the time, Pallas kernels for 0%

commit v1 on v0

v1 whole, which is shorter than its diff:
```python
import functools
import jax
import jax.numpy as jnp
from jax import lax
from jax.experimental import pallas as pl
from jax.experimental.pallas import tpu as pltpu
from jax.sharding import PartitionSpec as P

group = 8


def softplus(u):
    w = jnp.exp(u)
    return jnp.where(w < 0.004, w * (1.0 - 0.5 * w), jnp.log(1.0 + w))


def print_kernel(views, total_z, first_ref, active_ref, light_ref, gain_ref, bias_ref, volume_ref, halo_ref,
                 mix_ref, own_ref, over_ref, field, slope):
    rows = own_ref.shape[2]
    all_rows, slices, columns = volume_ref.shape
    first = first_ref[0]
    mix = mix_ref[...]

    def prepare(block, count, start):
        both = jnp.dot(block.reshape(count * slices, columns), mix, preferred_element_type=jnp.float32)
        at = pl.ds(start, count * slices)
        field[at, :] = both[:, :columns]
        slope[at, :] = both[:, columns:]

    def edge(row, start):
        inside = jnp.logical_and(row >= 0, row < all_rows)
        kept = jnp.clip(row, 0, all_rows - 1)
        block = volume_ref[pl.ds(kept, 1)].astype(jnp.float32)
        field[pl.ds(start, slices), :] = jnp.where(inside, block, 0.0).reshape(slices, columns)

    edge(first - 1, 0)
    edge(first + rows, (rows + 1) * slices)

    def fill(step, carry):
        at = pl.multiple_of(step * group, group)
        block = volume_ref[pl.ds(first + at, group)]
        prepare(block, group, pl.multiple_of((at + 1) * slices, group * slices // 8))
        return carry

    lax.fori_loop(0, rows // group, fill, 0)

    weight = active_ref[0, 0].astype(jnp.float32) * (1.0 / total_z)
    half_gain = [0.5 * gain_ref[k] for k in range(3)]
    half_bias = [0.5 * bias_ref[k] for k in range(3)]
    squares = []
    slants = []
    for v in range(views):
        parts = [light_ref[v, k] for k in range(3)]
        squares.append(0.25 * (parts[0] * parts[0] + parts[1] * parts[1] + parts[2] * parts[2]))
        slants.append([0.35 * part for part in parts])
    lane = lax.broadcasted_iota(jnp.int32, (group, columns), 1)
    rim = jnp.logical_or(lane == 0, lane == columns - 1)
    shears = [(v + 1) * columns // (2 * slices) for v in range(views)]

    def work(step, carry):
        at = pl.multiple_of(step * group, group)
        base = (at + 1) * slices
        halo = halo_ref[pl.ds(pl.multiple_of(first + at, group), group), :]

        def rows_of(ref, z, shift):
            return ref[pl.ds(base + shift * slices + z, group, stride=slices), :]

        zero = jnp.zeros((group, columns), jnp.float32)
        colours = [[zero] * 3 for _ in range(views)]
        before = [zero] * views
        behind = zero
        here = rows_of(field, 0, 0)
        for z in range(slices):
            ahead = rows_of(field, z + 1, 0) if z + 1 < slices else zero
            dy = rows_of(field, z, 1) - rows_of(field, z, -1)
            side = halo if z == 0 else pltpu.roll(halo, columns - 2 * z, 1)
            dx = rows_of(slope, z, 0) + jnp.where(rim, side, 0.0)
            dz = ahead - behind
            steep = dx * dx + dy * dy + dz * dz
            sigma = weight * 2.0 * softplus(gain_ref[3] * here + bias_ref[3])
            half = 0.5 * sigma
            tinted = [half + half * jnp.tanh(half_gain[k] * here + half_bias[k]) for k in range(3)]
            for v in range(views):
                lx, ly, lz = slants[v]
                facing = dx * lx + dy * ly + dz * lz
                shade = 0.3 + jnp.abs(facing) * lax.rsqrt(steep * squares[v] + 1.0)
                by = z * shears[v]
                glow = [part * shade for part in tinted]
                thick = sigma
                if by:
                    glow = [pltpu.roll(part, by, 1) for part in glow]
                    thick = pltpu.roll(sigma, by, 1)
                    crossed = jnp.logical_and(lane >= by - shears[v], lane < by)
                    for k in range(3):
                        pltpu.store(own_ref.at[v, k, pl.ds(at, group), :], colours[v][k], mask=crossed)
                    pltpu.store(own_ref.at[v, 3, pl.ds(at, group), :], before[v], mask=crossed)
                    before[v] = jnp.where(crossed, 0.0, before[v])
                through = jnp.exp(-before[v])
                for k in range(3):
                    colours[v][k] = colours[v][k] + glow[k] * through
                before[v] = before[v] + thick
            behind, here = here, ahead
        for v in range(views):
            whole = lane >= (slices - 1) * shears[v]
            finals = colours[v] + [before[v]]
            for k in range(4):
                row_at = (v, k, pl.ds(at, group), slice(None))
                pltpu.store(own_ref.at[v, k, pl.ds(at, group), :], finals[k], mask=whole)
                rest = finals[k] if k == 3 else finals[k] - own_ref[row_at]
                over_ref[row_at] = jnp.where(whole, 0.0, rest)
        return carry

    lax.fori_loop(0, rows // group, work, 0)


def prints_of(volume, halo, first, rows, active, light_vector, class_gain, class_bias, total_z):
    all_rows, slices, columns = volume.shape
    views = light_vector.shape[0]
    i = jnp.arange(columns)
    eye = (i[:, None] == i[None, :])
    diff = (i[:, None] == i[None, :] + 1).astype(jnp.bfloat16) - (i[:, None] == i[None, :] - 1).astype(jnp.bfloat16)
    mix = jnp.concatenate([eye.astype(jnp.bfloat16), diff], axis=1)
    smem = pl.BlockSpec(memory_space=pltpu.SMEM)
    vmem = pl.BlockSpec(memory_space=pltpu.VMEM)
    shape = jax.ShapeDtypeStruct((views, 4, rows, columns), jnp.float32)
    return pl.pallas_call(
        functools.partial(print_kernel, views, total_z),
        out_shape=[shape, shape],
        in_specs=[smem] * 5 + [vmem] * 3,
        out_specs=[vmem, vmem],
        scratch_shapes=[pltpu.VMEM(((rows + 2) * slices, columns), jnp.float32)] * 2,
        compiler_params=pltpu.CompilerParams(vmem_limit_bytes=40 * 1024 * 1024),
        name="prints",
    )(first, active, light_vector, class_gain, class_bias, volume, halo, mix)


def passed_along(x, axis, by):
    devices = lax.axis_size(axis)
    pairs = [(i, i + by) for i in range(devices) if 0 <= i + by < devices]
    return lax.ppermute(x, axis, pairs)


def halo_rows(volume):
    columns = volume.shape[2]
    left = passed_along(volume[:, :, -1], "tile", 1).astype(jnp.float32)
    right = passed_along(volume[:, :, 0], "tile", -1).astype(jnp.float32)
    woven = jnp.stack([-left, jnp.roll(right, -1, axis=1)], axis=2).reshape(left.shape[0], -1)
    gap = jnp.zeros((left.shape[0], columns - 1 - woven.shape[1]), jnp.float32)
    return jnp.concatenate([woven, gap, right[:, :1]], axis=1)


def over(front, back, axis):
    front_color = lax.slice_in_dim(front, 0, 3, axis=axis)
    front_depth = lax.slice_in_dim(front, 3, 4, axis=axis)
    back_color = lax.slice_in_dim(back, 0, 3, axis=axis)
    back_depth = lax.slice_in_dim(back, 3, 4, axis=axis)
    return jnp.concatenate(
        [front_color + jnp.exp(-front_depth) * back_color, front_depth + back_depth], axis=axis
    )


def composite(layers, depth_order):
    groups = layers.shape[0]
    group_ids = jnp.arange(groups, dtype=jnp.int32)
    places = jnp.sum(
        jnp.where(depth_order[:, :, None] == group_ids[None, None, :], group_ids[None, :, None], 0),
        axis=1,
    )
    ahead = (places[:, None, :] < places[:, :, None]).astype(jnp.float32)
    depths = layers[:, :, 3]
    front = jnp.einsum("vgh,hvrc->gvrc", ahead, depths, precision=lax.Precision.HIGHEST)
    colour = jnp.sum(layers[:, :, :3] * jnp.exp(-front)[:, :, None], axis=0)
    total = jnp.sum(depths, axis=0)
    return jnp.concatenate([colour, (1.0 - jnp.exp(-total))[:, None]], axis=1)


def local(volume, active, depth_order, light_vector, class_gain, class_bias):
    depth_count = lax.axis_size("depth")
    tile_count = lax.axis_size("tile")
    rows, slices, width = volume.shape
    total_z = slices * depth_count
    share = rows // (depth_count * tile_count)
    halo = halo_rows(volume)
    first = jnp.zeros((1,), jnp.int32)
    own, overhang = prints_of(volume, halo, first, rows, active, light_vector, class_gain, class_bias, total_z)
    views, channels = own.shape[:2]
    arrived = passed_along(overhang.astype(jnp.bfloat16), "tile", 1).astype(overhang.dtype)
    merged = over(own, arrived, 1)
    received = lax.all_to_all(merged, ("depth", "tile"), split_axis=2, concat_axis=3, tiled=True)
    every = received.reshape(views, channels, share, depth_count, tile_count * width)
    every = jnp.transpose(every, (3, 0, 1, 2, 4))
    return composite(every, depth_order)


def solution(mesh):
    placed = (P(None, "depth", "tile"), P("depth", "tile"), P(), P(), P(), P())
    return jax.shard_map(
        local,
        mesh=mesh,
        in_specs=placed,
        out_specs=P(None, None, ("depth", "tile"), None),
        check_vma=False,
    )
```

time: 672 us -> 134 us (0.20)
  other arithmetic: 398 us -> 2.61 us
  local copies, waits for them, and re-layouts: 151 us -> 19.2 us
  Pallas kernels: 0 us -> 30.4 us
  loops' own time: 26.6 us -> 0 us
  between operations: 12.1 us -> 0.96 us
    another operation x256 -> x3, other arithmetic: 321 us -> 0.03 us  [halo_rows(): jnp.stack([-left, jnp.roll(right, -1, axis=1)], axis=2)]
    reshape x64 -> x2, local copies, waits for them, and re-layouts: 38.3 us -> 0.17 us  [halo_rows(): jnp.stack([-left, jnp.roll(right, -1, axis=1)], axis=2)]
    slice x195 -> x4, local copies, waits for them, and re-layouts: 36.1 us -> 4.74 us  [the longest x1 4.5 us: halo_rows(): left = passed_along(volume[:, :, -1], 'tile', 1).astype(jnp.float32)]
    pallas_call x0 -> x1, Pallas kernels: none -> 30.4 us  [prints_of(): pl.pallas_call(functools.partial(print_kernel, views, total_z), out_shape...]
    convert_element_type x33 -> x3, other arithmetic: 30.1 us -> 0.31 us  [the longest x1 0.16 us: local(): overhang.astype(jnp.bfloat16)]
    another operation x1 -> x0, loops' own time: 26.6 us -> none  [footprint(): stacked = lax.map(one_block, jnp.arange(blocks, dtype=jnp.int32))]
    dynamic_update_slice x32 -> x0, other arithmetic: 21.9 us -> none  [footprint(): stacked = lax.map(one_block, jnp.arange(blocks, dtype=jnp.int32))]
    while x128 -> x0, local copies, waits for them, and re-layouts: 21.2 us -> none
  transfers between devices with their start and end apart: 4 -> 4, of which waited for: 2 -> 2; matrix products, arithmetic and copies ran while one was open for 1% -> 2% of each run, Pallas kernels for 0% -> 0%
where the time goes in v1:
time: 134 us
  waiting for transfers between devices  51 us (38%)
  Pallas kernels  30.4 us (23%)
  starting transfers between devices  28.8 us (21%)
  local copies, waits for them, and re-layouts  19.2 us (14%)
  other arithmetic  2.61 us (2%)
    all_to_all x1, waiting for transfers between devices, local(): lax.all_to_all(merged, ('depth', 'tile'), split_axis=2, concat_axis=3, ti...  48.8 us
    pallas_call x1, Pallas kernels, prints_of(): pl.pallas_call(functools.partial(print_kernel, views, total_z), out_shape...  30.4 us
    all_to_all x1, starting transfers between devices, local(): lax.all_to_all(merged, ('depth', 'tile'), split_axis=2, concat_axis=3, ti...  19.8 us
    ppermute x3, starting transfers between devices, passed_along(): return lax.ppermute(x, axis, pairs)  8.99 us
    unnamed x13, local copies, waits for them, and re-layouts  6.12 us
    slice x1, local copies, waits for them, and re-layouts, halo_rows(): left = passed_along(volume[:, :, -1], 'tile', 1).astype(jnp.float32)  4.5 us
    concatenate x1, local copies, waits for them, and re-layouts, over(): jnp.concatenate([front_color + jnp.exp(-front_depth) * back_color, front_...  2.69 us
  transfers between devices with their start and end apart: 4, of which 2 were waited for; matrix products, arithmetic and copies ran while one was open for 2% of the time, Pallas kernels for 0%

profile of v1, /device:TPU:0, one launch (start us, length us, event | category | flops | bytes accessed | tf_op | source)
XLA Modules:
  0.0 133.6 jit_solution(6075183830747380631)
XLA Ops:
  0.0 4.5 %fusion.14 = (bf16[512,16,1]{2,1,0:T(8,128)(2,1)S(1)}, bf16[512,16,1]{2,1,0:T(8,128)(2,1)}) fusion(bf16[512,16,128]{2,1,0:T(8,128)(2,1)} %volume_ref.1), kind=kLoop, calls=%fused_computation.36 | loop fusion | bytes 65536 | tf_op jit(solution)/shard_map/slice | solution.py:145
  4.5 4.3 %copy.35 = bf16[512,16,1]{1,0,2:T(8,128)(2,1)S(1)} copy(bf16[512,16,1]{2,1,0:T(8,128)(2,1)} %get-tuple-element.12) | data formatting | bytes 32768
  8.9 1.3 collective-permute-start.1
  10.2 1.6 %copy.34 = bf16[512,16,1]{0,1,2:T(8,128)(2,1)S(1)} copy(bf16[512,16,1]{2,1,0:T(8,128)(2,1)S(1)} %get-tuple-element.11) | data formatting | bytes 32768
  11.8 3.2 %collective-permute-start = (bf16[512,16]{0,1:T(8,128)(2,1)S(1)}, bf16[512,16]{0,1:T(8,128)(2,1)S(1)}, u32[]{:S(2)}, u32[]{:S(2)}) collective-permute-start(bf16[512,16]{0,1:T(8,128)(2,1)S(1)} %bitcast.37), channel_id=1, source_target_pairs={{0,1},{1,2},{2,3},{3,4},{4,5},{5,6},{6,7},{8,9},{9,10},{10,11},{11... | collective-permute-start | bytes 49160 | tf_op jit(solution)/shard_map/ppermute | solution.py:140
  16.0 0.1 slice.43
  16.4 0.1 copy.29
  16.5 0.1 pad_maximum_fusion.2.halo_ref
  16.7 30.4 %prints.1 = (f32[2,4,512,128]{3,2,1,0:T(8,128)S(1)}, f32[2,4,512,128]{3,2,1,0:T(8,128)S(1)}) custom-call(s32[1]{0:T(128)} %constant.1.clone.1.first_ref, s32[1,1]{1,0:T(1,128)S(6)} %copy.39.active_ref, f32[2,3]{1,0:T(2,128)S(1)} %copy-done.1, f32[4]{0:T(128)S(1)} %copy-done.2, f32[4]{0:T(128)S(1)} %copy-done.3, bf16[512,16,128]{2,1,0:T(8,128)(2,1)S(1)} %copy-done, ...), custom_call_target="tpu_custom_call" | custom-call | tf_op jit(solution)/shard_map/prints/pallas_call | solution.py:126
  47.1 0.2 convert_element_type.27
  47.3 4.5 %collective-permute-start.2 = (bf16[2,4,512,128]{3,2,1,0:T(8,128)(2,1)S(1)}, bf16[2,4,512,128]{3,2,1,0:T(8,128)(2,1)S(1)}, u32[]{:S(2)}, u32[]{:S(2)}) collective-permute-start(bf16[2,4,512,128]{3,2,1,0:T(8,128)(2,1)S(1)} %convert_element_type.27), channel_id=1, source_target_pairs={{0,1},{1,2},{2,3},{3,4},{4,5},{5,6},{6,7},{8,9},{9,10},{10,11},{11... | collective-permute-start | bytes 3145736 | tf_op jit(solution)/shard_map/ppermute | solution.py:140
  51.8 2.2 %collective-permute-done.2 = bf16[2,4,512,128]{3,2,1,0:T(8,128)(2,1)S(1)} collective-permute-done((bf16[2,4,512,128]{3,2,1,0:T(8,128)(2,1)S(1)}, bf16[2,4,512,128]{3,2,1,0:T(8,128)(2,1)S(1)}, u32[]{:S(2)}, u32[]{:S(2)}) %collective-permute-start.2) | collective-permute-done | bytes 1048608 | tf_op jit(solution)/shard_map/ppermute | solution.py:140
  54.0 0.1 convert_element_type.28
  54.3 0.3 fusion.1
  54.5 0.1 pad_maximum_fusion
  54.7 2.7 %copy.30 = f32[2,4,512,128]{3,1,0,2:T(4,128)} copy(f32[2,4,512,128]{3,2,1,0:T(8,128)S(1)} %pad_maximum_fusion) | data formatting | bytes 4194304 | tf_op jit(solution)/shard_map/concatenate | solution.py:157
  57.4 19.8 %all-to-all-start = ((f32[2,4,512,128]{3,1,0,2:T(4,128)}), f32[2,4,512,128]{3,1,0,2:T(4,128)S(1)}, u32[]{:S(2)}, u32[]{:S(2)}) async-start(f32[2,4,512,128]{3,1,0,2:T(4,128)} %copy.30), calls=%async_computation | async-start | bytes 4194304 | tf_op jit(solution)/shard_map/all_to_all | solution.py:189
  77.3 48.8 %all-to-all-done = f32[2,4,512,128]{3,1,0,2:T(4,128)S(1)} async-done(((f32[2,4,512,128]{3,1,0,2:T(4,128)}), f32[2,4,512,128]{3,1,0,2:T(4,128)S(1)}, u32[]{:S(2)}, u32[]{:S(2)}) %all-to-all-start) | async-done | bytes 2097184 | tf_op jit(solution)/shard_map/all_to_all | solution.py:189
  126.1 2.6 %copy.38 = f32[2,4,32,16,128]{4,2,3,0,1:T(8,128)} copy(f32[2,4,32,16,128]{4,1,0,3,2:T(4,128)S(1)} %bitcast.34) | data formatting | bytes 4194304 | tf_op jit(solution)/shard_map/all_to_all | solution.py:189
  128.7 1.9 %reshape.39 = f32[2,4,16,4,1024]{4,3,2,0,1:T(4,128)S(1)} reshape(f32[2,4,16,32,128]{4,3,2,0,1:T(8,128)} %bitcast.35) | data formatting | bytes 4194304 | tf_op jit(solution)/shard_map/reshape | solution.py:190
  130.6 0.2 slice_reduce_fusion
  130.9 0.7 fusion.3
  131.6 1.2 fusion
  132.8 0.8 copy.32
  (30 shorter events, 0.8 us)
Async XLA Ops:
  8.9 7.0 %collective-permute-start.1 = (bf16[512,16]{1,0:T(8,128)(2,1)S(1)}, bf16[512,16]{1,0:T(8,128)(2,1)S(1)}, u32[]{:S(2)}, u32[]{:S(2)}) collective-permute-start(bf16[512,16]{1,0:T(8,128)(2,1)S(1)} %bitcast.36), channel_id=1, source_target_pairs={{1,0},{2,1},{3,2},{4,3},{5,4},{6,5},{7,6},{9,8},{10,9},{11,10},{12... | collective-permute-start | bytes 49160 | tf_op jit(solution)/shard_map/ppermute | solution.py:140
  11.8 4.9 %copy-start = (bf16[512,16,128]{2,1,0:T(8,128)(2,1)S(1)}, bf16[512,16,128]{2,1,0:T(8,128)(2,1)}, u32[]{:S(2)}) copy-start(bf16[512,16,128]{2,1,0:T(8,128)(2,1)} %volume_ref.1) | copy-start | bytes 6291460
  11.8 4.8 %copy-start.1 = (f32[2,3]{1,0:T(2,128)S(1)}, f32[2,3]{1,0:T(2,128)}, u32[]{:S(2)}) copy-start(f32[2,3]{1,0:T(2,128)} %light_ref.1) | copy-start | bytes 76
  11.8 4.8 %copy-start.2 = (f32[4]{0:T(128)S(1)}, f32[4]{0:T(128)}, u32[]{:S(2)}) copy-start(f32[4]{0:T(128)} %gain_ref.1) | copy-start | bytes 52
  11.8 4.8 %copy-start.3 = (f32[4]{0:T(128)S(1)}, f32[4]{0:T(128)}, u32[]{:S(2)}) copy-start(f32[4]{0:T(128)} %bias_ref.1) | copy-start | bytes 52
  11.8 4.4 %collective-permute-start = (bf16[512,16]{0,1:T(8,128)(2,1)S(1)}, bf16[512,16]{0,1:T(8,128)(2,1)S(1)}, u32[]{:S(2)}, u32[]{:S(2)}) collective-permute-start(bf16[512,16]{0,1:T(8,128)(2,1)S(1)} %bitcast.37), channel_id=1, source_target_pairs={{0,1},{1,2},{2,3},{3,4},{4,5},{5,6},{6,7},{8,9},{9,10},{10,11},{11... | collective-permute-start | bytes 49160 | tf_op jit(solution)/shard_map/ppermute | solution.py:140
  47.3 6.7 %collective-permute-start.2 = (bf16[2,4,512,128]{3,2,1,0:T(8,128)(2,1)S(1)}, bf16[2,4,512,128]{3,2,1,0:T(8,128)(2,1)S(1)}, u32[]{:S(2)}, u32[]{:S(2)}) collective-permute-start(bf16[2,4,512,128]{3,2,1,0:T(8,128)(2,1)S(1)} %convert_element_type.27), channel_id=1, source_target_pairs={{0,1},{1,2},{2,3},{3,4},{4,5},{5,6},{6,7},{8,9},{9,10},{10,11},{11... | collective-permute-start | bytes 3145736 | tf_op jit(solution)/shard_map/ppermute | solution.py:140
  57.4 19.8 %copy-start.4 = (s32[2,4]{1,0:T(2,128)S(1)}, s32[2,4]{1,0:T(2,128)}, u32[]{:S(2)}) copy-start(s32[2,4]{1,0:T(2,128)} %param.8) | copy-start | bytes 100
  57.4 68.7 %all-to-all-start = ((f32[2,4,512,128]{3,1,0,2:T(4,128)}), f32[2,4,512,128]{3,1,0,2:T(4,128)S(1)}, u32[]{:S(2)}, u32[]{:S(2)}) async-start(f32[2,4,512,128]{3,1,0,2:T(4,128)} %copy.30), calls=%async_computation | async-start | bytes 4194304 | tf_op jit(solution)/shard_map/all_to_all | solution.py:189

commit v2 on v0

v2 whole, which is shorter than its diff:
```python
import functools
import math
import jax
import jax.numpy as jnp
from jax import lax
from jax.experimental import pallas as pl
from jax.experimental.pallas import tpu as pltpu
from jax.sharding import PartitionSpec as P

LN2 = math.log(2.0)
code_step = 1638.0
code_middle = 16.0
code_none = -32768.0

smem = pl.BlockSpec(memory_space=pltpu.SMEM)
vmem = pl.BlockSpec(memory_space=pltpu.VMEM)
params = pltpu.CompilerParams(vmem_limit_bytes=24 * 1024 * 1024)


def encode(x):
    return jnp.round(jnp.maximum(code_step * lax.log2(x) + code_step * code_middle, code_none)).astype(jnp.int16)


def decode(q):
    value = q.astype(jnp.int32).astype(jnp.float32)
    return jnp.where(value == code_none, 0.0, lax.exp2(value * (1.0 / code_step) - code_middle))


def turn_kernel(volume_ref, field_ref, edges_ref, ordered):
    rows, slices, columns = volume_ref.shape
    blocks, _, _, width = field_ref.shape
    blocks = blocks - 2

    def order(index, carry):
        at = pl.multiple_of(index * slices, slices)
        ordered[:, pl.ds(at, slices), :] = jnp.swapaxes(volume_ref[pl.ds(at, slices)], 0, 1)
        return carry

    lax.fori_loop(0, rows // slices, order, 0, unroll=2)
    field_ref[0] = jnp.zeros((slices, columns, width), jnp.float32)
    field_ref[blocks + 1] = jnp.zeros((slices, columns, width), jnp.float32)

    def turn(z, carry):
        for block in range(blocks):
            field_ref[block + 1, z] = ordered[z, block * width:(block + 1) * width, :].T.astype(jnp.float32)
        return carry

    lax.fori_loop(0, slices, turn, 0)
    for side, x in enumerate((0, columns - 1)):
        for block in range(blocks):
            edges_ref[side, :, block * width:(block + 1) * width] = field_ref[block + 1, :, x, :].astype(edges_ref.dtype)


def print_kernel(views, total_z, shift, counts_ref, numbers_ref, field_ref, left_ref, right_ref, own_ref, over_ref, *sums):
    _, slices, columns, width = field_ref.shape
    group = 8
    quad = columns // (2 * slices)
    count = columns // group
    block = lax.rem(counts_ref[0] + shift, field_ref.shape[0] - 2)
    scale = counts_ref[1].astype(jnp.float32) * (-2.0 / total_z)
    light = [[numbers_ref[3 * v + k] for k in range(3)] for v in range(views)]
    gain = [numbers_ref[3 * views + k] for k in range(4)]
    bias = [numbers_ref[3 * views + 4 + k] for k in range(4)]
    half_gain = [0.5 * gain[k] for k in range(3)]
    half_bias = [0.5 * bias[k] for k in range(3)]
    thick_gain = gain[3] * (1.0 / LN2)
    thick_bias = bias[3] * (1.0 / LN2)
    offsets = []
    slants = []
    for v in range(views):
        parts = [jnp.full((group, width), light[v][k], jnp.float32) for k in range(3)]
        square = jnp.maximum(parts[0] * parts[0] + parts[1] * parts[1] + parts[2] * parts[2], 1e-30)
        offsets.append(4.0 / square)
        unit = (0.35 * LN2) * lax.rsqrt(square)
        slants.append([part * unit for part in parts])
    line = lax.broadcasted_iota(jnp.int32, (group, width), 0)
    lane = lax.broadcasted_iota(jnp.int32, (group, width), 1)
    start = lane == 0
    end = lane == width - 1
    for part in sums:
        part[...] = jnp.zeros(part.shape, jnp.float32)
    along = pl.ds(pl.multiple_of(block * width, width), width)
    left = left_ref[:, along].astype(jnp.float32)
    right = right_ref[:, along].astype(jnp.float32)

    def work(j):
        base = j * group if isinstance(j, int) else pl.multiple_of(j * group, group)
        here_rows = pl.ds(base, group)
        fields = [field_ref[block + 1, z, here_rows, :] for z in range(slices)]
        for z in range(slices):
            here = fields[z]
            if isinstance(j, int) and j == 0:
                less = jnp.where(line == 0, left[z:z + 1, :], pltpu.roll(here, 1, 0))
            else:
                less = field_ref[block + 1, z, pl.ds(base - 1, group), :]
            if isinstance(j, int) and j == count - 1:
                more = jnp.where(line == group - 1, right[z:z + 1, :], pltpu.roll(here, group - 1, 0))
            else:
                more = field_ref[block + 1, z, pl.ds(base + 1, group), :]
            dx = more - less
            prior = pltpu.roll(jnp.where(end, field_ref[block, z, here_rows, :], here), 1, 1)
            later = pltpu.roll(jnp.where(start, field_ref[block + 2, z, here_rows, :], here), width - 1, 1)
            dy = later - prior
            if z == 0:
                dz = fields[1]
            elif z == slices - 1:
                dz = -fields[z - 1]
            else:
                dz = fields[z + 1] - fields[z - 1]
            steep = dx * dx + dy * dy + dz * dz
            w = lax.exp2(thick_gain * here + thick_bias)
            thick = scale * jnp.where(w < 0.001, w * (1.0 / LN2 - (0.5 / LN2) * w), lax.log2(1.0 + w))
            tints = [1.0 + jnp.tanh(half_gain[k] * here + half_bias[k]) for k in range(3)]
            for v in range(views):
                place = pl.ds(base + z * (v + 1) * quad, group)
                lx, ly, lz = slants[v]
                facing = dx * lx + dy * ly + dz * lz
                shade = thick * ((-0.15 * LN2) - jnp.abs(facing) * lax.rsqrt(steep + offsets[v]))
                depth = sums[4 * v + 3][place, :]
                sums[4 * v + 3][place, :] = depth + thick
                shade = shade * lax.exp2(depth)
                for k in range(3):
                    sums[4 * v + k][place, :] = sums[4 * v + k][place, :] + tints[k] * shade

    work(count - 1)

    def inner(index, carry):
        work(count - 2 - index)
        return carry

    lax.fori_loop(0, count - 2, inner, 0)
    work(0)
    for v in range(views):
        for k in range(4):
            part = sums[4 * v + k]
            own_ref[v, k] = part[:columns, :]
            rest = part[columns:, :]
            over_ref[v, k] = encode(-rest if k == 3 else rest)


def turn_volume(volume, blocks):
    rows, slices, columns = volume.shape
    return pl.pallas_call(
        turn_kernel,
        out_shape=[jax.ShapeDtypeStruct((blocks + 2, slices, columns, rows // blocks), jnp.float32),
                   jax.ShapeDtypeStruct((2, slices, rows), volume.dtype)],
        in_specs=[vmem], out_specs=[vmem] * 2, scratch_shapes=[pltpu.VMEM((slices, rows, columns), volume.dtype)],
        compiler_params=params, name="turn_rows")(volume)


def merged(own_ref, over_ref, v):
    through = lax.exp2(own_ref[v, 3])
    parts = [own_ref[v, k] + through * decode(over_ref[v, k]) for k in range(3)]
    return parts + [decode(over_ref[v, 3]) - own_ref[v, 3]]


def merge_kernel(views, own_ref, over_ref, layer_ref):
    for v in range(views):
        for k, part in enumerate(merged(own_ref, over_ref, v)):
            layer_ref[v, k] = encode(part)


def final_kernel(views, share, shifts, counts_ref, own_ref, over_ref, *refs):
    layer_refs, image_ref = refs[:-1], refs[-1]
    groups = len(shifts) + 1
    owner = counts_ref[0]
    ids = [owner] + [lax.rem(owner + groups - shift, groups) for shift in shifts]
    for v in range(views):
        order = [counts_ref[2 + v * groups + r] for r in range(groups)]
        places = [sum(jnp.where(order[r] == one, r, 0) for r in range(groups)) for one in ids]
        layers = [merged(own_ref, over_ref, v)] + [[decode(ref[v, k]) for k in range(4)] for ref in layer_refs]
        colours = [0.0] * 3
        total = 0.0
        for g in range(groups):
            front = 0.0
            for h in range(groups):
                if h != g:
                    front = front + layers[h][3] * jnp.where(places[h] < places[g], 1.0, 0.0)
            through = lax.exp2(-front)
            colours = [colours[k] + layers[g][k] * through for k in range(3)]
            total = total + layers[g][3]
        for k, part in enumerate(colours + [1.0 - lax.exp2(-total)]):
            turned = part.T
            for t in range(turned.shape[0] // share):
                block = turned[t * share:(t + 1) * share, :]
                image_ref[t, v, k] = encode(block) if image_ref.dtype == jnp.int16 else block


def place_kernel(blocks_ref, image_ref):
    tiles, views, channels, share, columns = blocks_ref.shape
    for t in range(tiles):
        for v in range(views):
            for k in range(channels):
                block = blocks_ref[t, v, k]
                block = decode(block) if block.dtype == jnp.int16 else block
                image_ref[v, k, :, t * columns:(t + 1) * columns] = block


def prints_of(field, left, right, shift, counts, numbers, views, total_z):
    blocks, slices, columns, width = field.shape
    shape = (views, 4, columns, width)
    return pl.pallas_call(
        functools.partial(print_kernel, views, total_z, shift),
        out_shape=[jax.ShapeDtypeStruct(shape, jnp.float32), jax.ShapeDtypeStruct(shape, jnp.int16)],
        in_specs=[smem] * 2 + [vmem] * 3, out_specs=[vmem] * 2,
        scratch_shapes=[pltpu.VMEM((2 * columns, width), jnp.float32)] * (4 * views),
        cost_estimate=pl.CostEstimate(flops=100 * slices * columns * width, bytes_accessed=12 * 2**20, transcendentals=0),
        compiler_params=params, name="prints")(counts, numbers, field, left, right)


def merge_of(own, over):
    return pl.pallas_call(
        functools.partial(merge_kernel, own.shape[0]), out_shape=jax.ShapeDtypeStruct(own.shape, jnp.int16),
        in_specs=[vmem] * 2, out_specs=vmem, compiler_params=params, name="merge")(own, over)


def final_of(counts, own, over, layers, shifts, share):
    views, channels, columns, width = own.shape
    kind = jnp.int16 if share % 16 == 0 else jnp.float32
    return pl.pallas_call(
        functools.partial(final_kernel, views, share, shifts),
        out_shape=jax.ShapeDtypeStruct((width // share, views, channels, share, columns), kind),
        in_specs=[smem] + [vmem] * (2 + len(layers)), out_specs=vmem, compiler_params=params,
        name="final")(counts, own, over, *layers)


def place_of(blocks):
    tiles, views, channels, share, columns = blocks.shape
    return pl.pallas_call(
        place_kernel, out_shape=jax.ShapeDtypeStruct((views, channels, share, tiles * columns), jnp.float32),
        in_specs=[vmem], out_specs=vmem, compiler_params=params, name="place")(blocks)


def passed_along(x, axis, by):
    devices = lax.axis_size(axis)
    pairs = [(i, i + by) for i in range(devices) if 0 <= i + by < devices]
    return lax.ppermute(x, axis, pairs)


def passed_round(x, axis, by):
    devices = lax.axis_size(axis)
    return lax.ppermute(x, axis, [(i, (i + by) % devices) for i in range(devices)])


def local(volume, active, depth_order, light_vector, class_gain, class_bias):
    depth_count = lax.axis_size("depth")
    tile_count = lax.axis_size("tile")
    rows, slices, columns = volume.shape
    views = light_vector.shape[0]
    total_z = slices * depth_count
    share = rows // (depth_count * tile_count)
    numbers = jnp.concatenate([light_vector.reshape(-1), class_gain, class_bias])
    here = lax.axis_index("depth").astype(jnp.int32)
    counts = jnp.concatenate([here[None], active.reshape(-1), depth_order.reshape(-1)])
    field, edges = turn_volume(volume, depth_count)
    left = passed_along(edges[1], "tile", 1)
    right = passed_along(edges[0], "tile", -1)
    far_first = sorted(range(1, depth_count), key=lambda shift: -min(shift, depth_count - shift))
    layers = []
    for shift in far_first + [0]:
        own, over = prints_of(field, left, right, shift, counts, numbers, views, total_z)
        over = passed_along(over, "tile", 1)
        if shift:
            layers.append(passed_round(merge_of(own, over), "depth", shift))
    blocks = final_of(counts, own, over, layers, far_first, share)
    blocks = lax.all_to_all(blocks, "tile", split_axis=0, concat_axis=0, tiled=True)
    return place_of(blocks)


def solution(mesh):
    placed = (P(None, "depth", "tile"), P("depth", "tile"), P(), P(), P(), P())
    return jax.shard_map(
        local,
        mesh=mesh,
        in_specs=placed,
        out_specs=P(None, None, ("depth", "tile"), None),
        check_vma=False,
    )
```

time: 672 us -> 87.9 us (0.13)
  other arithmetic: 398 us -> 0.82 us
  local copies, waits for them, and re-layouts: 151 us -> 8.55 us
  waiting for transfers between devices: 50.8 us -> 21.6 us
  loops' own time: 26.6 us -> 0 us
  Pallas kernels: 0 us -> 23.8 us
  between operations: 12.1 us -> 0.8 us
  blocking collectives: 0 us -> 9.35 us
    another operation x256 -> x0, other arithmetic: 321 us -> none  [the longest x128 306 us: shade_block(): jnp.stack([sigma * tints[0] * shade, sigma * tints[1] * shade, sigma * ti...]
    all_to_all x1 -> x0, waiting for transfers between devices: 48.8 us -> none  [local(): lax.all_to_all(merged, ('depth', 'tile'), split_axis=2, concat_axis=3, ti...]
    reshape x65 -> x2, local copies, waits for them, and re-layouts: 40.3 us -> 1.52 us  [the longest x1 0.76 us: local(): depth_order.reshape(-1)]
    slice x195 -> x0, local copies, waits for them, and re-layouts: 36.1 us -> none  [the longest x32 21.6 us: shade_block(): class_gain[channel] * center + class_bias[channel]]
    convert_element_type x33 -> x0, other arithmetic: 30.1 us -> none  [the longest x32 29.9 us: shade_block(): field = block.astype(jnp.float32)]
    another operation x1 -> x0, loops' own time: 26.6 us -> none  [footprint(): stacked = lax.map(one_block, jnp.arange(blocks, dtype=jnp.int32))]
    pallas_call x0 -> x10, Pallas kernels: none -> 23.8 us  [the longest x4 18.2 us: prints_of(): pl.pallas_call(functools.partial(print_kernel, views, total_z, shift), ou...]
    dynamic_update_slice x32 -> x0, other arithmetic: 21.9 us -> none  [footprint(): stacked = lax.map(one_block, jnp.arange(blocks, dtype=jnp.int32))]
  transfers between devices with their start and end apart: 4 -> 9, of which waited for: 2 -> 4; matrix products, arithmetic and copies ran while one was open for 1% -> 3% of each run, Pallas kernels for 0% -> 17%
where the time goes in v2:
time: 87.9 us; the launch traced here: 87.5 us
  Pallas kernels  23.8 us (27%)
  starting transfers between devices  22.6 us (26%)
  waiting for transfers between devices  21.6 us (25%)
  blocking collectives  9.35 us (11%)
  local copies, waits for them, and re-layouts  8.55 us (10%)
    ppermute x3, waiting for transfers between devices, passed_round(): lax.ppermute(x, axis, [(i, (i + by) % devices) for i in range(devices)])  20.7 us
    pallas_call x4, Pallas kernels, prints_of(): pl.pallas_call(functools.partial(print_kernel, views, total_z, shift), ou...  18.2 us
    ppermute x6, starting transfers between devices, passed_along(): return lax.ppermute(x, axis, pairs)  17.9 us
    all_to_all x1, blocking collectives, local(): lax.all_to_all(blocks, 'tile', split_axis=0, concat_axis=0, tiled=True)  9.35 us
    unnamed x6, local copies, waits for them, and re-layouts  7.03 us
    ppermute x3, starting transfers between devices, passed_round(): lax.ppermute(x, axis, [(i, (i + by) % devices) for i in range(devices)])  4.76 us
    pallas_call x1, Pallas kernels, turn_volume(): pl.pallas_call(turn_kernel, out_shape=[jax.ShapeDtypeStruct((blocks + 2,...  2.32 us
  transfers between devices with their start and end apart: 9, of which 4 were waited for; matrix products, arithmetic and copies ran while one was open for 3% of the time, Pallas kernels for 17%

profile of v2, /device:TPU:0, one launch (start us, length us, event | category | flops | bytes accessed | tf_op | source)
XLA Modules:
  0.0 87.5 jit_solution(13139309819853979833)
XLA Ops:
  0.0 1.6 %copy-done.2 = bf16[512,16,128]{2,1,0:T(8,128)(2,1)S(1)} copy-done((bf16[512,16,128]{2,1,0:T(8,128)(2,1)S(1)}, bf16[512,16,128]{2,1,0:T(8,128)(2,1)}, u32[]{:S(2)}) %copy-start.2) | copy-done | bytes 2097176
  1.6 2.3 %turn_rows.1 = (f32[6,16,128,128]{3,2,1,0:T(8,128)S(1)}, bf16[2,16,512]{2,1,0:T(8,128)(2,1)S(1)}) custom-call(bf16[512,16,128]{2,1,0:T(8,128)(2,1)S(1)} %copy-done.2), custom_call_target="tpu_custom_call" | custom-call | tf_op jit(solution)/shard_map/turn_rows/pallas_call | solution.py:143
  3.9 2.7 %copy-done = f32[6,16,128,128]{3,2,1,0:T(8,128)} copy-done((f32[6,16,128,128]{3,2,1,0:T(8,128)}, f32[6,16,128,128]{3,2,1,0:T(8,128)S(1)}, u32[]{:S(2)}) %copy-start) | copy-done | bytes 6291480
  6.6 2.3 %collective-permute-start = (bf16[16,512]{1,0:T(8,128)(2,1)S(1)}, bf16[16,512]{1,0:T(8,128)(2,1)S(1)}, u32[]{:S(2)}, u32[]{:S(2)}) collective-permute-start(bf16[16,512]{1,0:T(8,128)(2,1)S(1)} %get-tuple-element.26), channel_id=1, source_target_pairs={{0,1},{1,2},{2,3},{3,4},{4,5},{5,6},{6,7},{8,9},{9,10},{10,11},{11... | collective-permute-start | bytes 49160 | tf_op jit(solution)/shard_map/ppermute | solution.py:237
  8.9 1.3 %collective-permute-start.1 = (bf16[16,512]{1,0:T(8,128)(2,1)S(1)}, bf16[16,512]{1,0:T(8,128)(2,1)S(1)}, u32[]{:S(2)}, u32[]{:S(2)}) collective-permute-start(bf16[16,512]{1,0:T(8,128)(2,1)S(1)} %get-tuple-element.25), channel_id=1, source_target_pairs={{1,0},{2,1},{3,2},{4,3},{5,4},{6,5},{7,6},{9,8},{10,9},{11,10},{12... | collective-permute-start | bytes 49160 | tf_op jit(solution)/shard_map/ppermute | solution.py:237
  10.9 0.8 reshape.10
  13.2 0.9 %collective-permute-done.1.right_ref = bf16[16,512]{1,0:T(8,128)(2,1)S(1)} collective-permute-done((bf16[16,512]{1,0:T(8,128)(2,1)S(1)}, bf16[16,512]{1,0:T(8,128)(2,1)S(1)}, u32[]{:S(2)}, u32[]{:S(2)}) %collective-permute-start.1) | collective-permute-done | bytes 16416 | tf_op jit(solution)/shard_map/ppermute | solution.py:237
  14.1 2.8 %copy-done.1 = f32[6,16,128,128]{3,2,1,0:T(8,128)S(1)} copy-done((f32[6,16,128,128]{3,2,1,0:T(8,128)S(1)}, f32[6,16,128,128]{3,2,1,0:T(8,128)}, u32[]{:S(2)}) %copy-start.1) | copy-done | bytes 6291480
  16.9 4.5 %prints.7 = (f32[2,4,128,128]{3,2,1,0:T(8,128)S(1)}, s16[2,4,128,128]{3,2,1,0:T(8,128)(2,1)S(1)}) custom-call(s32[10]{0:T(128)S(1)} %pad_add_fusion.counts_ref, f32[14]{0:T(128)S(1)} %pad_maximum_fusion.numbers_ref, f32[6,16,128,128]{3,2,1,0:T(8,128)S(1)} %copy-done.1, bf16[16,512]{1,0:T(8,128)(2,1)S(1)} %collective-permute-done.left_ref, ...), custom_call_target="tpu_custom_call" | custom-call | flops 26214400 | bytes 12582912 | tf_op jit(solution)/shard_map/prints/pallas_call | solution.py:202
  21.5 4.4 %collective-permute-start.7 = (s16[2,4,128,128]{3,2,1,0:T(8,128)(2,1)S(1)}, s16[2,4,128,128]{3,2,1,0:T(8,128)(2,1)S(1)}, u32[]{:S(2)}, u32[]{:S(2)}) collective-permute-start(s16[2,4,128,128]{3,2,1,0:T(8,128)(2,1)S(1)} %get-tuple-element.24), channel_id=1, source_target_pairs={{0,1},{1,2},{2,3},{3,4},{4,5},{5,6},{6,7},{8,9},{9,10},{10,11},{11... | collective-permute-start | bytes 786440 | tf_op jit(solution)/shard_map/ppermute | solution.py:237
  25.9 4.5 %prints.6 = (f32[2,4,128,128]{3,2,1,0:T(8,128)S(1)}, s16[2,4,128,128]{3,2,1,0:T(8,128)(2,1)S(1)}) custom-call(s32[10]{0:T(128)S(1)} %pad_add_fusion.counts_ref, f32[14]{0:T(128)S(1)} %pad_maximum_fusion.numbers_ref, f32[6,16,128,128]{3,2,1,0:T(8,128)S(1)} %copy-done.1, bf16[16,512]{1,0:T(8,128)(2,1)S(1)} %collective-permute-done.left_ref, ...), custom_call_target="tpu_custom_call" | custom-call | flops 26214400 | bytes 12582912 | tf_op jit(solution)/shard_map/prints/pallas_call | solution.py:202
  30.4 3.5 %collective-permute-start.5 = (s16[2,4,128,128]{3,2,1,0:T(8,128)(2,1)S(1)}, s16[2,4,128,128]{3,2,1,0:T(8,128)(2,1)S(1)}, u32[]{:S(2)}, u32[]{:S(2)}) collective-permute-start(s16[2,4,128,128]{3,2,1,0:T(8,128)(2,1)S(1)} %get-tuple-element.22), channel_id=1, source_target_pairs={{0,1},{1,2},{2,3},{3,4},{4,5},{5,6},{6,7},{8,9},{9,10},{10,11},{11... | collective-permute-start | bytes 786440 | tf_op jit(solution)/shard_map/ppermute | solution.py:237
  34.0 4.6 %prints.5 = (f32[2,4,128,128]{3,2,1,0:T(8,128)S(1)}, s16[2,4,128,128]{3,2,1,0:T(8,128)(2,1)S(1)}) custom-call(s32[10]{0:T(128)S(1)} %pad_add_fusion.counts_ref, f32[14]{0:T(128)S(1)} %pad_maximum_fusion.numbers_ref, f32[6,16,128,128]{3,2,1,0:T(8,128)S(1)} %copy-done.1, bf16[16,512]{1,0:T(8,128)(2,1)S(1)} %collective-permute-done.left_ref, ...), custom_call_target="tpu_custom_call" | custom-call | flops 26214400 | bytes 12582912 | tf_op jit(solution)/shard_map/prints/pallas_call | solution.py:202
  38.5 2.8 %collective-permute-start.3 = (s16[2,4,128,128]{3,2,1,0:T(8,128)(2,1)S(1)}, s16[2,4,128,128]{3,2,1,0:T(8,128)(2,1)S(1)}, u32[]{:S(2)}, u32[]{:S(2)}) collective-permute-start(s16[2,4,128,128]{3,2,1,0:T(8,128)(2,1)S(1)} %get-tuple-element.20), channel_id=1, source_target_pairs={{0,1},{1,2},{2,3},{3,4},{4,5},{5,6},{6,7},{8,9},{9,10},{10,11},{11... | collective-permute-start | bytes 786440 | tf_op jit(solution)/shard_map/ppermute | solution.py:237
  41.3 4.5 %prints.4 = (f32[2,4,128,128]{3,2,1,0:T(8,128)S(1)}, s16[2,4,128,128]{3,2,1,0:T(8,128)(2,1)S(1)}) custom-call(s32[10]{0:T(128)S(1)} %pad_add_fusion.counts_ref, f32[14]{0:T(128)S(1)} %pad_maximum_fusion.numbers_ref, f32[6,16,128,128]{3,2,1,0:T(8,128)S(1)} %copy-done.1, bf16[16,512]{1,0:T(8,128)(2,1)S(1)} %collective-permute-done.left_ref, ...), custom_call_target="tpu_custom_call" | custom-call | flops 26214400 | bytes 12582912 | tf_op jit(solution)/shard_map/prints/pallas_call | solution.py:202
  45.9 3.5 %collective-permute-start.2 = (s16[2,4,128,128]{3,2,1,0:T(8,128)(2,1)S(1)}, s16[2,4,128,128]{3,2,1,0:T(8,128)(2,1)S(1)}, u32[]{:S(2)}, u32[]{:S(2)}) collective-permute-start(s16[2,4,128,128]{3,2,1,0:T(8,128)(2,1)S(1)} %get-tuple-element.18), channel_id=1, source_target_pairs={{0,1},{1,2},{2,3},{3,4},{4,5},{5,6},{6,7},{8,9},{9,10},{10,11},{11... | collective-permute-start | bytes 786440 | tf_op jit(solution)/shard_map/ppermute | solution.py:237
  49.7 3.7 %collective-permute-start.8 = (s16[2,4,128,128]{3,2,1,0:T(8,128)(2,1)S(1)}, s16[2,4,128,128]{3,2,1,0:T(8,128)(2,1)S(1)}, u32[]{:S(2)}, u32[]{:S(2)}) collective-permute-start(s16[2,4,128,128]{3,2,1,0:T(8,128)(2,1)S(1)} %merge.5), channel_id=1, source_target_pairs={{0,24},{8,0},{16,8},{24,16},{1,25},{9,1},{17,9},{25,17},{2,26},{10... | collective-permute-start | bytes 786440 | tf_op jit(solution)/shard_map/ppermute | solution.py:242
  54.1 1.1 %collective-permute-start.4 = (s16[2,4,128,128]{3,2,1,0:T(8,128)(2,1)S(1)}, s16[2,4,128,128]{3,2,1,0:T(8,128)(2,1)S(1)}, u32[]{:S(2)}, u32[]{:S(2)}) collective-permute-start(s16[2,4,128,128]{3,2,1,0:T(8,128)(2,1)S(1)} %merge.3), channel_id=1, source_target_pairs={{0,16},{8,24},{16,0},{24,8},{1,17},{9,25},{17,1},{25,9},{2,18},{10... | collective-permute-start | bytes 786440 | tf_op jit(solution)/shard_map/ppermute | solution.py:242
  55.1 5.0 %collective-permute-done.8.refs_2_ = s16[2,4,128,128]{3,2,1,0:T(8,128)(2,1)S(1)} collective-permute-done((s16[2,4,128,128]{3,2,1,0:T(8,128)(2,1)S(1)}, s16[2,4,128,128]{3,2,1,0:T(8,128)(2,1)S(1)}, u32[]{:S(2)}, u32[]{:S(2)}) %collective-permute-start.8) | collective-permute-done | bytes 262176 | tf_op jit(solution)/shard_map/ppermute | solution.py:242
  60.1 6.6 %collective-permute-done.6.refs_1_ = s16[2,4,128,128]{3,2,1,0:T(8,128)(2,1)S(1)} collective-permute-done((s16[2,4,128,128]{3,2,1,0:T(8,128)(2,1)S(1)}, s16[2,4,128,128]{3,2,1,0:T(8,128)(2,1)S(1)}, u32[]{:S(2)}, u32[]{:S(2)}) %collective-permute-start.6) | collective-permute-done | bytes 262176 | tf_op jit(solution)/shard_map/ppermute | solution.py:242
  66.7 9.2 %collective-permute-done.4.refs_0_ = s16[2,4,128,128]{3,2,1,0:T(8,128)(2,1)S(1)} collective-permute-done((s16[2,4,128,128]{3,2,1,0:T(8,128)(2,1)S(1)}, s16[2,4,128,128]{3,2,1,0:T(8,128)(2,1)S(1)}, u32[]{:S(2)}, u32[]{:S(2)}) %collective-permute-start.4) | collective-permute-done | bytes 262176 | tf_op jit(solution)/shard_map/ppermute | solution.py:242
  75.8 1.4 %final.1 = s16[8,2,4,16,128]{4,3,2,1,0:T(8,128)(2,1)S(1)} custom-call(s32[10]{0:T(128)S(1)} %pad_add_fusion.counts_ref, f32[2,4,128,128]{3,2,1,0:T(8,128)S(1)} %get-tuple-element.17.own_ref, s16[2,4,128,128]{3,2,1,0:T(8,128)(2,1)S(1)} %collective-permute-done.2.over_ref, s16[2,4,128,128]{3,2,1,0:T(8,128)(2,1)S(1)} %collective-permute-done.4.refs_0_, ...), custom_call_target="tpu_custom_call" | custom-call | tf_op jit(solution)/shard_map/final/pallas_call | solution.py:220
  77.3 9.3 %all_to_all.5.blocks_ref = s16[8,2,4,16,128]{4,3,2,1,0:T(8,128)(2,1)S(1)} all-to-all(s16[8,2,4,16,128]{4,3,2,1,0:T(8,128)(2,1)S(1)} %final.1), channel_id=1, replica_groups=mesh['depth'=4,'tile'=8] {'tile'}, dimensions={0} | all-to-all | bytes 524288 | tf_op jit(solution)/shard_map/all_to_all | solution.py:266
  86.6 0.9 %place.1 = f32[2,4,16,1024]{3,2,1,0:T(8,128)} custom-call(s16[8,2,4,16,128]{4,3,2,1,0:T(8,128)(2,1)S(1)} %all_to_all.5.blocks_ref), custom_call_target="tpu_custom_call" | custom-call | tf_op jit(solution)/shard_map/place/pallas_call | solution.py:229
  (16 shorter events, 2.6 us)
Async XLA Ops:
  0.0 1.6 %copy-start.2 = (bf16[512,16,128]{2,1,0:T(8,128)(2,1)S(1)}, bf16[512,16,128]{2,1,0:T(8,128)(2,1)}, u32[]{:S(2)}) copy-start(bf16[512,16,128]{2,1,0:T(8,128)(2,1)} %volume_ref.1) | copy-start | bytes 6291460
  3.9 2.7 %copy-start = (f32[6,16,128,128]{3,2,1,0:T(8,128)}, f32[6,16,128,128]{3,2,1,0:T(8,128)S(1)}, u32[]{:S(2)}) copy-start(f32[6,16,128,128]{3,2,1,0:T(8,128)S(1)} %get-tuple-element.15.field_ref) | copy-start | bytes 18874372
  6.6 6.7 %collective-permute-start = (bf16[16,512]{1,0:T(8,128)(2,1)S(1)}, bf16[16,512]{1,0:T(8,128)(2,1)S(1)}, u32[]{:S(2)}, u32[]{:S(2)}) collective-permute-start(bf16[16,512]{1,0:T(8,128)(2,1)S(1)} %get-tuple-element.26), channel_id=1, source_target_pairs={{0,1},{1,2},{2,3},{3,4},{4,5},{5,6},{6,7},{8,9},{9,10},{10,11},{11... | collective-permute-start | bytes 49160 | tf_op jit(solution)/shard_map/ppermute | solution.py:237
  8.9 5.2 %collective-permute-start.1 = (bf16[16,512]{1,0:T(8,128)(2,1)S(1)}, bf16[16,512]{1,0:T(8,128)(2,1)S(1)}, u32[]{:S(2)}, u32[]{:S(2)}) collective-permute-start(bf16[16,512]{1,0:T(8,128)(2,1)S(1)} %get-tuple-element.25), channel_id=1, source_target_pairs={{1,0},{2,1},{3,2},{4,3},{5,4},{6,5},{7,6},{9,8},{10,9},{11,10},{12... | collective-permute-start | bytes 49160 | tf_op jit(solution)/shard_map/ppermute | solution.py:237
  14.1 2.8 %copy-start.1 = (f32[6,16,128,128]{3,2,1,0:T(8,128)S(1)}, f32[6,16,128,128]{3,2,1,0:T(8,128)}, u32[]{:S(2)}) copy-start(f32[6,16,128,128]{3,2,1,0:T(8,128)} %copy-done) | copy-start | bytes 18874372
  21.5 27.9 %collective-permute-start.7 = (s16[2,4,128,128]{3,2,1,0:T(8,128)(2,1)S(1)}, s16[2,4,128,128]{3,2,1,0:T(8,128)(2,1)S(1)}, u32[]{:S(2)}, u32[]{:S(2)}) collective-permute-start(s16[2,4,128,128]{3,2,1,0:T(8,128)(2,1)S(1)} %get-tuple-element.24), channel_id=1, source_target_pairs={{0,1},{1,2},{2,3},{3,4},{4,5},{5,6},{6,7},{8,9},{9,10},{10,11},{11... | collective-permute-start | bytes 786440 | tf_op jit(solution)/shard_map/ppermute | solution.py:237
  30.4 22.9 %collective-permute-start.5 = (s16[2,4,128,128]{3,2,1,0:T(8,128)(2,1)S(1)}, s16[2,4,128,128]{3,2,1,0:T(8,128)(2,1)S(1)}, u32[]{:S(2)}, u32[]{:S(2)}) collective-permute-start(s16[2,4,128,128]{3,2,1,0:T(8,128)(2,1)S(1)} %get-tuple-element.22), channel_id=1, source_target_pairs={{0,1},{1,2},{2,3},{3,4},{4,5},{5,6},{6,7},{8,9},{9,10},{10,11},{11... | collective-permute-start | bytes 786440 | tf_op jit(solution)/shard_map/ppermute | solution.py:237
  38.5 15.2 %collective-permute-start.3 = (s16[2,4,128,128]{3,2,1,0:T(8,128)(2,1)S(1)}, s16[2,4,128,128]{3,2,1,0:T(8,128)(2,1)S(1)}, u32[]{:S(2)}, u32[]{:S(2)}) collective-permute-start(s16[2,4,128,128]{3,2,1,0:T(8,128)(2,1)S(1)} %get-tuple-element.20), channel_id=1, source_target_pairs={{0,1},{1,2},{2,3},{3,4},{4,5},{5,6},{6,7},{8,9},{9,10},{10,11},{11... | collective-permute-start | bytes 786440 | tf_op jit(solution)/shard_map/ppermute | solution.py:237
  45.9 9.2 %collective-permute-start.2 = (s16[2,4,128,128]{3,2,1,0:T(8,128)(2,1)S(1)}, s16[2,4,128,128]{3,2,1,0:T(8,128)(2,1)S(1)}, u32[]{:S(2)}, u32[]{:S(2)}) collective-permute-start(s16[2,4,128,128]{3,2,1,0:T(8,128)(2,1)S(1)} %get-tuple-element.18), channel_id=1, source_target_pairs={{0,1},{1,2},{2,3},{3,4},{4,5},{5,6},{6,7},{8,9},{9,10},{10,11},{11... | collective-permute-start | bytes 786440 | tf_op jit(solution)/shard_map/ppermute | solution.py:237
  49.7 10.4 %collective-permute-start.8 = (s16[2,4,128,128]{3,2,1,0:T(8,128)(2,1)S(1)}, s16[2,4,128,128]{3,2,1,0:T(8,128)(2,1)S(1)}, u32[]{:S(2)}, u32[]{:S(2)}) collective-permute-start(s16[2,4,128,128]{3,2,1,0:T(8,128)(2,1)S(1)} %merge.5), channel_id=1, source_target_pairs={{0,24},{8,0},{16,8},{24,16},{1,25},{9,1},{17,9},{25,17},{2,26},{10... | collective-permute-start | bytes 786440 | tf_op jit(solution)/shard_map/ppermute | solution.py:242
  53.7 13.0 %collective-permute-start.6 = (s16[2,4,128,128]{3,2,1,0:T(8,128)(2,1)S(1)}, s16[2,4,128,128]{3,2,1,0:T(8,128)(2,1)S(1)}, u32[]{:S(2)}, u32[]{:S(2)}) collective-permute-start(s16[2,4,128,128]{3,2,1,0:T(8,128)(2,1)S(1)} %merge.4), channel_id=1, source_target_pairs={{0,8},{8,16},{16,24},{24,0},{1,9},{9,17},{17,25},{25,1},{2,10},{10... | collective-permute-start | bytes 786440 | tf_op jit(solution)/shard_map/ppermute | solution.py:242
  54.1 21.8 %collective-permute-start.4 = (s16[2,4,128,128]{3,2,1,0:T(8,128)(2,1)S(1)}, s16[2,4,128,128]{3,2,1,0:T(8,128)(2,1)S(1)}, u32[]{:S(2)}, u32[]{:S(2)}) collective-permute-start(s16[2,4,128,128]{3,2,1,0:T(8,128)(2,1)S(1)} %merge.3), channel_id=1, source_target_pairs={{0,16},{8,24},{16,0},{24,8},{1,17},{9,25},{17,1},{25,9},{2,18},{10... | collective-permute-start | bytes 786440 | tf_op jit(solution)/shard_map/ppermute | solution.py:242

commit v3 on v2

v3 whole, which is shorter than its diff:
```python
import functools
import math
import jax
import jax.numpy as jnp
from jax import lax
from jax.experimental import pallas as pl
from jax.experimental.pallas import tpu as pltpu
from jax.sharding import PartitionSpec as P

LN2 = math.log(2.0)
code_step = 1638.0
code_middle = 16.0
code_none = -32768.0

smem = pl.BlockSpec(memory_space=pltpu.SMEM)
vmem = pl.BlockSpec(memory_space=pltpu.VMEM)
far = pl.BlockSpec(memory_space=pl.ANY)
small_cost = pl.CostEstimate(flops=10**10, bytes_accessed=10**8, transcendentals=0)
params = pltpu.CompilerParams(vmem_limit_bytes=12 * 1024 * 1024)
turn_params = pltpu.CompilerParams(vmem_limit_bytes=12 * 1024 * 1024)


def encode(x):
    return jnp.round(jnp.maximum(code_step * lax.log2(x) + code_step * code_middle, code_none)).astype(jnp.int16)


def decode(q):
    value = q.astype(jnp.int32).astype(jnp.float32)
    return jnp.where(value == code_none, 0.0, lax.exp2(value * (1.0 / code_step) - code_middle))


def turn_kernel(volume_ref, field_ref, low_ref, high_ref, brick, ordered, arrived):
    rows, slices, columns = volume_ref.shape
    blocks, _, _, width = field_ref.shape
    blocks = blocks - 2
    copies = []
    for block in range(blocks):
        part = pl.ds(block * width, width)
        copies.append(pltpu.make_async_copy(volume_ref.at[part], brick.at[part], arrived.at[block]))
    for copy in copies:
        copy.start()
    field_ref[0] = jnp.zeros((slices, columns, width), jnp.float32)
    field_ref[blocks + 1] = jnp.zeros((slices, columns, width), jnp.float32)
    for block in range(blocks):
        copies[block].wait()

        def order(index, carry):
            at = pl.multiple_of(block * width + index * slices, slices)
            ordered[:, pl.ds(at, slices), :] = jnp.swapaxes(brick[pl.ds(at, slices)], 0, 1)
            return carry

        lax.fori_loop(0, width // slices, order, 0, unroll=2)

        def turn(z, carry):
            field_ref[block + 1, z] = ordered[z, block * width:(block + 1) * width, :].T.astype(jnp.float32)
            return carry

        lax.fori_loop(0, slices, turn, 0, unroll=2)
        for edge_ref, x in ((low_ref, 0), (high_ref, columns - 1)):
            edge_ref[:, block * width:(block + 1) * width] = field_ref[block + 1, :, x, :].astype(edge_ref.dtype)


def make_table(total_z, active_ref, light_ref, gain_ref, bias_ref, table_ref):
    def spread(value):
        return jnp.full(table_ref.shape[1:], value, jnp.float32)

    values = [spread(active_ref[0, 0].astype(jnp.float32) * (-2.0 / total_z))]
    values += [spread(0.5 * gain_ref[k]) for k in range(3)] + [spread(gain_ref[3] * (1.0 / LN2))]
    values += [spread(0.5 * bias_ref[k]) for k in range(3)] + [spread(bias_ref[3] * (1.0 / LN2))]
    for v in range(light_ref.shape[0]):
        parts = [spread(light_ref[v, k]) for k in range(3)]
        square = jnp.maximum(parts[0] * parts[0] + parts[1] * parts[1] + parts[2] * parts[2], 1e-30)
        unit = (0.35 * LN2) * lax.rsqrt(square)
        values += [part * unit for part in parts] + [4.0 / square]
    for index, value in enumerate(values):
        table_ref[index] = value


def matter_kernel(shifts, field_ref, table_ref, thick_ref, tints_ref, slope_ref):
    _, slices, columns, width = thick_ref.shape
    group = table_ref.shape[1]
    scale = table_ref[0]
    gain = [table_ref[1 + k] for k in range(4)]
    bias = [table_ref[5 + k] for k in range(4)]
    lane = lax.broadcasted_iota(jnp.int32, (group, width), 1)
    start = lane == 0
    end = lane == width - 1
    deep = 2
    places = [(part, at * group) for part in range(deep) for at in range(columns // group)]
    for index, shift in enumerate(shifts):
        block = lax.rem(lax.axis_index("depth") + shift, field_ref.shape[0] - 2)

        def work(step, carry):
            z = step * deep
            heres = [field_ref[block + 1, z + part, at:at + group, :] for part, at in places]
            priors = [field_ref[block, z + part, at:at + group, :] for part, at in places]
            laters = [field_ref[block + 2, z + part, at:at + group, :] for part, at in places]
            done = []
            for here, prior, later in zip(heres, priors, laters):
                w = lax.exp2(gain[3] * here + bias[3])
                thick = scale * jnp.where(w < 0.001, w * (1.0 / LN2 - (0.5 / LN2) * w), lax.log2(1.0 + w))
                tints = [1.0 + jnp.tanh(gain[k] * here + bias[k]) for k in range(3)]
                prior = pltpu.roll(jnp.where(end, prior, here), 1, 1)
                later = pltpu.roll(jnp.where(start, later, here), width - 1, 1)
                done.append((thick, tints, later - prior))
            for (part, at), (thick, tints, slope) in zip(places, done):
                thick_ref[index, z + part, at:at + group, :] = thick
                for k in range(3):
                    tints_ref[index, k, z + part, at:at + group, :] = tints[k]
                slope_ref[index, z + part, at:at + group, :] = slope
            return carry

        lax.fori_loop(0, slices // deep, work, 0)


def first_matter_kernel(shifts, total_z, active_ref, light_ref, gain_ref, bias_ref, field_ref, table_ref, *refs):
    make_table(total_z, active_ref, light_ref, gain_ref, bias_ref, table_ref)
    matter_kernel(shifts, field_ref, table_ref, *refs)


def print_kernel(parts, matters, field_ref, table_ref, left_ref, right_ref, after_ref, *refs):
    matter_refs, own_ref, over_ref, sums = refs[:3 * matters], refs[3 * matters], refs[3 * matters + 1], refs[3 * matters + 2:]
    for index, (shift, source, place) in enumerate(parts):
        chosen = [ref.at[place] for ref in matter_refs[3 * source:3 * source + 3]]
        print_chunk(shift, field_ref, table_ref, left_ref, right_ref, *chosen, own_ref.at[index], over_ref.at[index], *sums)


def print_chunk(shift, field_ref, table_ref, left_ref, right_ref, thick_ref, tints_ref, slope_ref, own_ref, over_ref, *sums):
    blocks, slices, columns, width = field_ref.shape
    group = table_ref.shape[1]
    views = own_ref.shape[0]
    quad = columns // (2 * slices)
    count = columns // group
    block = lax.rem(lax.axis_index("depth") + shift, blocks - 2)
    slants = [[table_ref[9 + 4 * v + k] for k in range(3)] for v in range(views)]
    offsets = [table_ref[12 + 4 * v] for v in range(views)]
    line = lax.broadcasted_iota(jnp.int32, (group, width), 0)
    for part in sums:
        part[...] = jnp.zeros(part.shape, jnp.float32)
    along = pl.ds(pl.multiple_of(block * width, width), width)
    left = left_ref[:, along].astype(jnp.float32)
    right = right_ref[:, along].astype(jnp.float32)

    def work(j):
        base = j * group if isinstance(j, int) else pl.multiple_of(j * group, group)
        here_rows = pl.ds(base, group)
        for z in range(slices):
            if isinstance(j, int) and j == 0:
                less = jnp.where(line == 0, left[z:z + 1, :], pltpu.roll(field_ref[block + 1, z, here_rows, :], 1, 0))
            else:
                less = field_ref[block + 1, z, pl.ds(base - 1, group), :]
            if isinstance(j, int) and j == count - 1:
                more = jnp.where(line == group - 1, right[z:z + 1, :],
                                 pltpu.roll(field_ref[block + 1, z, here_rows, :], group - 1, 0))
            else:
                more = field_ref[block + 1, z, pl.ds(base + 1, group), :]
            dx = more - less
            dy = slope_ref[z, here_rows, :]
            if z == 0:
                dz = field_ref[block + 1, z + 1, here_rows, :]
            elif z == slices - 1:
                dz = -field_ref[block + 1, z - 1, here_rows, :]
            else:
                dz = field_ref[block + 1, z + 1, here_rows, :] - field_ref[block + 1, z - 1, here_rows, :]
            steep = dx * dx + dy * dy + dz * dz
            thick = thick_ref[z, here_rows, :]
            tints = [tints_ref[k, z, here_rows, :] for k in range(3)]
            for v in range(views):
                place = pl.ds(base + z * (v + 1) * quad, group)
                lx, ly, lz = slants[v]
                facing = dx * lx + dy * ly + dz * lz
                shade = thick * ((-0.15 * LN2) - jnp.abs(facing) * lax.rsqrt(steep + offsets[v]))
                depth = sums[4 * v + 3][place, :]
                sums[4 * v + 3][place, :] = depth + thick
                shade = shade * lax.exp2(depth)
                for k in range(3):
                    sums[4 * v + k][place, :] = sums[4 * v + k][place, :] + tints[k] * shade

    work(count - 1)

    def inner(index, carry):
        work(count - 2 - index)
        return carry

    lax.fori_loop(0, count - 2, inner, 0)
    work(0)
    for v in range(views):
        for k in range(4):
            part = sums[4 * v + k]
            own_ref[v, k] = part[:columns, :]
            first, count = over_rows(v, slices, columns)
            rest = part[columns:columns + count, :]
            over_ref[k, first:first + count, :] = encode(-rest if k == 3 else rest)


def over_rows(v, slices, columns):
    quad = columns // (2 * slices)
    ends = [-(-(slices - 1) * (view + 1) * quad // 16) * 16 for view in range(v + 1)]
    return sum(ends[:-1]), ends[-1]


def merged(own_ref, over_ref, v, slices):
    first, count = over_rows(v, slices, own_ref.shape[2])
    through = lax.exp2(own_ref[v, 3, :count, :])
    overs = [decode(over_ref[k, first:first + count, :]) for k in range(4)]
    tops = [own_ref[v, k, :count, :] + through * overs[k] for k in range(3)] + [overs[3] - own_ref[v, 3, :count, :]]
    if count == own_ref.shape[2]:
        return tops
    lows = [own_ref[v, k, count:, :] * (1.0 if k < 3 else -1.0) for k in range(4)]
    return [jnp.concatenate([top, low]) for top, low in zip(tops, lows)]


def merge_kernel(slices, layers, own_ref, over_ref, later_ref, *refs):
    for index, layer_ref in enumerate(refs[:layers]):
        for v in range(own_ref.shape[1]):
            for k, part in enumerate(merged(own_ref.at[index], over_ref.at[index], v, slices)):
                layer_ref[v, k] = encode(part)
    for ref in refs[layers:]:
        ref[...] = later_ref[...]


def final_kernel(views, share, slices, shifts, order_ref, own_ref, over_ref, *refs):
    layer_refs, image_ref = refs[:-1], refs[-1]
    groups = len(shifts) + 1
    owner = lax.axis_index("depth")
    ids = [owner] + [lax.rem(owner + groups - shift, groups) for shift in shifts]
    for v in range(views):
        order = [order_ref[v, r] for r in range(groups)]
        places = [sum(jnp.where(order[r] == one, r, 0) for r in range(groups)) for one in ids]
        layers = [merged(own_ref.at[0], over_ref.at[0], v, slices)] + [[decode(ref[v, k]) for k in range(4)] for ref in layer_refs]
        colours = [0.0] * 3
        total = 0.0
        for g in range(groups):
            front = 0.0
            for h in range(groups):
                if h != g:
                    front = front + layers[h][3] * jnp.where(places[h] < places[g], 1.0, 0.0)
            through = lax.exp2(-front)
            colours = [colours[k] + layers[g][k] * through for k in range(3)]
            total = total + layers[g][3]
        for k, part in enumerate(colours + [1.0 - lax.exp2(-total)]):
            turned = part.T
            for t in range(turned.shape[0] // share):
                block = turned[t * share:(t + 1) * share, :]
                image_ref[t, v, k] = encode(block) if image_ref.dtype == jnp.int16 else block


def place_kernel(blocks_ref, image_ref):
    tiles, views, channels, share, columns = blocks_ref.shape
    for t in range(tiles):
        for v in range(views):
            for k in range(channels):
                block = blocks_ref[t, v, k]
                block = decode(block) if block.dtype == jnp.int16 else block
                image_ref[v, k, :, t * columns:(t + 1) * columns] = block


def turn_volume(volume, blocks):
    rows, slices, columns = volume.shape
    width = rows // blocks
    edge = jax.ShapeDtypeStruct((slices, rows), volume.dtype)
    return pl.pallas_call(
        turn_kernel,
        out_shape=[jax.ShapeDtypeStruct((blocks + 2, slices, columns, width), jnp.float32), edge, edge],
        in_specs=[far], out_specs=[vmem] * 3,
        scratch_shapes=[pltpu.VMEM(volume.shape, volume.dtype), pltpu.VMEM((slices, rows, columns), volume.dtype),
                        pltpu.SemaphoreType.DMA((blocks,))],
        cost_estimate=pl.CostEstimate(flops=1, bytes_accessed=16 * 1024 * 1024, transcendentals=0),
        compiler_params=turn_params, name="turn_rows")(volume)


def matter_of(field, shifts, table=None, smalls=(), after=()):
    blocks, slices, columns, width = field.shape
    shape = (len(shifts), slices, columns, width)
    outs = [jax.ShapeDtypeStruct(shape, jnp.float32), jax.ShapeDtypeStruct((len(shifts), 3) + shape[1:], jnp.float32),
            jax.ShapeDtypeStruct(shape, jnp.float32)]
    if table is not None:
        return pl.pallas_call(
            functools.partial(matter_kernel, shifts), out_shape=outs, in_specs=[vmem] * 2, out_specs=[vmem] * 3,
            cost_estimate=small_cost, compiler_params=params, name="matter")(field, table)
    table = jax.ShapeDtypeStruct((9 + 4 * smalls[1].shape[0], 8, width), jnp.float32)
    return pl.pallas_call(
        functools.partial(first_matter_kernel, shifts, slices * (blocks - 2)), out_shape=[table] + outs,
        in_specs=[smem] * 4 + [vmem], out_specs=[vmem] * 4,
        cost_estimate=small_cost, compiler_params=params, name="matter")(*smalls, field)


def prints_of(field, matters, table, left, right, after, parts, views):
    blocks, slices, columns, width = field.shape
    shape = (len(parts), views, 4, columns, width)
    over_shape = (len(parts), 4, sum(over_rows(views - 1, slices, columns)), width)
    arrays = [array for matter in matters for array in matter]
    return pl.pallas_call(
        functools.partial(print_kernel, parts, len(matters)),
        out_shape=[jax.ShapeDtypeStruct(shape, jnp.float32), jax.ShapeDtypeStruct(over_shape, jnp.int16)],
        in_specs=[vmem] * 4 + [far] + [vmem] * len(arrays), out_specs=[vmem] * 2,
        scratch_shapes=[pltpu.VMEM((2 * columns, width), jnp.float32)] * (4 * views),
        cost_estimate=small_cost, compiler_params=params, name="prints")(field, table, left, right, after, *arrays)


def merge_of(own, over, later, slices, pass_later):
    layers = own.shape[0]
    outs = [jax.ShapeDtypeStruct(own.shape[1:], jnp.int16)] * layers
    outs += [jax.ShapeDtypeStruct(later.shape, later.dtype)] * pass_later
    return pl.pallas_call(
        functools.partial(merge_kernel, slices, layers), out_shape=outs,
        in_specs=[vmem] * 2 + [vmem if pass_later else far], out_specs=[vmem] * len(outs), cost_estimate=small_cost,
        compiler_params=params, name="merge")(own, over, later)


def final_of(depth_order, own, over, layers, shifts, share, slices):
    _, views, channels, columns, width = own.shape
    kind = jnp.int16 if share % 16 == 0 else jnp.float32
    return pl.pallas_call(
        functools.partial(final_kernel, views, share, slices, shifts),
        out_shape=jax.ShapeDtypeStruct((width // share, views, channels, share, columns), kind),
        in_specs=[smem] + [vmem] * (2 + len(layers)), out_specs=vmem, compiler_params=params,
        name="final")(depth_order, own, over, *layers)


def place_of(blocks):
    tiles, views, channels, share, columns = blocks.shape
    return pl.pallas_call(
        place_kernel, out_shape=jax.ShapeDtypeStruct((views, channels, share, tiles * columns), jnp.float32),
        in_specs=[vmem], out_specs=vmem, compiler_params=params, name="place")(blocks)


def passed_along(x, axis, by):
    devices = lax.axis_size(axis)
    pairs = [(i, i + by) for i in range(devices) if 0 <= i + by < devices]
    return lax.ppermute(x, axis, pairs)


def passed_round(x, axis, by):
    devices = lax.axis_size(axis)
    return lax.ppermute(x, axis, [(i, (i + by) % devices) for i in range(devices)])


def local(volume, active, depth_order, light_vector, class_gain, class_bias):
    depth_count = lax.axis_size("depth")
    tile_count = lax.axis_size("tile")
    rows, slices, columns = volume.shape
    share = rows // (depth_count * tile_count)
    field, low, high = turn_volume(volume, depth_count)
    left = passed_along(high, "tile", 1)
    right = passed_along(low, "tile", -1)
    shifts = sorted(range(1, depth_count), key=lambda shift: -min(shift, depth_count - shift)) + [0]
    half = (len(shifts) + 1) // 2
    table, *early = matter_of(field, shifts[:half], smalls=(active, light_vector, class_gain, class_bias))
    late = matter_of(field, shifts[half:], table=table)
    sources = [(shift, index // half, index % half) for index, shift in enumerate(shifts)]

    def chunks(parts, after):
        return prints_of(field, (early, late) if any(part[1] for part in parts) else (early,), table, left, right, after,
                         parts, light_vector.shape[0])

    own, over = chunks(sources[:1], left)
    layer, = merge_of(own, passed_along(over, "tile", 1), left, slices, 0)
    layers = [passed_round(layer, "depth", shifts[0])]
    middle, middle_over = chunks(sources[1:-1], layer)
    last, last_over = chunks(sources[-1:], middle)
    *middle_layers, last_over = merge_of(middle, passed_along(middle_over, "tile", 1), last_over, slices, 1)
    last_over = passed_along(last_over, "tile", 1)
    layers += [passed_round(layer, "depth", shift) for layer, shift in zip(middle_layers, shifts[1:-1])]
    blocks = final_of(depth_order, last, last_over, layers, shifts[:-1], share, slices)
    blocks = lax.all_to_all(blocks, "tile", split_axis=0, concat_axis=0, tiled=True)
    return place_of(blocks)


def solution(mesh):
    placed = (P(None, "depth", "tile"), P("depth", "tile"), P(), P(), P(), P())
    return jax.shard_map(
        local,
        mesh=mesh,
        in_specs=placed,
        out_specs=P(None, None, ("depth", "tile"), None),
        check_vma=False,
    )
```

time: 87.9 us -> 71.7 us (0.82)
  waiting for transfers between devices: 21.6 us -> 5.96 us
  local copies, waits for them, and re-layouts: 8.55 us -> 1.61 us
  blocking collectives: 9.35 us -> 15.3 us
  starting transfers between devices: 22.6 us -> 24.7 us
    ppermute x3, waiting for transfers between devices: 20.7 us -> 4.92 us  [passed_round(): lax.ppermute(x, axis, [(i, (i + by) % devices) for i in range(devices)])]
    all_to_all x1, blocking collectives: 9.35 us -> 15.3 us  [local(): lax.all_to_all(blocks, 'tile', split_axis=0, concat_axis=0, tiled=True)]
    unnamed x6 -> x10, local copies, waits for them, and re-layouts: 7.03 us -> 1.61 us
    pallas_call x8, Pallas kernels: 20.5 us -> 18.7 us  [the longest x3 10.5 us: prints_of(): pl.pallas_call(functools.partial(print_kernel, parts, len(matters)), out_...]
    ppermute x3, starting transfers between devices: 4.76 us -> 6.53 us  [passed_round(): lax.ppermute(x, axis, [(i, (i + by) % devices) for i in range(devices)])]
    reshape x2 -> x0, local copies, waits for them, and re-layouts: 1.52 us -> none  [the longest x1 0.76 us: local(): depth_order.reshape(-1)]
    pallas_call x1, Pallas kernels: 2.32 us -> 3.39 us  [turn_volume(): pl.pallas_call(turn_kernel, out_shape=[jax.ShapeDtypeStruct((blocks + 2,...]
    ppermute x6 -> x5, starting transfers between devices: 17.9 us -> 18.1 us  [passed_along(): return lax.ppermute(x, axis, pairs)]
  transfers between devices with their start and end apart: 9 -> 8, of which waited for: 4 -> 2; matrix products, arithmetic and copies ran while one was open for 3% -> 0% of each run, Pallas kernels for 17% -> 20%
where the time goes in v3:
time: 71.7 us; the launch traced here: 71.4 us
  starting transfers between devices  24.7 us (34%)
  Pallas kernels  23 us (32%)
  blocking collectives  15.3 us (21%)
  waiting for transfers between devices  5.96 us (8%)
  local copies, waits for them, and re-layouts  1.61 us (2%)
  between operations  0.82 us (1%)
    ppermute x5, starting transfers between devices, passed_along(): return lax.ppermute(x, axis, pairs)  18.1 us
    all_to_all x1, blocking collectives, local(): lax.all_to_all(blocks, 'tile', split_axis=0, concat_axis=0, tiled=True)  15.3 us
    pallas_call x3, Pallas kernels, prints_of(): pl.pallas_call(functools.partial(print_kernel, parts, len(matters)), out_...  10.5 us
    ppermute x3, starting transfers between devices, passed_round(): lax.ppermute(x, axis, [(i, (i + by) % devices) for i in range(devices)])  6.53 us
    ppermute x3, waiting for transfers between devices, passed_round(): lax.ppermute(x, axis, [(i, (i + by) % devices) for i in range(devices)])  4.92 us
    pallas_call x1, Pallas kernels, turn_volume(): pl.pallas_call(turn_kernel, out_shape=[jax.ShapeDtypeStruct((blocks + 2,...  3.39 us
    pallas_call x1, Pallas kernels, matter_of(): pl.pallas_call(functools.partial(first_matter_kernel, shifts, slices * (b...  3.3 us
    pallas_call x1, Pallas kernels, matter_of(): pl.pallas_call(functools.partial(matter_kernel, shifts), out_shape=outs,...  2.74 us
  transfers between devices with their start and end apart: 8, of which 2 were waited for; matrix products, arithmetic and copies ran while one was open for 0% of the time, Pallas kernels for 20%

profile of v3, /device:TPU:0, one launch (start us, length us, event | category | flops | bytes accessed | tf_op | source)
XLA Modules:
  0.0 71.4 jit_solution(7335524564787492845)
XLA Ops:
  0.0 1.6 %copy-done = bf16[512,16,128]{2,1,0:T(8,128)(2,1)S(1)} copy-done((bf16[512,16,128]{2,1,0:T(8,128)(2,1)S(1)}, bf16[512,16,128]{2,1,0:T(8,128)(2,1)}, u32[]{:S(2)}) %copy-start) | copy-done | bytes 2097176
  1.6 3.4 %turn_rows.1 = (f32[6,16,128,128]{3,2,1,0:T(8,128)S(1)}, bf16[16,512]{1,0:T(8,128)(2,1)S(1)}, bf16[16,512]{1,0:T(8,128)(2,1)S(1)}) custom-call(bf16[512,16,128]{2,1,0:T(8,128)(2,1)S(1)} %copy-done), custom_call_target="tpu_custom_call" | custom-call | flops 1 | bytes 16777216 | tf_op jit(solution)/shard_map/turn_rows/pallas_call | solution.py:262
  5.0 2.4 %collective-permute-start = (bf16[16,512]{1,0:T(8,128)(2,1)S(1)}, bf16[16,512]{1,0:T(8,128)(2,1)S(1)}, u32[]{:S(2)}, u32[]{:S(2)}) collective-permute-start(bf16[16,512]{1,0:T(8,128)(2,1)S(1)} %get-tuple-element.26), channel_id=1, source_target_pairs={{0,1},{1,2},{2,3},{3,4},{4,5},{5,6},{6,7},{8,9},{9,10},{10,11},{11... | collective-permute-start | bytes 49160 | tf_op jit(solution)/shard_map/ppermute | solution.py:331
  7.4 1.3 %collective-permute-start.1 = (bf16[16,512]{1,0:T(8,128)(2,1)S(1)}, bf16[16,512]{1,0:T(8,128)(2,1)S(1)}, u32[]{:S(2)}, u32[]{:S(2)}) collective-permute-start(bf16[16,512]{1,0:T(8,128)(2,1)S(1)} %get-tuple-element.27), channel_id=1, source_target_pairs={{1,0},{2,1},{3,2},{4,3},{5,4},{6,5},{7,6},{9,8},{10,9},{11,10},{12... | collective-permute-start | bytes 49160 | tf_op jit(solution)/shard_map/ppermute | solution.py:331
  9.3 3.3 %matter.2 = (f32[17,8,128]{2,1,0:T(8,128)S(1)}, f32[2,16,128,128]{3,2,1,0:T(8,128)S(1)}, f32[2,3,16,128,128]{4,3,2,1,0:T(8,128)S(1)}, f32[2,16,128,128]{3,2,1,0:T(8,128)S(1)}) custom-call(s32[1,1]{1,0:T(1,128)S(6)} %copy.7.active_ref, f32[2,3]{1,0:T(2,128)S(1)} %copy-done.2, f32[4]{0:T(128)S(1)} %copy-done.3, f32[4]{0:T(128)S(1)} %copy-done.4, ...), custom_call_target="tpu_custom_call" | custom-call | flops 10000000000 | bytes 100000000 | tf_op jit(solution)/shard_map/matter/pallas_call | solution.py:282
  12.6 0.0 collective-permute-done.left_ref.after_ref.later_ref
  12.7 2.6 %prints.3 = (f32[1,2,4,128,128]{4,3,2,1,0:T(8,128)S(1)}, s16[1,4,192,128]{3,2,1,0:T(8,128)(2,1)S(1)}) custom-call(f32[6,16,128,128]{3,2,1,0:T(8,128)S(1)} %get-tuple-element.24.field_ref, f32[17,8,128]{2,1,0:T(8,128)S(1)} %get-tuple-element.25.table_ref, bf16[16,512]{1,0:T(8,128)(2,1)S(1)} %collective-permute-done.left_ref.after_ref.later_ref, ...), custom_call_target="tpu_custom_call" | custom-call | flops 10000000000 | bytes 100000000 | tf_op jit(solution)/shard_map/prints/pallas_call | solution.py:293
  15.3 5.1 %collective-permute-start.2 = (s16[1,4,192,128]{3,2,1,0:T(8,128)(2,1)S(1)}, s16[1,4,192,128]{3,2,1,0:T(8,128)(2,1)S(1)}, u32[]{:S(2)}, u32[]{:S(2)}) collective-permute-start(s16[1,4,192,128]{3,2,1,0:T(8,128)(2,1)S(1)} %get-tuple-element.32), channel_id=1, source_target_pairs={{0,1},{1,2},{2,3},{3,4},{4,5},{5,6},{6,7},{8,9},{9,10},{10,11},{11... | collective-permute-start | bytes 589832 | tf_op jit(solution)/shard_map/ppermute | solution.py:331
  20.5 2.7 %matter.3 = (f32[2,16,128,128]{3,2,1,0:T(8,128)S(1)}, f32[2,3,16,128,128]{4,3,2,1,0:T(8,128)S(1)}, f32[2,16,128,128]{3,2,1,0:T(8,128)S(1)}) custom-call(f32[6,16,128,128]{3,2,1,0:T(8,128)S(1)} %get-tuple-element.24.field_ref, f32[17,8,128]{2,1,0:T(8,128)S(1)} %get-tuple-element.25.table_ref), custom_call_target="tpu_custom_call" | custom-call | flops 10000000000 | bytes 100000000 | tf_op jit(solution)/shard_map/matter/pallas_call | solution.py:278
  23.2 0.3 merge.2.after_ref
  23.5 2.7 %collective-permute-start.5 = (s16[2,4,128,128]{3,2,1,0:T(8,128)(2,1)S(1)}, s16[2,4,128,128]{3,2,1,0:T(8,128)(2,1)S(1)}, u32[]{:S(2)}, u32[]{:S(2)}) collective-permute-start(s16[2,4,128,128]{3,2,1,0:T(8,128)(2,1)S(1)} %merge.2.after_ref), channel_id=1, source_target_pairs={{0,16},{8,24},{16,0},{24,8},{1,17},{9,25},{17,1},{25,9},{2,18},{10... | collective-permute-start | bytes 786440 | tf_op jit(solution)/shard_map/ppermute | solution.py:336
  26.1 5.2 %prints.4 = (f32[2,2,4,128,128]{4,3,2,1,0:T(8,128)S(1)}, s16[2,4,192,128]{3,2,1,0:T(8,128)(2,1)S(1)}) custom-call(f32[6,16,128,128]{3,2,1,0:T(8,128)S(1)} %get-tuple-element.24.field_ref, f32[17,8,128]{2,1,0:T(8,128)S(1)} %get-tuple-element.25.table_ref, bf16[16,512]{1,0:T(8,128)(2,1)S(1)} %collective-permute-done.left_ref.after_ref.later_ref, ...), custom_call_target="tpu_custom_call" | custom-call | flops 10000000000 | bytes 100000000 | tf_op jit(solution)/shard_map/prints/pallas_call | solution.py:293
  31.4 3.4 %collective-permute-start.3 = (s16[2,4,192,128]{3,2,1,0:T(8,128)(2,1)S(1)}, s16[2,4,192,128]{3,2,1,0:T(8,128)(2,1)S(1)}, u32[]{:S(2)}, u32[]{:S(2)}) collective-permute-start(s16[2,4,192,128]{3,2,1,0:T(8,128)(2,1)S(1)} %get-tuple-element.38), channel_id=1, source_target_pairs={{0,1},{1,2},{2,3},{3,4},{4,5},{5,6},{6,7},{8,9},{9,10},{10,11},{11... | collective-permute-start | bytes 1179656 | tf_op jit(solution)/shard_map/ppermute | solution.py:331
  34.8 2.6 %prints.5 = (f32[1,2,4,128,128]{4,3,2,1,0:T(8,128)S(1)}, s16[1,4,192,128]{3,2,1,0:T(8,128)(2,1)S(1)}) custom-call(f32[6,16,128,128]{3,2,1,0:T(8,128)S(1)} %get-tuple-element.24.field_ref, f32[17,8,128]{2,1,0:T(8,128)S(1)} %get-tuple-element.25.table_ref, bf16[16,512]{1,0:T(8,128)(2,1)S(1)} %collective-permute-done.left_ref.after_ref.later_ref, ...), custom_call_target="tpu_custom_call" | custom-call | flops 10000000000 | bytes 100000000 | tf_op jit(solution)/shard_map/prints/pallas_call | solution.py:293
  37.4 0.0 copy-start.1
  37.4 0.5 merge.3
  38.0 1.6 %collective-permute-start.6 = (s16[2,4,128,128]{3,2,1,0:T(8,128)(2,1)S(1)}, s16[2,4,128,128]{3,2,1,0:T(8,128)(2,1)S(1)}, u32[]{:S(2)}, u32[]{:S(2)}) collective-permute-start(s16[2,4,128,128]{3,2,1,0:T(8,128)(2,1)S(1)} %get-tuple-element.41), channel_id=1, source_target_pairs={{0,8},{8,16},{16,24},{24,0},{1,9},{9,17},{17,25},{25,1},{2,10},{10... | collective-permute-start | bytes 786440 | tf_op jit(solution)/shard_map/ppermute | solution.py:336
  39.6 2.2 %collective-permute-start.7 = (s16[2,4,128,128]{3,2,1,0:T(8,128)(2,1)S(1)}, s16[2,4,128,128]{3,2,1,0:T(8,128)(2,1)S(1)}, u32[]{:S(2)}, u32[]{:S(2)}) collective-permute-start(s16[2,4,128,128]{3,2,1,0:T(8,128)(2,1)S(1)} %get-tuple-element.42), channel_id=1, source_target_pairs={{0,24},{8,0},{16,8},{24,16},{1,25},{9,1},{17,9},{25,17},{2,26},{10... | collective-permute-start | bytes 786440 | tf_op jit(solution)/shard_map/ppermute | solution.py:336
  41.8 6.0 %collective-permute-start.4 = (s16[1,4,192,128]{3,2,1,0:T(8,128)(2,1)S(1)}, s16[1,4,192,128]{3,2,1,0:T(8,128)(2,1)S(1)}, u32[]{:S(2)}, u32[]{:S(2)}) collective-permute-start(s16[1,4,192,128]{3,2,1,0:T(8,128)(2,1)S(1)} %get-tuple-element.40), channel_id=1, source_target_pairs={{0,1},{1,2},{2,3},{3,4},{4,5},{5,6},{6,7},{8,9},{9,10},{10,11},{11... | collective-permute-start | bytes 589832 | tf_op jit(solution)/shard_map/ppermute | solution.py:331
  47.8 1.0 %collective-permute-done.4.over_ref = s16[1,4,192,128]{3,2,1,0:T(8,128)(2,1)S(1)} collective-permute-done((s16[1,4,192,128]{3,2,1,0:T(8,128)(2,1)S(1)}, s16[1,4,192,128]{3,2,1,0:T(8,128)(2,1)S(1)}, u32[]{:S(2)}, u32[]{:S(2)}) %collective-permute-start.4) | collective-permute-done | bytes 196640 | tf_op jit(solution)/shard_map/ppermute | solution.py:331
  48.8 4.9 %collective-permute-done.7.refs_2_ = s16[2,4,128,128]{3,2,1,0:T(8,128)(2,1)S(1)} collective-permute-done((s16[2,4,128,128]{3,2,1,0:T(8,128)(2,1)S(1)}, s16[2,4,128,128]{3,2,1,0:T(8,128)(2,1)S(1)}, u32[]{:S(2)}, u32[]{:S(2)}) %collective-permute-start.7) | collective-permute-done | bytes 262176 | tf_op jit(solution)/shard_map/ppermute | solution.py:336
  53.8 1.4 %final.1 = s16[8,2,4,16,128]{4,3,2,1,0:T(8,128)(2,1)S(1)} custom-call(s32[2,4]{1,0:T(2,128)S(1)} %copy-done.1, f32[1,2,4,128,128]{4,3,2,1,0:T(8,128)S(1)} %get-tuple-element.37.own_ref, s16[1,4,192,128]{3,2,1,0:T(8,128)(2,1)S(1)} %collective-permute-done.4.over_ref, s16[2,4,128,128]{3,2,1,0:T(8,128)(2,1)S(1)} %collective-permute-done.5.refs_0_, ...), custom_call_target="tpu_custom_call" | custom-call | tf_op jit(solution)/shard_map/final/pallas_call | solution.py:314
  55.2 15.3 %all_to_all.5.blocks_ref = s16[8,2,4,16,128]{4,3,2,1,0:T(8,128)(2,1)S(1)} all-to-all(s16[8,2,4,16,128]{4,3,2,1,0:T(8,128)(2,1)S(1)} %final.1), channel_id=1, replica_groups=mesh['depth'=4,'tile'=8] {'tile'}, dimensions={0} | all-to-all | bytes 524288 | tf_op jit(solution)/shard_map/all_to_all | solution.py:366
  70.5 0.9 %place.1 = f32[2,4,16,1024]{3,2,1,0:T(8,128)} custom-call(s16[8,2,4,16,128]{4,3,2,1,0:T(8,128)(2,1)S(1)} %all_to_all.5.blocks_ref), custom_call_target="tpu_custom_call" | custom-call | tf_op jit(solution)/shard_map/place/pallas_call | solution.py:323
  (13 shorter events, 0.0 us)
Async XLA Ops:
  0.0 1.6 %copy-start = (bf16[512,16,128]{2,1,0:T(8,128)(2,1)S(1)}, bf16[512,16,128]{2,1,0:T(8,128)(2,1)}, u32[]{:S(2)}) copy-start(bf16[512,16,128]{2,1,0:T(8,128)(2,1)} %volume_ref.1) | copy-start | bytes 6291460
  1.6 7.7 %copy-start.2 = (f32[2,3]{1,0:T(2,128)S(1)}, f32[2,3]{1,0:T(2,128)}, u32[]{:S(2)}) copy-start(f32[2,3]{1,0:T(2,128)} %light_ref.1) | copy-start | bytes 76
  1.6 7.7 %copy-start.3 = (f32[4]{0:T(128)S(1)}, f32[4]{0:T(128)}, u32[]{:S(2)}) copy-start(f32[4]{0:T(128)} %gain_ref.1) | copy-start | bytes 52
  1.6 7.7 %copy-start.4 = (f32[4]{0:T(128)S(1)}, f32[4]{0:T(128)}, u32[]{:S(2)}) copy-start(f32[4]{0:T(128)} %bias_ref.1) | copy-start | bytes 52
  5.0 7.7 %collective-permute-start = (bf16[16,512]{1,0:T(8,128)(2,1)S(1)}, bf16[16,512]{1,0:T(8,128)(2,1)S(1)}, u32[]{:S(2)}, u32[]{:S(2)}) collective-permute-start(bf16[16,512]{1,0:T(8,128)(2,1)S(1)} %get-tuple-element.26), channel_id=1, source_target_pairs={{0,1},{1,2},{2,3},{3,4},{4,5},{5,6},{6,7},{8,9},{9,10},{10,11},{11... | collective-permute-start | bytes 49160 | tf_op jit(solution)/shard_map/ppermute | solution.py:331
  7.4 5.3 %collective-permute-start.1 = (bf16[16,512]{1,0:T(8,128)(2,1)S(1)}, bf16[16,512]{1,0:T(8,128)(2,1)S(1)}, u32[]{:S(2)}, u32[]{:S(2)}) collective-permute-start(bf16[16,512]{1,0:T(8,128)(2,1)S(1)} %get-tuple-element.27), channel_id=1, source_target_pairs={{1,0},{2,1},{3,2},{4,3},{5,4},{6,5},{7,6},{9,8},{10,9},{11,10},{12... | collective-permute-start | bytes 49160 | tf_op jit(solution)/shard_map/ppermute | solution.py:331
  15.3 7.9 %collective-permute-start.2 = (s16[1,4,192,128]{3,2,1,0:T(8,128)(2,1)S(1)}, s16[1,4,192,128]{3,2,1,0:T(8,128)(2,1)S(1)}, u32[]{:S(2)}, u32[]{:S(2)}) collective-permute-start(s16[1,4,192,128]{3,2,1,0:T(8,128)(2,1)S(1)} %get-tuple-element.32), channel_id=1, source_target_pairs={{0,1},{1,2},{2,3},{3,4},{4,5},{5,6},{6,7},{8,9},{9,10},{10,11},{11... | collective-permute-start | bytes 589832 | tf_op jit(solution)/shard_map/ppermute | solution.py:331
  23.5 24.3 %collective-permute-start.5 = (s16[2,4,128,128]{3,2,1,0:T(8,128)(2,1)S(1)}, s16[2,4,128,128]{3,2,1,0:T(8,128)(2,1)S(1)}, u32[]{:S(2)}, u32[]{:S(2)}) collective-permute-start(s16[2,4,128,128]{3,2,1,0:T(8,128)(2,1)S(1)} %merge.2.after_ref), channel_id=1, source_target_pairs={{0,16},{8,24},{16,0},{24,8},{1,17},{9,25},{17,1},{25,9},{2,18},{10... | collective-permute-start | bytes 786440 | tf_op jit(solution)/shard_map/ppermute | solution.py:336
  31.4 6.0 %collective-permute-start.3 = (s16[2,4,192,128]{3,2,1,0:T(8,128)(2,1)S(1)}, s16[2,4,192,128]{3,2,1,0:T(8,128)(2,1)S(1)}, u32[]{:S(2)}, u32[]{:S(2)}) collective-permute-start(s16[2,4,192,128]{3,2,1,0:T(8,128)(2,1)S(1)} %get-tuple-element.38), channel_id=1, source_target_pairs={{0,1},{1,2},{2,3},{3,4},{4,5},{5,6},{6,7},{8,9},{9,10},{10,11},{11... | collective-permute-start | bytes 1179656 | tf_op jit(solution)/shard_map/ppermute | solution.py:331
  37.4 16.3 %copy-start.1 = (s32[2,4]{1,0:T(2,128)S(1)}, s32[2,4]{1,0:T(2,128)}, u32[]{:S(2)}) copy-start(s32[2,4]{1,0:T(2,128)} %order_ref.1) | copy-start | bytes 100
  38.0 10.9 %collective-permute-start.6 = (s16[2,4,128,128]{3,2,1,0:T(8,128)(2,1)S(1)}, s16[2,4,128,128]{3,2,1,0:T(8,128)(2,1)S(1)}, u32[]{:S(2)}, u32[]{:S(2)}) collective-permute-start(s16[2,4,128,128]{3,2,1,0:T(8,128)(2,1)S(1)} %get-tuple-element.41), channel_id=1, source_target_pairs={{0,8},{8,16},{16,24},{24,0},{1,9},{9,17},{17,25},{25,1},{2,10},{10... | collective-permute-start | bytes 786440 | tf_op jit(solution)/shard_map/ppermute | solution.py:336
  39.6 14.2 %collective-permute-start.7 = (s16[2,4,128,128]{3,2,1,0:T(8,128)(2,1)S(1)}, s16[2,4,128,128]{3,2,1,0:T(8,128)(2,1)S(1)}, u32[]{:S(2)}, u32[]{:S(2)}) collective-permute-start(s16[2,4,128,128]{3,2,1,0:T(8,128)(2,1)S(1)} %get-tuple-element.42), channel_id=1, source_target_pairs={{0,24},{8,0},{16,8},{24,16},{1,25},{9,1},{17,9},{25,17},{2,26},{10... | collective-permute-start | bytes 786440 | tf_op jit(solution)/shard_map/ppermute | solution.py:336
  41.8 7.0 %collective-permute-start.4 = (s16[1,4,192,128]{3,2,1,0:T(8,128)(2,1)S(1)}, s16[1,4,192,128]{3,2,1,0:T(8,128)(2,1)S(1)}, u32[]{:S(2)}, u32[]{:S(2)}) collective-permute-start(s16[1,4,192,128]{3,2,1,0:T(8,128)(2,1)S(1)} %get-tuple-element.40), channel_id=1, source_target_pairs={{0,1},{1,2},{2,3},{3,4},{4,5},{5,6},{6,7},{8,9},{9,10},{10,11},{11... | collective-permute-start | bytes 589832 | tf_op jit(solution)/shard_map/ppermute | solution.py:331

commit v4 on v3

--- a/solution.py
+++ b/solution.py
@@ -29,34 +29,28 @@
     return jnp.where(value == code_none, 0.0, lax.exp2(value * (1.0 / code_step) - code_middle))
 
 
-def turn_kernel(volume_ref, field_ref, low_ref, high_ref, brick, ordered, arrived):
+def turn_kernel(volume_ref, field_ref, low_ref, high_ref, ordered):
     rows, slices, columns = volume_ref.shape
     blocks, _, _, width = field_ref.shape
     blocks = blocks - 2
-    copies = []
-    for block in range(blocks):
-        part = pl.ds(block * width, width)
-        copies.append(pltpu.make_async_copy(volume_ref.at[part], brick.at[part], arrived.at[block]))
-    for copy in copies:
-        copy.start()
+
+    def order(index, carry):
+        at = pl.multiple_of(index * slices, slices)
+        ordered[:, pl.ds(at, slices), :] = jnp.swapaxes(volume_ref[pl.ds(at, slices)], 0, 1)
+        return carry
+
+    lax.fori_loop(0, rows // slices, order, 0, unroll=4)
     field_ref[0] = jnp.zeros((slices, columns, width), jnp.float32)
     field_ref[blocks + 1] = jnp.zeros((slices, columns, width), jnp.float32)
-    for block in range(blocks):
-        copies[block].wait()
-
-        def order(index, carry):
-            at = pl.multiple_of(block * width + index * slices, slices)
-            ordered[:, pl.ds(at, slices), :] = jnp.swapaxes(brick[pl.ds(at, slices)], 0, 1)
-            return carry
-
-        lax.fori_loop(0, width // slices, order, 0, unroll=2)
-
-        def turn(z, carry):
+
+    def turn(z, carry):
+        for block in range(blocks):
             field_ref[block + 1, z] = ordered[z, block * width:(block + 1) * width, :].T.astype(jnp.float32)
-            return carry
-
-        lax.fori_loop(0, slices, turn, 0, unroll=2)
-        for edge_ref, x in ((low_ref, 0), (high_ref, columns - 1)):
+        return carry
+
+    lax.fori_loop(0, slices, turn, 0)
+    for edge_ref, x in ((low_ref, 0), (high_ref, columns - 1)):
+        for block in range(blocks):
             edge_ref[:, block * width:(block + 1) * width] = field_ref[block + 1, :, x, :].astype(edge_ref.dtype)
 
 
@@ -76,7 +70,7 @@
         table_ref[index] = value
 
 
-def matter_kernel(shifts, field_ref, table_ref, thick_ref, tints_ref, slope_ref):
+def matter_kernel(shifts, field_ref, table_ref, after_ref, thick_ref, tints_ref, slope_ref):
     _, slices, columns, width = thick_ref.shape
     group = table_ref.shape[1]
     scale = table_ref[0]
@@ -115,7 +109,7 @@
 
 def first_matter_kernel(shifts, total_z, active_ref, light_ref, gain_ref, bias_ref, field_ref, table_ref, *refs):
     make_table(total_z, active_ref, light_ref, gain_ref, bias_ref, table_ref)
-    matter_kernel(shifts, field_ref, table_ref, *refs)
+    matter_kernel(shifts, field_ref, table_ref, None, *refs)
 
 
 def print_kernel(parts, matters, field_ref, table_ref, left_ref, right_ref, after_ref, *refs):
@@ -138,8 +132,9 @@
     for part in sums:
         part[...] = jnp.zeros(part.shape, jnp.float32)
     along = pl.ds(pl.multiple_of(block * width, width), width)
-    left = left_ref[:, along].astype(jnp.float32)
-    right = right_ref[:, along].astype(jnp.float32)
+    tile = lax.axis_index("tile")
+    left = left_ref[:, along].astype(jnp.float32) * jnp.where(tile > 0, 1.0, 0.0)
+    right = right_ref[:, along].astype(jnp.float32) * jnp.where(tile + 1 < lax.axis_size("tile"), 1.0, 0.0)
 
     def work(j):
         base = j * group if isinstance(j, int) else pl.multiple_of(j * group, group)
@@ -202,7 +197,8 @@
 def merged(own_ref, over_ref, v, slices):
     first, count = over_rows(v, slices, own_ref.shape[2])
     through = lax.exp2(own_ref[v, 3, :count, :])
-    overs = [decode(over_ref[k, first:first + count, :]) for k in range(4)]
+    inside = jnp.where(lax.axis_index("tile") > 0, 1.0, 0.0)
+    overs = [decode(over_ref[k, first:first + count, :]) * inside for k in range(4)]
     tops = [own_ref[v, k, :count, :] + through * overs[k] for k in range(3)] + [overs[3] - own_ref[v, 3, :count, :]]
     if count == own_ref.shape[2]:
         return tops
@@ -262,22 +258,20 @@
     return pl.pallas_call(
         turn_kernel,
         out_shape=[jax.ShapeDtypeStruct((blocks + 2, slices, columns, width), jnp.float32), edge, edge],
-        in_specs=[far], out_specs=[vmem] * 3,
-        scratch_shapes=[pltpu.VMEM(volume.shape, volume.dtype), pltpu.VMEM((slices, rows, columns), volume.dtype),
-                        pltpu.SemaphoreType.DMA((blocks,))],
+        in_specs=[vmem], out_specs=[vmem] * 3, scratch_shapes=[pltpu.VMEM((slices, rows, columns), volume.dtype)],
         cost_estimate=pl.CostEstimate(flops=1, bytes_accessed=16 * 1024 * 1024, transcendentals=0),
         compiler_params=turn_params, name="turn_rows")(volume)
 
 
-def matter_of(field, shifts, table=None, smalls=(), after=()):
+def matter_of(field, shifts, table=None, smalls=(), after=None):
     blocks, slices, columns, width = field.shape
     shape = (len(shifts), slices, columns, width)
     outs = [jax.ShapeDtypeStruct(shape, jnp.float32), jax.ShapeDtypeStruct((len(shifts), 3) + shape[1:], jnp.float32),
             jax.ShapeDtypeStruct(shape, jnp.float32)]
     if table is not None:
         return pl.pallas_call(
-            functools.partial(matter_kernel, shifts), out_shape=outs, in_specs=[vmem] * 2, out_specs=[vmem] * 3,
-            cost_estimate=small_cost, compiler_params=params, name="matter")(field, table)
+            functools.partial(matter_kernel, shifts), out_shape=outs, in_specs=[vmem] * 2 + [far], out_specs=[vmem] * 3,
+            cost_estimate=small_cost, compiler_params=params, name="matter")(field, table, after)
     table = jax.ShapeDtypeStruct((9 + 4 * smalls[1].shape[0], 8, width), jnp.float32)
     return pl.pallas_call(
         functools.partial(first_matter_kernel, shifts, slices * (blocks - 2)), out_shape=[table] + outs,
@@ -323,12 +317,6 @@
     return pl.pallas_call(
         place_kernel, out_shape=jax.ShapeDtypeStruct((views, channels, share, tiles * columns), jnp.float32),
         in_specs=[vmem], out_specs=vmem, compiler_params=params, name="place")(blocks)
-
-
-def passed_along(x, axis, by):
-    devices = lax.axis_size(axis)
-    pairs = [(i, i + by) for i in range(devices) if 0 <= i + by < devices]
-    return lax.ppermute(x, axis, pairs)
 
 
 def passed_round(x, axis, by):
@@ -342,27 +330,34 @@
     rows, slices, columns = volume.shape
     share = rows // (depth_count * tile_count)
     field, low, high = turn_volume(volume, depth_count)
-    left = passed_along(high, "tile", 1)
-    right = passed_along(low, "tile", -1)
+    left = passed_round(high, "tile", 1)
+    right = passed_round(low, "tile", -1)
     shifts = sorted(range(1, depth_count), key=lambda shift: -min(shift, depth_count - shift)) + [0]
     half = (len(shifts) + 1) // 2
     table, *early = matter_of(field, shifts[:half], smalls=(active, light_vector, class_gain, class_bias))
-    late = matter_of(field, shifts[half:], table=table)
     sources = [(shift, index // half, index % half) for index, shift in enumerate(shifts)]
 
-    def chunks(parts, after):
-        return prints_of(field, (early, late) if any(part[1] for part in parts) else (early,), table, left, right, after,
-                         parts, light_vector.shape[0])
-
-    own, over = chunks(sources[:1], left)
-    layer, = merge_of(own, passed_along(over, "tile", 1), left, slices, 0)
-    layers = [passed_round(layer, "depth", shifts[0])]
-    middle, middle_over = chunks(sources[1:-1], layer)
-    last, last_over = chunks(sources[-1:], middle)
-    *middle_layers, last_over = merge_of(middle, passed_along(middle_over, "tile", 1), last_over, slices, 1)
-    last_over = passed_along(last_over, "tile", 1)
-    layers += [passed_round(layer, "depth", shift) for layer, shift in zip(middle_layers, shifts[1:-1])]
-    blocks = final_of(depth_order, last, last_over, layers, shifts[:-1], share, slices)
+    def chunk(index, after):
+        matters = (early,) if index < half else (late,)
+        return prints_of(field, matters, table, left, right, after, [(shifts[index], 0, index % half)], light_vector.shape[0])
+
+    ready, waiting, layers = left, None, []
+    for index in range(len(shifts)):
+        if index == half:
+            late = matter_of(field, shifts[half:], table=table, after=ready)
+            layer, = merge_of(*waiting, late[0], slices, 0)
+            layers.append(layer)
+            ready, waiting = layer, None
+        own, over = chunk(index, ready)
+        ready = own
+        if waiting is not None:
+            layer, *passed = merge_of(*waiting, over, slices, int(index + 1 == len(shifts)))
+            over = passed[0] if passed else over
+            layers.append(layer)
+            ready = layer
+        waiting = own, passed_round(over, "tile", 1)
+    layers = [passed_round(layer, "depth", shift) for layer, shift in zip(layers, shifts)]
+    blocks = final_of(depth_order, *waiting, layers, shifts[:-1], share, slices)
     blocks = lax.all_to_all(blocks, "tile", split_axis=0, concat_axis=0, tiled=True)
     return place_of(blocks)
 

time: 71.7 us -> 57.6 us (0.80)
  starting transfers between devices: 24.7 us -> 12.3 us
  blocking collectives: 15.3 us -> 9.53 us
  waiting for transfers between devices: 5.96 us -> 11.3 us
  Pallas kernels: 23 us -> 21.8 us
    ppermute x5 -> x0, starting transfers between devices: 18.1 us -> none  [passed_along(): return lax.ppermute(x, axis, pairs)]
    ppermute x3 -> x9, waiting for transfers between devices: 4.92 us -> 11.3 us  [passed_round(): lax.ppermute(x, axis, [(i, (i + by) % devices) for i in range(devices)])]
    all_to_all x1, blocking collectives: 15.3 us -> 9.53 us  [local(): lax.all_to_all(blocks, 'tile', split_axis=0, concat_axis=0, tiled=True)]
    ppermute x3 -> x9, starting transfers between devices: 6.53 us -> 12.3 us  [passed_round(): lax.ppermute(x, axis, [(i, (i + by) % devices) for i in range(devices)])]
    pallas_call x1, Pallas kernels: 3.39 us -> 2.27 us  [turn_volume(): pl.pallas_call(turn_kernel, out_shape=[jax.ShapeDtypeStruct((blocks + 2,...]
    ppermute x5 -> x0, waiting for transfers between devices: 1.04 us -> none  [passed_along(): return lax.ppermute(x, axis, pairs)]
    pallas_call x3 -> x4, Pallas kernels: 10.5 us -> 10.4 us  [prints_of(): pl.pallas_call(functools.partial(print_kernel, parts, len(matters)), out_...]
  transfers between devices with their start and end apart: 8 -> 9, of which waited for: 2 -> 4; matrix products, arithmetic and copies ran while one was open for 0% -> 0% of each run, Pallas kernels for 20% -> 26%
where the time goes in v4:
time: 57.6 us; the launch traced here: 57.4 us
  Pallas kernels  21.8 us (38%)
  starting transfers between devices  12.3 us (21%)
  waiting for transfers between devices  11.3 us (20%)
  blocking collectives  9.53 us (17%)
  local copies, waits for them, and re-layouts  1.61 us (3%)
  between operations  0.79 us (1%)
    ppermute x9, starting transfers between devices, passed_round(): lax.ppermute(x, axis, [(i, (i + by) % devices) for i in range(devices)])  12.3 us
    ppermute x9, waiting for transfers between devices, passed_round(): lax.ppermute(x, axis, [(i, (i + by) % devices) for i in range(devices)])  11.3 us
    pallas_call x4, Pallas kernels, prints_of(): pl.pallas_call(functools.partial(print_kernel, parts, len(matters)), out_...  10.4 us
    all_to_all x1, blocking collectives, local(): lax.all_to_all(blocks, 'tile', split_axis=0, concat_axis=0, tiled=True)  9.53 us
    pallas_call x1, Pallas kernels, matter_of(): pl.pallas_call(functools.partial(first_matter_kernel, shifts, slices * (b...  3.3 us
    pallas_call x1, Pallas kernels, matter_of(): pl.pallas_call(functools.partial(matter_kernel, shifts), out_shape=outs,...  2.72 us
    pallas_call x1, Pallas kernels, turn_volume(): pl.pallas_call(turn_kernel, out_shape=[jax.ShapeDtypeStruct((blocks + 2,...  2.27 us
    unnamed x10, local copies, waits for them, and re-layouts  1.61 us
  transfers between devices with their start and end apart: 9, of which 4 were waited for; matrix products, arithmetic and copies ran while one was open for 0% of the time, Pallas kernels for 26%

profile of v4, /device:TPU:0, one launch (start us, length us, event | category | flops | bytes accessed | tf_op | source)
XLA Modules:
  0.0 57.4 jit_solution(4598665712917209191)
XLA Ops:
  0.0 1.6 %copy-done = bf16[512,16,128]{2,1,0:T(8,128)(2,1)S(1)} copy-done((bf16[512,16,128]{2,1,0:T(8,128)(2,1)S(1)}, bf16[512,16,128]{2,1,0:T(8,128)(2,1)}, u32[]{:S(2)}) %copy-start) | copy-done | bytes 2097176
  1.6 2.3 %turn_rows.1 = (f32[6,16,128,128]{3,2,1,0:T(8,128)S(1)}, bf16[16,512]{1,0:T(8,128)(2,1)S(1)}, bf16[16,512]{1,0:T(8,128)(2,1)S(1)}) custom-call(bf16[512,16,128]{2,1,0:T(8,128)(2,1)S(1)} %copy-done), custom_call_target="tpu_custom_call" | custom-call | flops 1 | bytes 16777216 | tf_op jit(solution)/shard_map/turn_rows/pallas_call | solution.py:258
  3.9 0.5 collective-permute-start
  4.4 2.9 %collective-permute-start.1 = (bf16[16,512]{1,0:T(8,128)(2,1)S(1)}, bf16[16,512]{1,0:T(8,128)(2,1)S(1)}, u32[]{:S(2)}, u32[]{:S(2)}) collective-permute-start(bf16[16,512]{1,0:T(8,128)(2,1)S(1)} %get-tuple-element.28), channel_id=1, source_target_pairs={{0,7},{1,0},{2,1},{3,2},{4,3},{5,4},{6,5},{7,6},{8,15},{9,8},{10,9... | collective-permute-start | bytes 49160 | tf_op jit(solution)/shard_map/ppermute | solution.py:324
  8.0 3.3 %matter.2 = (f32[17,8,128]{2,1,0:T(8,128)S(1)}, f32[2,16,128,128]{3,2,1,0:T(8,128)S(1)}, f32[2,3,16,128,128]{4,3,2,1,0:T(8,128)S(1)}, f32[2,16,128,128]{3,2,1,0:T(8,128)S(1)}) custom-call(s32[1,1]{1,0:T(1,128)S(6)} %copy.7.active_ref, f32[2,3]{1,0:T(2,128)S(1)} %copy-done.2, f32[4]{0:T(128)S(1)} %copy-done.3, f32[4]{0:T(128)S(1)} %copy-done.4, ...), custom_call_target="tpu_custom_call" | custom-call | flops 10000000000 | bytes 100000000 | tf_op jit(solution)/shard_map/matter/pallas_call | solution.py:276
  11.3 2.6 %prints.4 = (f32[1,2,4,128,128]{4,3,2,1,0:T(8,128)S(1)}, s16[1,4,192,128]{3,2,1,0:T(8,128)(2,1)S(1)}) custom-call(f32[6,16,128,128]{3,2,1,0:T(8,128)S(1)} %get-tuple-element.25.field_ref, f32[17,8,128]{2,1,0:T(8,128)S(1)} %get-tuple-element.26.table_ref, bf16[16,512]{1,0:T(8,128)(2,1)S(1)} %collective-permute-done.left_ref.after_ref, ...), custom_call_target="tpu_custom_call" | custom-call | flops 10000000000 | bytes 100000000 | tf_op jit(solution)/shard_map/prints/pallas_call | solution.py:287
  14.0 2.6 %prints.5 = (f32[1,2,4,128,128]{4,3,2,1,0:T(8,128)S(1)}, s16[1,4,192,128]{3,2,1,0:T(8,128)(2,1)S(1)}) custom-call(f32[6,16,128,128]{3,2,1,0:T(8,128)S(1)} %get-tuple-element.25.field_ref, f32[17,8,128]{2,1,0:T(8,128)S(1)} %get-tuple-element.26.table_ref, bf16[16,512]{1,0:T(8,128)(2,1)S(1)} %collective-permute-done.left_ref.after_ref, ...), custom_call_target="tpu_custom_call" | custom-call | flops 10000000000 | bytes 100000000 | tf_op jit(solution)/shard_map/prints/pallas_call | solution.py:287
  16.6 1.4 %collective-permute-start.2 = (s16[1,4,192,128]{3,2,1,0:T(8,128)(2,1)S(1)}, s16[1,4,192,128]{3,2,1,0:T(8,128)(2,1)S(1)}, u32[]{:S(2)}, u32[]{:S(2)}) collective-permute-start(s16[1,4,192,128]{3,2,1,0:T(8,128)(2,1)S(1)} %get-tuple-element.34.later_ref), channel_id=1, source_target_pairs={{0,1},{1,2},{2,3},{3,4},{4,5},{5,6},{6,7},{7,0},{8,9},{9,10},{10,1... | collective-permute-start | bytes 589832 | tf_op jit(solution)/shard_map/ppermute | solution.py:324
  18.0 2.0 %collective-permute-done.3.over_ref = s16[1,4,192,128]{3,2,1,0:T(8,128)(2,1)S(1)} collective-permute-done((s16[1,4,192,128]{3,2,1,0:T(8,128)(2,1)S(1)}, s16[1,4,192,128]{3,2,1,0:T(8,128)(2,1)S(1)}, u32[]{:S(2)}, u32[]{:S(2)}) %collective-permute-start.3) | collective-permute-done | bytes 196640 | tf_op jit(solution)/shard_map/ppermute | solution.py:324
  20.0 0.3 merge.3.after_ref
  20.3 3.3 %collective-permute-start.6 = (s16[2,4,128,128]{3,2,1,0:T(8,128)(2,1)S(1)}, s16[2,4,128,128]{3,2,1,0:T(8,128)(2,1)S(1)}, u32[]{:S(2)}, u32[]{:S(2)}) collective-permute-start(s16[2,4,128,128]{3,2,1,0:T(8,128)(2,1)S(1)} %merge.3.after_ref), channel_id=1, source_target_pairs={{0,16},{8,24},{16,0},{24,8},{1,17},{9,25},{17,1},{25,9},{2,18},{10... | collective-permute-start | bytes 786440 | tf_op jit(solution)/shard_map/ppermute | solution.py:324
  23.6 2.7 %matter.3 = (f32[2,16,128,128]{3,2,1,0:T(8,128)S(1)}, f32[2,3,16,128,128]{4,3,2,1,0:T(8,128)S(1)}, f32[2,16,128,128]{3,2,1,0:T(8,128)S(1)}) custom-call(f32[6,16,128,128]{3,2,1,0:T(8,128)S(1)} %get-tuple-element.25.field_ref, f32[17,8,128]{2,1,0:T(8,128)S(1)} %get-tuple-element.26.table_ref, s16[2,4,128,128]{3,2,1,0:T(8,128)(2,1)S(1)} %merge.3.after_ref), custom_call_target="tpu_custom_call" | custom-call | flops 10000000000 | bytes 100000000 | tf_op jit(solution)/shard_map/matter/pallas_call | solution.py:272
  26.4 0.3 merge.4.after_ref
  26.6 1.6 %collective-permute-start.7 = (s16[2,4,128,128]{3,2,1,0:T(8,128)(2,1)S(1)}, s16[2,4,128,128]{3,2,1,0:T(8,128)(2,1)S(1)}, u32[]{:S(2)}, u32[]{:S(2)}) collective-permute-start(s16[2,4,128,128]{3,2,1,0:T(8,128)(2,1)S(1)} %merge.4.after_ref), channel_id=1, source_target_pairs={{0,8},{8,16},{16,24},{24,0},{1,9},{9,17},{17,25},{25,1},{2,10},{10... | collective-permute-start | bytes 786440 | tf_op jit(solution)/shard_map/ppermute | solution.py:324
  28.3 2.6 %prints.6 = (f32[1,2,4,128,128]{4,3,2,1,0:T(8,128)S(1)}, s16[1,4,192,128]{3,2,1,0:T(8,128)(2,1)S(1)}) custom-call(f32[6,16,128,128]{3,2,1,0:T(8,128)S(1)} %get-tuple-element.25.field_ref, f32[17,8,128]{2,1,0:T(8,128)S(1)} %get-tuple-element.26.table_ref, bf16[16,512]{1,0:T(8,128)(2,1)S(1)} %collective-permute-done.left_ref.after_ref, ...), custom_call_target="tpu_custom_call" | custom-call | flops 10000000000 | bytes 100000000 | tf_op jit(solution)/shard_map/prints/pallas_call | solution.py:287
  30.9 2.6 %prints.7 = (f32[1,2,4,128,128]{4,3,2,1,0:T(8,128)S(1)}, s16[1,4,192,128]{3,2,1,0:T(8,128)(2,1)S(1)}) custom-call(f32[6,16,128,128]{3,2,1,0:T(8,128)S(1)} %get-tuple-element.25.field_ref, f32[17,8,128]{2,1,0:T(8,128)S(1)} %get-tuple-element.26.table_ref, bf16[16,512]{1,0:T(8,128)(2,1)S(1)} %collective-permute-done.left_ref.after_ref, ...), custom_call_target="tpu_custom_call" | custom-call | flops 10000000000 | bytes 100000000 | tf_op jit(solution)/shard_map/prints/pallas_call | solution.py:287
  33.6 3.4 %collective-permute-done.4.over_ref = s16[1,4,192,128]{3,2,1,0:T(8,128)(2,1)S(1)} collective-permute-done((s16[1,4,192,128]{3,2,1,0:T(8,128)(2,1)S(1)}, s16[1,4,192,128]{3,2,1,0:T(8,128)(2,1)S(1)}, u32[]{:S(2)}, u32[]{:S(2)}) %collective-permute-start.4) | collective-permute-done | bytes 196640 | tf_op jit(solution)/shard_map/ppermute | solution.py:324
  36.9 0.3 merge.5
  37.2 2.3 %collective-permute-start.8 = (s16[2,4,128,128]{3,2,1,0:T(8,128)(2,1)S(1)}, s16[2,4,128,128]{3,2,1,0:T(8,128)(2,1)S(1)}, u32[]{:S(2)}, u32[]{:S(2)}) collective-permute-start(s16[2,4,128,128]{3,2,1,0:T(8,128)(2,1)S(1)} %get-tuple-element.44), channel_id=1, source_target_pairs={{0,24},{8,0},{16,8},{24,16},{1,25},{9,1},{17,9},{25,17},{2,26},{10... | collective-permute-start | bytes 786440 | tf_op jit(solution)/shard_map/ppermute | solution.py:324
  39.5 0.4 collective-permute-done.6.refs_0_
  39.9 5.6 %collective-permute-done.5.over_ref = s16[1,4,192,128]{3,2,1,0:T(8,128)(2,1)S(1)} collective-permute-done((s16[1,4,192,128]{3,2,1,0:T(8,128)(2,1)S(1)}, s16[1,4,192,128]{3,2,1,0:T(8,128)(2,1)S(1)}, u32[]{:S(2)}, u32[]{:S(2)}) %collective-permute-start.5) | collective-permute-done | bytes 196640 | tf_op jit(solution)/shard_map/ppermute | solution.py:324
  45.5 1.4 %final.1 = s16[8,2,4,16,128]{4,3,2,1,0:T(8,128)(2,1)S(1)} custom-call(s32[2,4]{1,0:T(2,128)S(1)} %copy-done.1, f32[1,2,4,128,128]{4,3,2,1,0:T(8,128)S(1)} %get-tuple-element.40.own_ref, s16[1,4,192,128]{3,2,1,0:T(8,128)(2,1)S(1)} %collective-permute-done.5.over_ref, s16[2,4,128,128]{3,2,1,0:T(8,128)(2,1)S(1)} %collective-permute-done.6.refs_0_, ...), custom_call_target="tpu_custom_call" | custom-call | tf_op jit(solution)/shard_map/final/pallas_call | solution.py:308
  46.9 9.5 %all_to_all.5.blocks_ref = s16[8,2,4,16,128]{4,3,2,1,0:T(8,128)(2,1)S(1)} all-to-all(s16[8,2,4,16,128]{4,3,2,1,0:T(8,128)(2,1)S(1)} %final.1), channel_id=1, replica_groups=mesh['depth'=4,'tile'=8] {'tile'}, dimensions={0} | all-to-all | bytes 524288 | tf_op jit(solution)/shard_map/all_to_all | solution.py:361
  56.5 0.9 %place.1 = f32[2,4,16,1024]{3,2,1,0:T(8,128)} custom-call(s16[8,2,4,16,128]{4,3,2,1,0:T(8,128)(2,1)S(1)} %all_to_all.5.blocks_ref), custom_call_target="tpu_custom_call" | custom-call | tf_op jit(solution)/shard_map/place/pallas_call | solution.py:317
  (17 shorter events, 0.1 us)
Async XLA Ops:
  0.0 1.6 %copy-start = (bf16[512,16,128]{2,1,0:T(8,128)(2,1)S(1)}, bf16[512,16,128]{2,1,0:T(8,128)(2,1)}, u32[]{:S(2)}) copy-start(bf16[512,16,128]{2,1,0:T(8,128)(2,1)} %volume_ref.1) | copy-start | bytes 6291460
  1.6 6.4 %copy-start.2 = (f32[2,3]{1,0:T(2,128)S(1)}, f32[2,3]{1,0:T(2,128)}, u32[]{:S(2)}) copy-start(f32[2,3]{1,0:T(2,128)} %light_ref.1) | copy-start | bytes 76
  1.6 6.4 %copy-start.3 = (f32[4]{0:T(128)S(1)}, f32[4]{0:T(128)}, u32[]{:S(2)}) copy-start(f32[4]{0:T(128)} %gain_ref.1) | copy-start | bytes 52
  1.6 6.4 %copy-start.4 = (f32[4]{0:T(128)S(1)}, f32[4]{0:T(128)}, u32[]{:S(2)}) copy-start(f32[4]{0:T(128)} %bias_ref.1) | copy-start | bytes 52
  3.9 7.4 %collective-permute-start = (bf16[16,512]{1,0:T(8,128)(2,1)S(1)}, bf16[16,512]{1,0:T(8,128)(2,1)S(1)}, u32[]{:S(2)}, u32[]{:S(2)}) collective-permute-start(bf16[16,512]{1,0:T(8,128)(2,1)S(1)} %get-tuple-element.27), channel_id=1, source_target_pairs={{0,1},{1,2},{2,3},{3,4},{4,5},{5,6},{6,7},{7,0},{8,9},{9,10},{10,1... | collective-permute-start | bytes 49160 | tf_op jit(solution)/shard_map/ppermute | solution.py:324
  4.4 7.0 %collective-permute-start.1 = (bf16[16,512]{1,0:T(8,128)(2,1)S(1)}, bf16[16,512]{1,0:T(8,128)(2,1)S(1)}, u32[]{:S(2)}, u32[]{:S(2)}) collective-permute-start(bf16[16,512]{1,0:T(8,128)(2,1)S(1)} %get-tuple-element.28), channel_id=1, source_target_pairs={{0,7},{1,0},{2,1},{3,2},{4,3},{5,4},{6,5},{7,6},{8,15},{9,8},{10,9... | collective-permute-start | bytes 49160 | tf_op jit(solution)/shard_map/ppermute | solution.py:324
  13.9 6.0 %collective-permute-start.3 = (s16[1,4,192,128]{3,2,1,0:T(8,128)(2,1)S(1)}, s16[1,4,192,128]{3,2,1,0:T(8,128)(2,1)S(1)}, u32[]{:S(2)}, u32[]{:S(2)}) collective-permute-start(s16[1,4,192,128]{3,2,1,0:T(8,128)(2,1)S(1)} %get-tuple-element.35), channel_id=1, source_target_pairs={{0,1},{1,2},{2,3},{3,4},{4,5},{5,6},{6,7},{7,0},{8,9},{9,10},{10,1... | collective-permute-start | bytes 589832 | tf_op jit(solution)/shard_map/ppermute | solution.py:324
  16.6 9.8 %collective-permute-start.2 = (s16[1,4,192,128]{3,2,1,0:T(8,128)(2,1)S(1)}, s16[1,4,192,128]{3,2,1,0:T(8,128)(2,1)S(1)}, u32[]{:S(2)}, u32[]{:S(2)}) collective-permute-start(s16[1,4,192,128]{3,2,1,0:T(8,128)(2,1)S(1)} %get-tuple-element.34.later_ref), channel_id=1, source_target_pairs={{0,1},{1,2},{2,3},{3,4},{4,5},{5,6},{6,7},{7,0},{8,9},{9,10},{10,1... | collective-permute-start | bytes 589832 | tf_op jit(solution)/shard_map/ppermute | solution.py:324
  20.3 19.7 %collective-permute-start.6 = (s16[2,4,128,128]{3,2,1,0:T(8,128)(2,1)S(1)}, s16[2,4,128,128]{3,2,1,0:T(8,128)(2,1)S(1)}, u32[]{:S(2)}, u32[]{:S(2)}) collective-permute-start(s16[2,4,128,128]{3,2,1,0:T(8,128)(2,1)S(1)} %merge.3.after_ref), channel_id=1, source_target_pairs={{0,16},{8,24},{16,0},{24,8},{1,17},{9,25},{17,1},{25,9},{2,18},{10... | collective-permute-start | bytes 786440 | tf_op jit(solution)/shard_map/ppermute | solution.py:324
  26.6 13.3 %collective-permute-start.7 = (s16[2,4,128,128]{3,2,1,0:T(8,128)(2,1)S(1)}, s16[2,4,128,128]{3,2,1,0:T(8,128)(2,1)S(1)}, u32[]{:S(2)}, u32[]{:S(2)}) collective-permute-start(s16[2,4,128,128]{3,2,1,0:T(8,128)(2,1)S(1)} %merge.4.after_ref), channel_id=1, source_target_pairs={{0,8},{8,16},{16,24},{24,0},{1,9},{9,17},{17,25},{25,1},{2,10},{10... | collective-permute-start | bytes 786440 | tf_op jit(solution)/shard_map/ppermute | solution.py:324
  30.9 6.0 %collective-permute-start.4 = (s16[1,4,192,128]{3,2,1,0:T(8,128)(2,1)S(1)}, s16[1,4,192,128]{3,2,1,0:T(8,128)(2,1)S(1)}, u32[]{:S(2)}, u32[]{:S(2)}) collective-permute-start(s16[1,4,192,128]{3,2,1,0:T(8,128)(2,1)S(1)} %get-tuple-element.41), channel_id=1, source_target_pairs={{0,1},{1,2},{2,3},{3,4},{4,5},{5,6},{6,7},{7,0},{8,9},{9,10},{10,1... | collective-permute-start | bytes 589832 | tf_op jit(solution)/shard_map/ppermute | solution.py:324
  36.9 8.6 %copy-start.1 = (s32[2,4]{1,0:T(2,128)S(1)}, s32[2,4]{1,0:T(2,128)}, u32[]{:S(2)}) copy-start(s32[2,4]{1,0:T(2,128)} %order_ref.1) | copy-start | bytes 100
  37.2 8.3 %collective-permute-start.8 = (s16[2,4,128,128]{3,2,1,0:T(8,128)(2,1)S(1)}, s16[2,4,128,128]{3,2,1,0:T(8,128)(2,1)S(1)}, u32[]{:S(2)}, u32[]{:S(2)}) collective-permute-start(s16[2,4,128,128]{3,2,1,0:T(8,128)(2,1)S(1)} %get-tuple-element.44), channel_id=1, source_target_pairs={{0,24},{8,0},{16,8},{24,16},{1,25},{9,1},{17,9},{25,17},{2,26},{10... | collective-permute-start | bytes 786440 | tf_op jit(solution)/shard_map/ppermute | solution.py:324
  39.5 6.0 %collective-permute-start.5 = (s16[1,4,192,128]{3,2,1,0:T(8,128)(2,1)S(1)}, s16[1,4,192,128]{3,2,1,0:T(8,128)(2,1)S(1)}, u32[]{:S(2)}, u32[]{:S(2)}) collective-permute-start(s16[1,4,192,128]{3,2,1,0:T(8,128)(2,1)S(1)} %get-tuple-element.43), channel_id=1, source_target_pairs={{0,1},{1,2},{2,3},{3,4},{4,5},{5,6},{6,7},{7,0},{8,9},{9,10},{10,1... | collective-permute-start | bytes 589832 | tf_op jit(solution)/shard_map/ppermute | solution.py:324

commit v5 on v4

v5 whole, which is shorter than its diff:
```python
import functools
import math
import jax
import jax.numpy as jnp
from jax import lax
from jax.experimental import pallas as pl
from jax.experimental.pallas import tpu as pltpu
from jax.sharding import PartitionSpec as P

LN2 = math.log(2.0)
code_step = 1638.0
code_middle = 16.0
code_none = -32768.0

smem = pl.BlockSpec(memory_space=pltpu.SMEM)
vmem = pl.BlockSpec(memory_space=pltpu.VMEM)
far = pl.BlockSpec(memory_space=pl.ANY)
long_cost = pl.CostEstimate(flops=10**10, bytes_accessed=10**8, transcendentals=0)
short_cost = pl.CostEstimate(flops=10**8, bytes_accessed=10**6, transcendentals=0)
params = pltpu.CompilerParams(vmem_limit_bytes=12 * 1024 * 1024)
turn_params = pltpu.CompilerParams(vmem_limit_bytes=12 * 1024 * 1024)


def encode(x):
    return jnp.round(jnp.maximum(code_step * lax.log2(x) + code_step * code_middle, code_none)).astype(jnp.int16)


def decode(q):
    value = q.astype(jnp.int32).astype(jnp.float32)
    return jnp.where(value == code_none, 0.0, lax.exp2(value * (1.0 / code_step) - code_middle))


def turn_kernel(volume_ref, field_ref, low_ref, high_ref, ordered):
    rows, slices, columns = volume_ref.shape
    blocks, _, _, width = field_ref.shape
    blocks = blocks - 1

    def order(index, carry):
        at = pl.multiple_of(index * slices, slices)
        ordered[:, pl.ds(at, slices), :] = jnp.swapaxes(volume_ref[pl.ds(at, slices)], 0, 1)
        return carry

    lax.fori_loop(0, rows // slices, order, 0, unroll=4)
    field_ref[blocks] = jnp.zeros((slices, columns, width), jnp.float32)

    def turn(z, carry):
        for block in range(blocks):
            field_ref[block, z] = ordered[z, block * width:(block + 1) * width, :].T.astype(jnp.float32)
        return carry

    lax.fori_loop(0, slices, turn, 0)
    for edge_ref, x in ((low_ref, 0), (high_ref, columns - 1)):
        for block in range(blocks):
            edge_ref[:, block * width:(block + 1) * width] = field_ref[block, :, x, :].astype(edge_ref.dtype)


def make_table(total_z, active_ref, light_ref, gain_ref, bias_ref, table_ref):
    def spread(value):
        return jnp.full(table_ref.shape[1:], value, jnp.float32)

    values = [jnp.broadcast_to(active_ref[...].astype(jnp.float32) * (-2.0 / total_z), table_ref.shape[1:])]
    values += [spread(0.5 * gain_ref[k]) for k in range(3)] + [spread(gain_ref[3] * (1.0 / LN2))]
    values += [spread(0.5 * bias_ref[k]) for k in range(3)] + [spread(bias_ref[3] * (1.0 / LN2))]
    for v in range(light_ref.shape[0]):
        parts = [spread(light_ref[v, k]) for k in range(3)]
        square = jnp.maximum(parts[0] * parts[0] + parts[1] * parts[1] + parts[2] * parts[2], 1e-30)
        unit = (0.35 * LN2) * lax.rsqrt(square)
        values += [part * unit for part in parts] + [4.0 / square]
    for index, value in enumerate(values):
        table_ref[index] = value


def matter_kernel(shift, field_ref, table_ref, after_ref, thick_ref, tints_ref, slope_ref):
    slices, columns, width = thick_ref.shape
    group = table_ref.shape[1]
    scale = table_ref[0]
    gain = [table_ref[1 + k] for k in range(4)]
    bias = [table_ref[5 + k] for k in range(4)]
    lane = lax.broadcasted_iota(jnp.int32, (group, width), 1)
    start = lane == 0
    end = lane == width - 1
    deep = 2
    places = [(part, at * group) for part in range(deep) for at in range(columns // group)]
    blocks = field_ref.shape[0] - 1
    block = lax.rem(lax.axis_index("depth") + shift, blocks)
    before = jnp.where(block == 0, blocks, block - 1)
    behind = block + 1

    def work(step, carry):
        z = step * deep
        heres = [field_ref[block, z + part, at:at + group, :] for part, at in places]
        priors = [field_ref[before, z + part, at:at + group, :] for part, at in places]
        laters = [field_ref[behind, z + part, at:at + group, :] for part, at in places]
        done = []
        for here, prior, later in zip(heres, priors, laters):
            w = lax.exp2(gain[3] * here + bias[3])
            thick = scale * jnp.where(w < 0.001, w * (1.0 / LN2 - (0.5 / LN2) * w), lax.log2(1.0 + w))
            tints = [1.0 + jnp.tanh(gain[k] * here + bias[k]) for k in range(3)]
            prior = pltpu.roll(jnp.where(end, prior, here), 1, 1)
            later = pltpu.roll(jnp.where(start, later, here), width - 1, 1)
            done.append((thick, tints, later - prior))
        for (part, at), (thick, tints, slope) in zip(places, done):
            thick_ref[z + part, at:at + group, :] = thick
            for k in range(3):
                tints_ref[k, z + part, at:at + group, :] = tints[k]
            slope_ref[z + part, at:at + group, :] = slope
        return carry

    lax.fori_loop(0, slices // deep, work, 0)


def first_matter_kernel(shift, total_z, active_ref, light_ref, gain_ref, bias_ref, field_ref, table_ref, *refs):
    make_table(total_z, active_ref, light_ref, gain_ref, bias_ref, table_ref)
    matter_kernel(shift, field_ref, table_ref, None, *refs)


def print_kernel(shift, part, views, field_ref, table_ref, left_ref, right_ref, after_ref, thick_ref, tints_ref, slope_ref,
                 *refs):
    blocks, slices, columns, width = field_ref.shape
    group = table_ref.shape[1]
    quad = columns // (2 * slices)
    count = columns // group
    block = lax.rem(lax.axis_index("depth") + shift, blocks - 1)
    slants = [[table_ref[9 + 4 * v + k] for k in range(3)] for v in range(views)]
    offsets = [table_ref[12 + 4 * v] for v in range(views)]
    line = lax.broadcasted_iota(jnp.int32, (group, width), 0)
    outs, sums = refs[:-4 * views], refs[-4 * views:]
    used = {"all": (0, 2 * columns), "own": (0, columns), "over": (columns, columns)}[part]
    for total in sums:
        total[pl.ds(*used), :] = jnp.zeros((used[1], width), jnp.float32)
    along = pl.ds(pl.multiple_of(block * width, width), width)
    tile = lax.axis_index("tile")
    left = left_ref[:, along].astype(jnp.float32) * jnp.where(tile > 0, 1.0, 0.0)
    right = right_ref[:, along].astype(jnp.float32) * jnp.where(tile + 1 < lax.axis_size("tile"), 1.0, 0.0)

    def wanted(v, j, z):
        first = j * group + z * (v + 1) * quad
        return first < columns if part == "own" else first + group > columns

    def work(j):
        base = j * group if isinstance(j, int) else pl.multiple_of(j * group, group)
        here_rows = pl.ds(base, group)
        for z in range(slices):
            chosen = [v for v in range(views) if part == "all" or wanted(v, j, z)]
            if not chosen:
                continue
            if isinstance(j, int) and j == 0:
                less = jnp.where(line == 0, left[z:z + 1, :], pltpu.roll(field_ref[block, z, here_rows, :], 1, 0))
            else:
                less = field_ref[block, z, pl.ds(base - 1, group), :]
            if isinstance(j, int) and j == count - 1:
                more = jnp.where(line == group - 1, right[z:z + 1, :],
                                 pltpu.roll(field_ref[block, z, here_rows, :], group - 1, 0))
            else:
                more = field_ref[block, z, pl.ds(base + 1, group), :]
            dx = more - less
            dy = slope_ref[z, here_rows, :]
            if z == 0:
                dz = field_ref[block, z + 1, here_rows, :]
            elif z == slices - 1:
                dz = -field_ref[block, z - 1, here_rows, :]
            else:
                dz = field_ref[block, z + 1, here_rows, :] - field_ref[block, z - 1, here_rows, :]
            steep = dx * dx + dy * dy + dz * dz
            thick = thick_ref[z, here_rows, :]
            tints = [tints_ref[k, z, here_rows, :] for k in range(3)]
            for v in chosen:
                place = pl.ds(base + z * (v + 1) * quad, group)
                lx, ly, lz = slants[v]
                facing = dx * lx + dy * ly + dz * lz
                shade = thick * ((-0.15 * LN2) - jnp.abs(facing) * lax.rsqrt(steep + offsets[v]))
                depth = sums[4 * v + 3][place, :]
                sums[4 * v + 3][place, :] = depth + thick
                shade = shade * lax.exp2(depth)
                for k in range(3):
                    sums[4 * v + k][place, :] = sums[4 * v + k][place, :] + tints[k] * shade

    if part == "all":
        work(count - 1)

        def inner(index, carry):
            work(count - 2 - index)
            return carry

        lax.fori_loop(0, count - 2, inner, 0)
        work(0)
    else:
        for j in range(count - 1, -1, -1):
            work(j)
    if part != "over":
        for v in range(views):
            for k in range(4):
                outs[0][v, k] = sums[4 * v + k][:columns, :]
    if part != "own":
        for v in range(views):
            first, size = over_rows(v, slices, columns)
            for k in range(4):
                rest = sums[4 * v + k][columns:columns + size, :]
                outs[-1][k, first:first + size, :] = encode(-rest if k == 3 else rest)


def over_rows(v, slices, columns):
    quad = columns // (2 * slices)
    ends = [-(-(slices - 1) * (view + 1) * quad // 16) * 16 for view in range(v + 1)]
    return sum(ends[:-1]), ends[-1]


def merged(own_ref, over_ref, v, slices):
    first, count = over_rows(v, slices, own_ref.shape[2])
    through = lax.exp2(own_ref[v, 3, :count, :])
    inside = jnp.where(lax.axis_index("tile") > 0, 1.0, 0.0)
    overs = [decode(over_ref[k, first:first + count, :]) * inside for k in range(4)]
    tops = [own_ref[v, k, :count, :] + through * overs[k] for k in range(3)] + [overs[3] - own_ref[v, 3, :count, :]]
    if count == own_ref.shape[2]:
        return tops
    lows = [own_ref[v, k, count:, :] * (1.0 if k < 3 else -1.0) for k in range(4)]
    return [jnp.concatenate([top, low]) for top, low in zip(tops, lows)]


def merge_kernel(slices, own_ref, over_ref, later_ref, arrived_ref, layer_ref, *passed_refs):
    for v in range(own_ref.shape[0]):
        for k, part in enumerate(merged(own_ref, over_ref, v, slices)):
            layer_ref[v, k] = encode(part)
    for ref in passed_refs:
        ref[...] = later_ref[...]


def final_kernel(views, share, slices, shifts, order_ref, own_ref, over_ref, *refs):
    layer_refs, image_ref = refs[:-1], refs[-1]
    groups = len(shifts) + 1
    owner = lax.axis_index("depth")
    ids = [owner] + [lax.rem(owner + groups - shift, groups) for shift in shifts]
    for v in range(views):
        order = [order_ref[v, r] for r in range(groups)]
        places = [sum(jnp.where(order[r] == one, r, 0) for r in range(groups)) for one in ids]
        layers = [merged(own_ref, over_ref, v, slices)] + [[ref[v, k] if ref.dtype == jnp.float32 else decode(ref[v, k]) for k in range(4)] for ref in layer_refs]
        colours = [0.0] * 3
        total = 0.0
        for g in range(groups):
            front = 0.0
            for h in range(groups):
                if h != g:
                    front = front + layers[h][3] * jnp.where(places[h] < places[g], 1.0, 0.0)
            through = lax.exp2(-front)
            colours = [colours[k] + layers[g][k] * through for k in range(3)]
            total = total + layers[g][3]
        for k, part in enumerate(colours + [1.0 - lax.exp2(-total)]):
            turned = part.T
            for t in range(turned.shape[0] // share):
                block = turned[t * share:(t + 1) * share, :]
                image_ref[t, v, k] = encode(block) if image_ref.dtype == jnp.int16 else block


def place_kernel(blocks_ref, image_ref):
    tiles, views, channels, share, columns = blocks_ref.shape
    for t in range(tiles):
        for v in range(views):
            for k in range(channels):
                block = blocks_ref[t, v, k]
                block = decode(block) if block.dtype == jnp.int16 else block
                image_ref[v, k, :, t * columns:(t + 1) * columns] = block


def turn_volume(volume, blocks):
    rows, slices, columns = volume.shape
    width = rows // blocks
    edge = jax.ShapeDtypeStruct((slices, rows), volume.dtype)
    return pl.pallas_call(
        turn_kernel,
        out_shape=[jax.ShapeDtypeStruct((blocks + 1, slices, columns, width), jnp.float32), edge, edge],
        in_specs=[vmem], out_specs=[vmem] * 3, scratch_shapes=[pltpu.VMEM((slices, rows, columns), volume.dtype)],
        cost_estimate=long_cost,
        compiler_params=turn_params, name="turn_rows")(volume)


def matter_of(field, shift, table=None, smalls=(), after=None):
    blocks, slices, columns, width = field.shape
    shape = (slices, columns, width)
    outs = [jax.ShapeDtypeStruct(shape, jnp.float32), jax.ShapeDtypeStruct((3,) + shape, jnp.float32),
            jax.ShapeDtypeStruct(shape, jnp.float32)]
    if table is not None:
        return pl.pallas_call(
            functools.partial(matter_kernel, shift), out_shape=outs, in_specs=[vmem] * 2 + [far], out_specs=[vmem] * 3,
            cost_estimate=short_cost, compiler_params=params, name="matter")(field, table, after)
    table = jax.ShapeDtypeStruct((9 + 4 * smalls[1].shape[0], 8, width), jnp.float32)
    return pl.pallas_call(
        functools.partial(first_matter_kernel, shift, slices * (blocks - 1)), out_shape=[table] + outs,
        in_specs=[vmem] + [smem] * 3 + [vmem], out_specs=[vmem] * 4,
        cost_estimate=short_cost, compiler_params=params, name="matter")(*smalls, field)


def prints_of(field, matter, table, left, right, after, shift, views, part):
    blocks, slices, columns, width = field.shape
    shape = (views, 4, columns, width)
    over_shape = (4, sum(over_rows(views - 1, slices, columns)), width)
    outs = [jax.ShapeDtypeStruct(shape, jnp.float32)] if part != "over" else []
    outs += [jax.ShapeDtypeStruct(over_shape, jnp.int16)] if part != "own" else []
    return pl.pallas_call(
        functools.partial(print_kernel, shift, part, views), out_shape=outs,
        in_specs=[vmem] * 4 + [far] + [vmem] * 3, out_specs=[vmem] * len(outs),
        scratch_shapes=[pltpu.VMEM((2 * columns, width), jnp.float32)] * (4 * views),
        cost_estimate=short_cost, compiler_params=params, name="prints")(field, table, left, right, after, *matter)


def merge_of(own, over, later, arrived, slices, passing):
    layer = jax.ShapeDtypeStruct(own.shape, jnp.int16)
    passed = [jax.ShapeDtypeStruct(later.shape, later.dtype)] if passing else []
    return pl.pallas_call(
        functools.partial(merge_kernel, slices), out_shape=[layer] + passed,
        in_specs=[vmem] * 2 + [vmem if passing else far, far], out_specs=[vmem] * (1 + len(passed)), cost_estimate=short_cost,
        compiler_params=params, name="merge")(own, over, later, arrived)


def open_kernel(layer_ref, opened_ref):
    for v in range(layer_ref.shape[0]):
        for k in range(layer_ref.shape[1]):
            opened_ref[v, k] = decode(layer_ref[v, k])


def open_of(layer):
    return pl.pallas_call(
        open_kernel, out_shape=jax.ShapeDtypeStruct(layer.shape, jnp.float32), in_specs=[vmem], out_specs=vmem,
        cost_estimate=long_cost, compiler_params=params, name="opened")(layer)


def final_of(depth_order, own, over, layers, shifts, share, slices):
    views, channels, columns, width = own.shape
    kind = jnp.int16 if share % 16 == 0 else jnp.float32
    return pl.pallas_call(
        functools.partial(final_kernel, views, share, slices, shifts),
        out_shape=jax.ShapeDtypeStruct((width // share, views, channels, share, columns), kind),
        in_specs=[smem] + [vmem] * (2 + len(layers)), out_specs=vmem, compiler_params=params,
        name="final")(depth_order, own, over, *layers)


def place_of(blocks):
    tiles, views, channels, share, columns = blocks.shape
    return pl.pallas_call(
        place_kernel, out_shape=jax.ShapeDtypeStruct((views, channels, share, tiles * columns), jnp.float32),
        in_specs=[vmem], out_specs=vmem, compiler_params=params, name="place")(blocks)


def passed_round(x, axis, by):
    devices = lax.axis_size(axis)
    return lax.ppermute(x, axis, [(i, (i + by) % devices) for i in range(devices)])


def local(volume, active, depth_order, light_vector, class_gain, class_bias):
    depth_count = lax.axis_size("depth")
    tile_count = lax.axis_size("tile")
    rows, slices, columns = volume.shape
    share = rows // (depth_count * tile_count)
    field, low, high = turn_volume(volume, depth_count)
    left = passed_round(high, "tile", 1)
    right = passed_round(low, "tile", -1)
    shifts = sorted(range(1, depth_count), key=lambda shift: -min(shift, depth_count - shift)) + [0]
    smalls = (active, light_vector, class_gain, class_bias)
    table, ready, waiting, layers = None, left, [], []
    views = light_vector.shape[0]
    for index, shift in enumerate(shifts):
        last = index + 1 == len(shifts)
        if index == 0:
            table, *matter = matter_of(field, shift, smalls=smalls)
            sources = field, matter, table, left, right
            over, = prints_of(*sources, ready, shift, views, "over")
            own, = prints_of(*sources, over, shift, views, "own")
        else:
            matter = matter_of(field, shift, table=table, after=ready)
            if len(waiting) > 1:
                ready, = merge_of(*waiting.pop(0), matter[0], ready, slices, False)
                layers.append(passed_round(ready, "depth", shifts[len(layers)]))
            own, over = prints_of(field, matter, table, left, right, ready, shift, views, "all")
        ready = own
        if index == 1 or last and waiting:
            ready, *passed = merge_of(*waiting.pop(0), over if last else own, ready, slices, last)
            over = passed[0] if last else over
            layers.append(passed_round(ready, "depth", shifts[len(layers)]))
        waiting.append((own, passed_round(over, "tile", 1)))
    layers = [open_of(layers[0])] + layers[1:]
    blocks = final_of(depth_order, *waiting[0], layers, shifts[:-1], share, slices)
    blocks = lax.all_to_all(blocks, "tile", split_axis=0, concat_axis=0, tiled=True)
    return place_of(blocks)


def solution(mesh):
    placed = (P(None, "depth", "tile"), P("depth", "tile"), P(), P(), P(), P())
    return jax.shard_map(
        local,
        mesh=mesh,
        in_specs=placed,
        out_specs=P(None, None, ("depth", "tile"), None),
        check_vma=False,
    )
```

time: 57.6 us -> 56.8 us (0.986)
  waiting for transfers between devices: 11.3 us -> 9.56 us
  starting transfers between devices: 12.3 us -> 12.9 us
    ppermute x9, waiting for transfers between devices: 11.3 us -> 9.56 us  [passed_round(): lax.ppermute(x, axis, [(i, (i + by) % devices) for i in range(devices)])]
    ppermute x9, starting transfers between devices: 12.3 us -> 12.9 us  [passed_round(): lax.ppermute(x, axis, [(i, (i + by) % devices) for i in range(devices)])]
    pallas_call x10 -> x14, Pallas kernels: 19.5 us -> 19.6 us  [the longest x5 10.3 us: prints_of(): pl.pallas_call(functools.partial(print_kernel, shift, part, views), out_s...]
  transfers between devices with their start and end apart: 9 -> 9, of which waited for: 4 -> 4; matrix products, arithmetic and copies ran while one was open for 0% -> 0% of each run, Pallas kernels for 26% -> 29%
where the time goes in v5:
time: 56.8 us; the launch traced here: 56.6 us
  Pallas kernels  21.8 us (38%)
  starting transfers between devices  12.9 us (23%)
  blocking collectives  9.87 us (17%)
  waiting for transfers between devices  9.56 us (17%)
  local copies, waits for them, and re-layouts  1.65 us (3%)
  between operations  0.8 us (1%)
    ppermute x9, starting transfers between devices, passed_round(): lax.ppermute(x, axis, [(i, (i + by) % devices) for i in range(devices)])  12.9 us
    pallas_call x5, Pallas kernels, prints_of(): pl.pallas_call(functools.partial(print_kernel, shift, part, views), out_s...  10.3 us
    all_to_all x1, blocking collectives, local(): lax.all_to_all(blocks, 'tile', split_axis=0, concat_axis=0, tiled=True)  9.87 us
    ppermute x9, waiting for transfers between devices, passed_round(): lax.ppermute(x, axis, [(i, (i + by) % devices) for i in range(devices)])  9.56 us
    pallas_call x3, Pallas kernels, matter_of(): pl.pallas_call(functools.partial(matter_kernel, shift), out_shape=outs, i...  4.09 us
    pallas_call x1, Pallas kernels, turn_volume(): pl.pallas_call(turn_kernel, out_shape=[jax.ShapeDtypeStruct((blocks + 1,...  2.21 us
    pallas_call x1, Pallas kernels, matter_of(): pl.pallas_call(functools.partial(first_matter_kernel, shift, slices * (bl...  1.99 us
    unnamed x10, local copies, waits for them, and re-layouts  1.65 us
  transfers between devices with their start and end apart: 9, of which 4 were waited for; matrix products, arithmetic and copies ran while one was open for 0% of the time, Pallas kernels for 29%

profile of v5, /device:TPU:0, one launch (start us, length us, event | category | flops | bytes accessed | tf_op | source)
XLA Modules:
  0.0 56.6 jit_solution(16621079909478222974)
XLA Ops:
  0.0 1.6 %copy-done.4 = bf16[512,16,128]{2,1,0:T(8,128)(2,1)S(1)} copy-done((bf16[512,16,128]{2,1,0:T(8,128)(2,1)S(1)}, bf16[512,16,128]{2,1,0:T(8,128)(2,1)}, u32[]{:S(2)}) %copy-start.4) | copy-done | bytes 2097176
  1.6 2.2 %turn_rows.1 = (f32[5,16,128,128]{3,2,1,0:T(8,128)S(1)}, bf16[16,512]{1,0:T(8,128)(2,1)S(1)}, bf16[16,512]{1,0:T(8,128)(2,1)S(1)}) custom-call(bf16[512,16,128]{2,1,0:T(8,128)(2,1)S(1)} %copy-done.4), custom_call_target="tpu_custom_call" | custom-call | flops 10000000000 | bytes 100000000 | tf_op jit(solution)/shard_map/turn_rows/pallas_call | solution.py:268
  3.9 0.5 collective-permute-start
  4.4 2.9 %collective-permute-start.1 = (bf16[16,512]{1,0:T(8,128)(2,1)S(1)}, bf16[16,512]{1,0:T(8,128)(2,1)S(1)}, u32[]{:S(2)}, u32[]{:S(2)}) collective-permute-start(bf16[16,512]{1,0:T(8,128)(2,1)S(1)} %get-tuple-element.32), channel_id=1, source_target_pairs={{0,7},{1,0},{2,1},{3,2},{4,3},{5,4},{6,5},{7,6},{8,15},{9,8},{10,9... | collective-permute-start | bytes 49160 | tf_op jit(solution)/shard_map/ppermute | solution.py:345
  8.0 2.0 %matter.4 = (f32[17,8,128]{2,1,0:T(8,128)S(1)}, f32[16,128,128]{2,1,0:T(8,128)S(1)}, f32[3,16,128,128]{3,2,1,0:T(8,128)S(1)}, f32[16,128,128]{2,1,0:T(8,128)S(1)}) custom-call(s32[1,1]{1,0:T(1,128)S(6)} %copy.7.active_ref, f32[2,3]{1,0:T(2,128)S(1)} %copy-done.1, f32[4]{0:T(128)S(1)} %copy-done.2, f32[4]{0:T(128)S(1)} %copy-done.3, ...), custom_call_target="tpu_custom_call" | custom-call | flops 100000000 | bytes 1000000 | tf_op jit(solution)/shard_map/matter/pallas_call | solution.py:286
  10.0 0.9 %prints.5.after_ref = s16[4,192,128]{2,1,0:T(8,128)(2,1)S(1)} custom-call(f32[5,16,128,128]{3,2,1,0:T(8,128)S(1)} %get-tuple-element.29.field_ref, f32[17,8,128]{2,1,0:T(8,128)S(1)} %get-tuple-element.30.table_ref, bf16[16,512]{1,0:T(8,128)(2,1)S(1)} %collective-permute-done.left_ref.after_ref, bf16[16,512]{1,0:T(8,128)(2,1)S(1)} %collective-permute-done.1.right_ref, ...), custom_call_target="tpu_custom_call" | custom-call | flops 100000000 | bytes 1000000 | tf_op jit(solution)/shard_map/prints/pallas_call | solution.py:298
  11.1 1.6 %prints.6.after_ref.own_ref = f32[2,4,128,128]{3,2,1,0:T(8,128)S(1)} custom-call(f32[5,16,128,128]{3,2,1,0:T(8,128)S(1)} %get-tuple-element.29.field_ref, f32[17,8,128]{2,1,0:T(8,128)S(1)} %get-tuple-element.30.table_ref, bf16[16,512]{1,0:T(8,128)(2,1)S(1)} %collective-permute-done.left_ref.after_ref, bf16[16,512]{1,0:T(8,128)(2,1)S(1)} %collective-permute-done.1.right_ref, ...), custom_call_target="tpu_custom_call" | custom-call | flops 100000000 | bytes 1000000 | tf_op jit(solution)/shard_map/prints/pallas_call | solution.py:298
  12.7 1.4 %matter.5 = (f32[16,128,128]{2,1,0:T(8,128)S(1)}, f32[3,16,128,128]{3,2,1,0:T(8,128)S(1)}, f32[16,128,128]{2,1,0:T(8,128)S(1)}) custom-call(f32[5,16,128,128]{3,2,1,0:T(8,128)S(1)} %get-tuple-element.29.field_ref, f32[17,8,128]{2,1,0:T(8,128)S(1)} %get-tuple-element.30.table_ref, f32[2,4,128,128]{3,2,1,0:T(8,128)S(1)} %prints.6.after_ref.own_ref), custom_call_target="tpu_custom_call" | custom-call | flops 100000000 | bytes 1000000 | tf_op jit(solution)/shard_map/matter/pallas_call | solution.py:282
  14.0 2.6 %prints.7 = (f32[2,4,128,128]{3,2,1,0:T(8,128)S(1)}, s16[4,192,128]{2,1,0:T(8,128)(2,1)S(1)}) custom-call(f32[5,16,128,128]{3,2,1,0:T(8,128)S(1)} %get-tuple-element.29.field_ref, f32[17,8,128]{2,1,0:T(8,128)S(1)} %get-tuple-element.30.table_ref, bf16[16,512]{1,0:T(8,128)(2,1)S(1)} %collective-permute-done.left_ref.after_ref, ...), custom_call_target="tpu_custom_call" | custom-call | flops 100000000 | bytes 1000000 | tf_op jit(solution)/shard_map/prints/pallas_call | solution.py:298
  17.3 3.3 %collective-permute-start.6 = (s16[2,4,128,128]{3,2,1,0:T(8,128)(2,1)S(1)}, s16[2,4,128,128]{3,2,1,0:T(8,128)(2,1)S(1)}, u32[]{:S(2)}, u32[]{:S(2)}) collective-permute-start(s16[2,4,128,128]{3,2,1,0:T(8,128)(2,1)S(1)} %merge.3.after_ref), channel_id=1, source_target_pairs={{0,16},{8,24},{16,0},{24,8},{1,17},{9,25},{17,1},{25,9},{2,18},{10... | collective-permute-start | bytes 786440 | tf_op jit(solution)/shard_map/ppermute | solution.py:345
  20.6 1.4 %matter.6 = (f32[16,128,128]{2,1,0:T(8,128)S(1)}, f32[3,16,128,128]{3,2,1,0:T(8,128)S(1)}, f32[16,128,128]{2,1,0:T(8,128)S(1)}) custom-call(f32[5,16,128,128]{3,2,1,0:T(8,128)S(1)} %get-tuple-element.29.field_ref, f32[17,8,128]{2,1,0:T(8,128)S(1)} %get-tuple-element.30.table_ref, s16[2,4,128,128]{3,2,1,0:T(8,128)(2,1)S(1)} %merge.3.after_ref), custom_call_target="tpu_custom_call" | custom-call | flops 100000000 | bytes 1000000 | tf_op jit(solution)/shard_map/matter/pallas_call | solution.py:282
  22.0 2.6 %prints.8 = (f32[2,4,128,128]{3,2,1,0:T(8,128)S(1)}, s16[4,192,128]{2,1,0:T(8,128)(2,1)S(1)}) custom-call(f32[5,16,128,128]{3,2,1,0:T(8,128)S(1)} %get-tuple-element.29.field_ref, f32[17,8,128]{2,1,0:T(8,128)S(1)} %get-tuple-element.30.table_ref, bf16[16,512]{1,0:T(8,128)(2,1)S(1)} %collective-permute-done.left_ref.after_ref, ...), custom_call_target="tpu_custom_call" | custom-call | flops 100000000 | bytes 1000000 | tf_op jit(solution)/shard_map/prints/pallas_call | solution.py:298
  24.6 1.6 %collective-permute-start.4 = (s16[4,192,128]{2,1,0:T(8,128)(2,1)S(1)}, s16[4,192,128]{2,1,0:T(8,128)(2,1)S(1)}, u32[]{:S(2)}, u32[]{:S(2)}) collective-permute-start(s16[4,192,128]{2,1,0:T(8,128)(2,1)S(1)} %get-tuple-element.49), channel_id=1, source_target_pairs={{0,1},{1,2},{2,3},{3,4},{4,5},{5,6},{6,7},{7,0},{8,9},{9,10},{10,1... | collective-permute-start | bytes 589832 | tf_op jit(solution)/shard_map/ppermute | solution.py:345
  26.2 1.4 %matter.7 = (f32[16,128,128]{2,1,0:T(8,128)S(1)}, f32[3,16,128,128]{3,2,1,0:T(8,128)S(1)}, f32[16,128,128]{2,1,0:T(8,128)S(1)}) custom-call(f32[5,16,128,128]{3,2,1,0:T(8,128)S(1)} %get-tuple-element.29.field_ref, f32[17,8,128]{2,1,0:T(8,128)S(1)} %get-tuple-element.30.table_ref, f32[2,4,128,128]{3,2,1,0:T(8,128)S(1)} %get-tuple-element.44.after_ref.arrived_ref.own_ref), custom_call_target="tpu_custom_call" | custom-call | flops 100000000 | bytes 1000000 | tf_op jit(solution)/shard_map/matter/pallas_call | solution.py:282
  27.8 1.6 %collective-permute-start.7 = (s16[2,4,128,128]{3,2,1,0:T(8,128)(2,1)S(1)}, s16[2,4,128,128]{3,2,1,0:T(8,128)(2,1)S(1)}, u32[]{:S(2)}, u32[]{:S(2)}) collective-permute-start(s16[2,4,128,128]{3,2,1,0:T(8,128)(2,1)S(1)} %merge.4.after_ref), channel_id=1, source_target_pairs={{0,8},{8,16},{16,24},{24,0},{1,9},{9,17},{17,25},{25,1},{2,10},{10... | collective-permute-start | bytes 786440 | tf_op jit(solution)/shard_map/ppermute | solution.py:345
  29.4 2.6 %prints.9 = (f32[2,4,128,128]{3,2,1,0:T(8,128)S(1)}, s16[4,192,128]{2,1,0:T(8,128)(2,1)S(1)}) custom-call(f32[5,16,128,128]{3,2,1,0:T(8,128)S(1)} %get-tuple-element.29.field_ref, f32[17,8,128]{2,1,0:T(8,128)S(1)} %get-tuple-element.30.table_ref, bf16[16,512]{1,0:T(8,128)(2,1)S(1)} %collective-permute-done.left_ref.after_ref, ...), custom_call_target="tpu_custom_call" | custom-call | flops 100000000 | bytes 1000000 | tf_op jit(solution)/shard_map/prints/pallas_call | solution.py:298
  32.4 2.3 %collective-permute-start.8 = (s16[2,4,128,128]{3,2,1,0:T(8,128)(2,1)S(1)}, s16[2,4,128,128]{3,2,1,0:T(8,128)(2,1)S(1)}, u32[]{:S(2)}, u32[]{:S(2)}) collective-permute-start(s16[2,4,128,128]{3,2,1,0:T(8,128)(2,1)S(1)} %get-tuple-element.52), channel_id=1, source_target_pairs={{0,24},{8,0},{16,8},{24,16},{1,25},{9,1},{17,9},{25,17},{2,26},{10... | collective-permute-start | bytes 786440 | tf_op jit(solution)/shard_map/ppermute | solution.py:345
  34.7 0.4 collective-permute-start.5
  35.2 3.7 %collective-permute-done.7.refs_1_ = s16[2,4,128,128]{3,2,1,0:T(8,128)(2,1)S(1)} collective-permute-done((s16[2,4,128,128]{3,2,1,0:T(8,128)(2,1)S(1)}, s16[2,4,128,128]{3,2,1,0:T(8,128)(2,1)S(1)}, u32[]{:S(2)}, u32[]{:S(2)}) %collective-permute-start.7) | collective-permute-done | bytes 262176 | tf_op jit(solution)/shard_map/ppermute | solution.py:345
  39.0 1.7 %collective-permute-done.5.over_ref = s16[4,192,128]{2,1,0:T(8,128)(2,1)S(1)} collective-permute-done((s16[4,192,128]{2,1,0:T(8,128)(2,1)S(1)}, s16[4,192,128]{2,1,0:T(8,128)(2,1)S(1)}, u32[]{:S(2)}, u32[]{:S(2)}) %collective-permute-start.5) | collective-permute-done | bytes 196640 | tf_op jit(solution)/shard_map/ppermute | solution.py:345
  40.7 3.8 %collective-permute-done.8.refs_2_ = s16[2,4,128,128]{3,2,1,0:T(8,128)(2,1)S(1)} collective-permute-done((s16[2,4,128,128]{3,2,1,0:T(8,128)(2,1)S(1)}, s16[2,4,128,128]{3,2,1,0:T(8,128)(2,1)S(1)}, u32[]{:S(2)}, u32[]{:S(2)}) %collective-permute-start.8) | collective-permute-done | bytes 262176 | tf_op jit(solution)/shard_map/ppermute | solution.py:345
  44.5 1.3 %final.1 = s16[8,2,4,16,128]{4,3,2,1,0:T(8,128)(2,1)S(1)} custom-call(s32[2,4]{1,0:T(2,128)S(1)} %copy-done, f32[2,4,128,128]{3,2,1,0:T(8,128)S(1)} %get-tuple-element.48.arrived_ref.own_ref, s16[4,192,128]{2,1,0:T(8,128)(2,1)S(1)} %collective-permute-done.5.over_ref, f32[2,4,128,128]{3,2,1,0:T(8,128)S(1)} %opened.1.refs_0_, ...), custom_call_target="tpu_custom_call" | custom-call | tf_op jit(solution)/shard_map/final/pallas_call | solution.py:329
  45.8 9.9 %all_to_all.5.blocks_ref = s16[8,2,4,16,128]{4,3,2,1,0:T(8,128)(2,1)S(1)} all-to-all(s16[8,2,4,16,128]{4,3,2,1,0:T(8,128)(2,1)S(1)} %final.1), channel_id=1, replica_groups=mesh['depth'=4,'tile'=8] {'tile'}, dimensions={0} | all-to-all | bytes 524288 | tf_op jit(solution)/shard_map/all_to_all | solution.py:381
  55.7 0.9 %place.1 = f32[2,4,16,1024]{3,2,1,0:T(8,128)} custom-call(s16[8,2,4,16,128]{4,3,2,1,0:T(8,128)(2,1)S(1)} %all_to_all.5.blocks_ref), custom_call_target="tpu_custom_call" | custom-call | tf_op jit(solution)/shard_map/place/pallas_call | solution.py:338
  (21 shorter events, 1.5 us)
Async XLA Ops:
  0.0 8.0 %copy-start.2 = (f32[4]{0:T(128)S(1)}, f32[4]{0:T(128)}, u32[]{:S(2)}) copy-start(f32[4]{0:T(128)} %gain_ref.1) | copy-start | bytes 52
  0.0 8.0 %copy-start.3 = (f32[4]{0:T(128)S(1)}, f32[4]{0:T(128)}, u32[]{:S(2)}) copy-start(f32[4]{0:T(128)} %bias_ref.1) | copy-start | bytes 52
  0.0 8.0 %copy-start.1 = (f32[2,3]{1,0:T(2,128)S(1)}, f32[2,3]{1,0:T(2,128)}, u32[]{:S(2)}) copy-start(f32[2,3]{1,0:T(2,128)} %light_ref.1) | copy-start | bytes 76
  0.0 1.6 %copy-start.4 = (bf16[512,16,128]{2,1,0:T(8,128)(2,1)S(1)}, bf16[512,16,128]{2,1,0:T(8,128)(2,1)}, u32[]{:S(2)}) copy-start(bf16[512,16,128]{2,1,0:T(8,128)(2,1)} %volume_ref.1) | copy-start | bytes 6291460
  3.9 6.1 %collective-permute-start = (bf16[16,512]{1,0:T(8,128)(2,1)S(1)}, bf16[16,512]{1,0:T(8,128)(2,1)S(1)}, u32[]{:S(2)}, u32[]{:S(2)}) collective-permute-start(bf16[16,512]{1,0:T(8,128)(2,1)S(1)} %get-tuple-element.31), channel_id=1, source_target_pairs={{0,1},{1,2},{2,3},{3,4},{4,5},{5,6},{6,7},{7,0},{8,9},{9,10},{10,1... | collective-permute-start | bytes 49160 | tf_op jit(solution)/shard_map/ppermute | solution.py:345
  4.4 5.6 %collective-permute-start.1 = (bf16[16,512]{1,0:T(8,128)(2,1)S(1)}, bf16[16,512]{1,0:T(8,128)(2,1)S(1)}, u32[]{:S(2)}, u32[]{:S(2)}) collective-permute-start(bf16[16,512]{1,0:T(8,128)(2,1)S(1)} %get-tuple-element.32), channel_id=1, source_target_pairs={{0,7},{1,0},{2,1},{3,2},{4,3},{5,4},{6,5},{7,6},{8,15},{9,8},{10,9... | collective-permute-start | bytes 49160 | tf_op jit(solution)/shard_map/ppermute | solution.py:345
  10.9 6.0 %collective-permute-start.3 = (s16[4,192,128]{2,1,0:T(8,128)(2,1)S(1)}, s16[4,192,128]{2,1,0:T(8,128)(2,1)S(1)}, u32[]{:S(2)}, u32[]{:S(2)}) collective-permute-start(s16[4,192,128]{2,1,0:T(8,128)(2,1)S(1)} %prints.5.after_ref), channel_id=1, source_target_pairs={{0,1},{1,2},{2,3},{3,4},{4,5},{5,6},{6,7},{7,0},{8,9},{9,10},{10,1... | collective-permute-start | bytes 589832 | tf_op jit(solution)/shard_map/ppermute | solution.py:345
  17.3 17.9 %collective-permute-start.6 = (s16[2,4,128,128]{3,2,1,0:T(8,128)(2,1)S(1)}, s16[2,4,128,128]{3,2,1,0:T(8,128)(2,1)S(1)}, u32[]{:S(2)}, u32[]{:S(2)}) collective-permute-start(s16[2,4,128,128]{3,2,1,0:T(8,128)(2,1)S(1)} %merge.3.after_ref), channel_id=1, source_target_pairs={{0,16},{8,24},{16,0},{24,8},{1,17},{9,25},{17,1},{25,9},{2,18},{10... | collective-permute-start | bytes 786440 | tf_op jit(solution)/shard_map/ppermute | solution.py:345
  20.6 6.9 %collective-permute-start.2 = (s16[4,192,128]{2,1,0:T(8,128)(2,1)S(1)}, s16[4,192,128]{2,1,0:T(8,128)(2,1)S(1)}, u32[]{:S(2)}, u32[]{:S(2)}) collective-permute-start(s16[4,192,128]{2,1,0:T(8,128)(2,1)S(1)} %get-tuple-element.40), channel_id=1, source_target_pairs={{0,1},{1,2},{2,3},{3,4},{4,5},{5,6},{6,7},{7,0},{8,9},{9,10},{10,1... | collective-permute-start | bytes 589832 | tf_op jit(solution)/shard_map/ppermute | solution.py:345
  24.6 7.5 %collective-permute-start.4 = (s16[4,192,128]{2,1,0:T(8,128)(2,1)S(1)}, s16[4,192,128]{2,1,0:T(8,128)(2,1)S(1)}, u32[]{:S(2)}, u32[]{:S(2)}) collective-permute-start(s16[4,192,128]{2,1,0:T(8,128)(2,1)S(1)} %get-tuple-element.49), channel_id=1, source_target_pairs={{0,1},{1,2},{2,3},{3,4},{4,5},{5,6},{6,7},{7,0},{8,9},{9,10},{10,1... | collective-permute-start | bytes 589832 | tf_op jit(solution)/shard_map/ppermute | solution.py:345
  27.8 11.1 %collective-permute-start.7 = (s16[2,4,128,128]{3,2,1,0:T(8,128)(2,1)S(1)}, s16[2,4,128,128]{3,2,1,0:T(8,128)(2,1)S(1)}, u32[]{:S(2)}, u32[]{:S(2)}) collective-permute-start(s16[2,4,128,128]{3,2,1,0:T(8,128)(2,1)S(1)} %merge.4.after_ref), channel_id=1, source_target_pairs={{0,8},{8,16},{16,24},{24,0},{1,9},{9,17},{17,25},{25,1},{2,10},{10... | collective-permute-start | bytes 786440 | tf_op jit(solution)/shard_map/ppermute | solution.py:345
  32.4 12.1 %collective-permute-start.8 = (s16[2,4,128,128]{3,2,1,0:T(8,128)(2,1)S(1)}, s16[2,4,128,128]{3,2,1,0:T(8,128)(2,1)S(1)}, u32[]{:S(2)}, u32[]{:S(2)}) collective-permute-start(s16[2,4,128,128]{3,2,1,0:T(8,128)(2,1)S(1)} %get-tuple-element.52), channel_id=1, source_target_pairs={{0,24},{8,0},{16,8},{24,16},{1,25},{9,1},{17,9},{25,17},{2,26},{10... | collective-permute-start | bytes 786440 | tf_op jit(solution)/shard_map/ppermute | solution.py:345
  34.7 9.8 %copy-start = (s32[2,4]{1,0:T(2,128)S(1)}, s32[2,4]{1,0:T(2,128)}, u32[]{:S(2)}) copy-start(s32[2,4]{1,0:T(2,128)} %order_ref.1) | copy-start | bytes 100
  34.7 6.0 %collective-permute-start.5 = (s16[4,192,128]{2,1,0:T(8,128)(2,1)S(1)}, s16[4,192,128]{2,1,0:T(8,128)(2,1)S(1)}, u32[]{:S(2)}, u32[]{:S(2)}) collective-permute-start(s16[4,192,128]{2,1,0:T(8,128)(2,1)S(1)} %get-tuple-element.51), channel_id=1, source_target_pairs={{0,1},{1,2},{2,3},{3,4},{4,5},{5,6},{6,7},{7,0},{8,9},{9,10},{10,1... | collective-permute-start | bytes 589832 | tf_op jit(solution)/shard_map/ppermute | solution.py:345

commit v6 on v5

--- a/solution.py
+++ b/solution.py
@@ -125,7 +125,7 @@
     offsets = [table_ref[12 + 4 * v] for v in range(views)]
     line = lax.broadcasted_iota(jnp.int32, (group, width), 0)
     outs, sums = refs[:-4 * views], refs[-4 * views:]
-    used = {"all": (0, 2 * columns), "own": (0, columns), "over": (columns, columns)}[part]
+    used = {"all": (0, 2 * columns), "own": (0, columns + group), "over": (columns - group, columns + group)}[part]
     for total in sums:
         total[pl.ds(*used), :] = jnp.zeros((used[1], width), jnp.float32)
     along = pl.ds(pl.multiple_of(block * width, width), width)
@@ -225,26 +225,42 @@
         ref[...] = later_ref[...]
 
 
-def final_kernel(views, share, slices, shifts, order_ref, own_ref, over_ref, *refs):
-    layer_refs, image_ref = refs[:-1], refs[-1]
+def early_kernel(slices, shifts, order_ref, own_ref, over_ref, *refs):
+    layer_refs, mix_ref = refs[:-1], refs[-1]
     groups = len(shifts) + 1
     owner = lax.axis_index("depth")
     ids = [owner] + [lax.rem(owner + groups - shift, groups) for shift in shifts]
-    for v in range(views):
+    for v in range(own_ref.shape[0]):
         order = [order_ref[v, r] for r in range(groups)]
         places = [sum(jnp.where(order[r] == one, r, 0) for r in range(groups)) for one in ids]
-        layers = [merged(own_ref, over_ref, v, slices)] + [[ref[v, k] if ref.dtype == jnp.float32 else decode(ref[v, k]) for k in range(4)] for ref in layer_refs]
-        colours = [0.0] * 3
+        layers = [merged(own_ref, over_ref, v, slices)]
+        layers += [[ref[v, k] if ref.dtype == jnp.float32 else decode(ref[v, k]) for k in range(4)] for ref in layer_refs]
+        ahead = [0.0] * 3
+        after = [0.0] * 3
+        depth_ahead = 0.0
         total = 0.0
-        for g in range(groups):
+        for g in range(groups - 1):
             front = 0.0
-            for h in range(groups):
+            for h in range(groups - 1):
                 if h != g:
                     front = front + layers[h][3] * jnp.where(places[h] < places[g], 1.0, 0.0)
+            first = jnp.where(places[g] < places[-1], 1.0, 0.0)
             through = lax.exp2(-front)
-            colours = [colours[k] + layers[g][k] * through for k in range(3)]
+            near, far_off = through * first, through * (1.0 - first)
+            ahead = [ahead[k] + layers[g][k] * near for k in range(3)]
+            after = [after[k] + layers[g][k] * far_off for k in range(3)]
+            depth_ahead = depth_ahead + layers[g][3] * first
             total = total + layers[g][3]
-        for k, part in enumerate(colours + [1.0 - lax.exp2(-total)]):
+        for k, part in enumerate(ahead + after + [lax.exp2(-depth_ahead), total]):
+            mix_ref[v, k] = part
+
+
+def final_kernel(share, mix_ref, layer_ref, image_ref):
+    for v in range(mix_ref.shape[0]):
+        depth = decode(layer_ref[v, 3])
+        through = lax.exp2(-depth)
+        colours = [mix_ref[v, k] + mix_ref[v, 6] * decode(layer_ref[v, k]) + through * mix_ref[v, 3 + k] for k in range(3)]
+        for k, part in enumerate(colours + [1.0 - lax.exp2(-(mix_ref[v, 7] + depth))]):
             turned = part.T
             for t in range(turned.shape[0] // share):
                 block = turned[t * share:(t + 1) * share, :]
@@ -323,14 +339,21 @@
         cost_estimate=long_cost, compiler_params=params, name="opened")(layer)
 
 
-def final_of(depth_order, own, over, layers, shifts, share, slices):
+def early_of(depth_order, own, over, layers, shifts, slices):
     views, channels, columns, width = own.shape
+    return pl.pallas_call(
+        functools.partial(early_kernel, slices, shifts), out_shape=jax.ShapeDtypeStruct((views, 8, columns, width), jnp.float32),
+        in_specs=[smem] + [vmem] * (2 + len(layers)), out_specs=vmem, cost_estimate=short_cost,
+        compiler_params=params, name="early")(depth_order, own, over, *layers)
+
+
+def final_of(mix, layer, share):
+    views, channels, columns, width = layer.shape
     kind = jnp.int16 if share % 16 == 0 else jnp.float32
     return pl.pallas_call(
-        functools.partial(final_kernel, views, share, slices, shifts),
+        functools.partial(final_kernel, share),
         out_shape=jax.ShapeDtypeStruct((width // share, views, channels, share, columns), kind),
-        in_specs=[smem] + [vmem] * (2 + len(layers)), out_specs=vmem, compiler_params=params,
-        name="final")(depth_order, own, over, *layers)
+        in_specs=[vmem] * 2, out_specs=vmem, compiler_params=params, name="final")(mix, layer)
 
 
 def place_of(blocks):
@@ -376,8 +399,8 @@
             over = passed[0] if last else over
             layers.append(passed_round(ready, "depth", shifts[len(layers)]))
         waiting.append((own, passed_round(over, "tile", 1)))
-    layers = [open_of(layers[0])] + layers[1:]
-    blocks = final_of(depth_order, *waiting[0], layers, shifts[:-1], share, slices)
+    mix = early_of(depth_order, *waiting[0], [open_of(layers[0])] + layers[1:-1], shifts[:-1], slices)
+    blocks = final_of(mix, layers[-1], share)
     blocks = lax.all_to_all(blocks, "tile", split_axis=0, concat_axis=0, tiled=True)
     return place_of(blocks)
 

time: 56.8 us -> 55.8 us (0.982)
  waiting for transfers between devices: 9.56 us -> 8.22 us
    ppermute x9, waiting for transfers between devices: 9.56 us -> 8.22 us  [passed_round(): lax.ppermute(x, axis, [(i, (i + by) % devices) for i in range(devices)])]
    pallas_call x1 -> x2, Pallas kernels: 1.31 us -> 1.42 us  [the longest x1 1.07 us: early_of(): pl.pallas_call(functools.partial(early_kernel, slices, shifts), out_shape...]
  transfers between devices with their start and end apart: 9 -> 9, of which waited for: 4 -> 3; matrix products, arithmetic and copies ran while one was open for 0% -> 0% of each run, Pallas kernels for 29% -> 31%
where the time goes in v6:
time: 55.8 us; the launch traced here: 55.6 us
  Pallas kernels  21.9 us (39%)
  starting transfers between devices  13.2 us (24%)
  blocking collectives  9.85 us (18%)
  waiting for transfers between devices  8.22 us (15%)
  local copies, waits for them, and re-layouts  1.65 us (3%)
  between operations  0.81 us (1%)
    ppermute x9, starting transfers between devices, passed_round(): lax.ppermute(x, axis, [(i, (i + by) % devices) for i in range(devices)])  13.2 us
    pallas_call x5, Pallas kernels, prints_of(): pl.pallas_call(functools.partial(print_kernel, shift, part, views), out_s...  10.3 us
    all_to_all x1, blocking collectives, local(): lax.all_to_all(blocks, 'tile', split_axis=0, concat_axis=0, tiled=True)  9.85 us
    ppermute x9, waiting for transfers between devices, passed_round(): lax.ppermute(x, axis, [(i, (i + by) % devices) for i in range(devices)])  8.22 us
    pallas_call x3, Pallas kernels, matter_of(): pl.pallas_call(functools.partial(matter_kernel, shift), out_shape=outs, i...  4.09 us
    pallas_call x1, Pallas kernels, turn_volume(): pl.pallas_call(turn_kernel, out_shape=[jax.ShapeDtypeStruct((blocks + 1,...  2.21 us
    pallas_call x1, Pallas kernels, matter_of(): pl.pallas_call(functools.partial(first_matter_kernel, shift, slices * (bl...  1.99 us
    unnamed x10, local copies, waits for them, and re-layouts  1.65 us
  transfers between devices with their start and end apart: 9, of which 3 were waited for; matrix products, arithmetic and copies ran while one was open for 0% of the time, Pallas kernels for 31%

profile of v6, /device:TPU:0, one launch (start us, length us, event | category | flops | bytes accessed | tf_op | source)
XLA Modules:
  0.0 55.6 jit_solution(10170758220985209436)
XLA Ops:
  0.0 1.6 %copy-done.4 = bf16[512,16,128]{2,1,0:T(8,128)(2,1)S(1)} copy-done((bf16[512,16,128]{2,1,0:T(8,128)(2,1)S(1)}, bf16[512,16,128]{2,1,0:T(8,128)(2,1)}, u32[]{:S(2)}) %copy-start.4) | copy-done | bytes 2097176
  1.6 2.2 %turn_rows.1 = (f32[5,16,128,128]{3,2,1,0:T(8,128)S(1)}, bf16[16,512]{1,0:T(8,128)(2,1)S(1)}, bf16[16,512]{1,0:T(8,128)(2,1)S(1)}) custom-call(bf16[512,16,128]{2,1,0:T(8,128)(2,1)S(1)} %copy-done.4), custom_call_target="tpu_custom_call" | custom-call | flops 10000000000 | bytes 100000000 | tf_op jit(solution)/shard_map/turn_rows/pallas_call | solution.py:284
  3.9 0.5 collective-permute-start
  4.4 2.9 %collective-permute-start.1 = (bf16[16,512]{1,0:T(8,128)(2,1)S(1)}, bf16[16,512]{1,0:T(8,128)(2,1)S(1)}, u32[]{:S(2)}, u32[]{:S(2)}) collective-permute-start(bf16[16,512]{1,0:T(8,128)(2,1)S(1)} %get-tuple-element.32), channel_id=1, source_target_pairs={{0,7},{1,0},{2,1},{3,2},{4,3},{5,4},{6,5},{7,6},{8,15},{9,8},{10,9... | collective-permute-start | bytes 49160 | tf_op jit(solution)/shard_map/ppermute | solution.py:368
  8.0 2.0 %matter.4 = (f32[17,8,128]{2,1,0:T(8,128)S(1)}, f32[16,128,128]{2,1,0:T(8,128)S(1)}, f32[3,16,128,128]{3,2,1,0:T(8,128)S(1)}, f32[16,128,128]{2,1,0:T(8,128)S(1)}) custom-call(s32[1,1]{1,0:T(1,128)S(6)} %copy.7.active_ref, f32[2,3]{1,0:T(2,128)S(1)} %copy-done, f32[4]{0:T(128)S(1)} %copy-done.2, f32[4]{0:T(128)S(1)} %copy-done.3, ...), custom_call_target="tpu_custom_call" | custom-call | flops 100000000 | bytes 1000000 | tf_op jit(solution)/shard_map/matter/pallas_call | solution.py:302
  10.0 0.9 %prints.5.after_ref = s16[4,192,128]{2,1,0:T(8,128)(2,1)S(1)} custom-call(f32[5,16,128,128]{3,2,1,0:T(8,128)S(1)} %get-tuple-element.29.field_ref, f32[17,8,128]{2,1,0:T(8,128)S(1)} %get-tuple-element.30.table_ref, bf16[16,512]{1,0:T(8,128)(2,1)S(1)} %collective-permute-done.left_ref.after_ref, bf16[16,512]{1,0:T(8,128)(2,1)S(1)} %collective-permute-done.1.right_ref, ...), custom_call_target="tpu_custom_call" | custom-call | flops 100000000 | bytes 1000000 | tf_op jit(solution)/shard_map/prints/pallas_call | solution.py:314
  11.1 1.6 %prints.6.after_ref.own_ref = f32[2,4,128,128]{3,2,1,0:T(8,128)S(1)} custom-call(f32[5,16,128,128]{3,2,1,0:T(8,128)S(1)} %get-tuple-element.29.field_ref, f32[17,8,128]{2,1,0:T(8,128)S(1)} %get-tuple-element.30.table_ref, bf16[16,512]{1,0:T(8,128)(2,1)S(1)} %collective-permute-done.left_ref.after_ref, bf16[16,512]{1,0:T(8,128)(2,1)S(1)} %collective-permute-done.1.right_ref, ...), custom_call_target="tpu_custom_call" | custom-call | flops 100000000 | bytes 1000000 | tf_op jit(solution)/shard_map/prints/pallas_call | solution.py:314
  12.7 1.4 %matter.5 = (f32[16,128,128]{2,1,0:T(8,128)S(1)}, f32[3,16,128,128]{3,2,1,0:T(8,128)S(1)}, f32[16,128,128]{2,1,0:T(8,128)S(1)}) custom-call(f32[5,16,128,128]{3,2,1,0:T(8,128)S(1)} %get-tuple-element.29.field_ref, f32[17,8,128]{2,1,0:T(8,128)S(1)} %get-tuple-element.30.table_ref, f32[2,4,128,128]{3,2,1,0:T(8,128)S(1)} %prints.6.after_ref.own_ref), custom_call_target="tpu_custom_call" | custom-call | flops 100000000 | bytes 1000000 | tf_op jit(solution)/shard_map/matter/pallas_call | solution.py:298
  14.0 2.6 %prints.7 = (f32[2,4,128,128]{3,2,1,0:T(8,128)S(1)}, s16[4,192,128]{2,1,0:T(8,128)(2,1)S(1)}) custom-call(f32[5,16,128,128]{3,2,1,0:T(8,128)S(1)} %get-tuple-element.29.field_ref, f32[17,8,128]{2,1,0:T(8,128)S(1)} %get-tuple-element.30.table_ref, bf16[16,512]{1,0:T(8,128)(2,1)S(1)} %collective-permute-done.left_ref.after_ref, ...), custom_call_target="tpu_custom_call" | custom-call | flops 100000000 | bytes 1000000 | tf_op jit(solution)/shard_map/prints/pallas_call | solution.py:314
  17.3 3.3 %collective-permute-start.6 = (s16[2,4,128,128]{3,2,1,0:T(8,128)(2,1)S(1)}, s16[2,4,128,128]{3,2,1,0:T(8,128)(2,1)S(1)}, u32[]{:S(2)}, u32[]{:S(2)}) collective-permute-start(s16[2,4,128,128]{3,2,1,0:T(8,128)(2,1)S(1)} %merge.3.after_ref), channel_id=1, source_target_pairs={{0,16},{8,24},{16,0},{24,8},{1,17},{9,25},{17,1},{25,9},{2,18},{10... | collective-permute-start | bytes 786440 | tf_op jit(solution)/shard_map/ppermute | solution.py:368
  20.6 1.4 %matter.6 = (f32[16,128,128]{2,1,0:T(8,128)S(1)}, f32[3,16,128,128]{3,2,1,0:T(8,128)S(1)}, f32[16,128,128]{2,1,0:T(8,128)S(1)}) custom-call(f32[5,16,128,128]{3,2,1,0:T(8,128)S(1)} %get-tuple-element.29.field_ref, f32[17,8,128]{2,1,0:T(8,128)S(1)} %get-tuple-element.30.table_ref, s16[2,4,128,128]{3,2,1,0:T(8,128)(2,1)S(1)} %merge.3.after_ref), custom_call_target="tpu_custom_call" | custom-call | flops 100000000 | bytes 1000000 | tf_op jit(solution)/shard_map/matter/pallas_call | solution.py:298
  22.0 2.6 %prints.8 = (f32[2,4,128,128]{3,2,1,0:T(8,128)S(1)}, s16[4,192,128]{2,1,0:T(8,128)(2,1)S(1)}) custom-call(f32[5,16,128,128]{3,2,1,0:T(8,128)S(1)} %get-tuple-element.29.field_ref, f32[17,8,128]{2,1,0:T(8,128)S(1)} %get-tuple-element.30.table_ref, bf16[16,512]{1,0:T(8,128)(2,1)S(1)} %collective-permute-done.left_ref.after_ref, ...), custom_call_target="tpu_custom_call" | custom-call | flops 100000000 | bytes 1000000 | tf_op jit(solution)/shard_map/prints/pallas_call | solution.py:314
  24.6 1.6 %collective-permute-start.4 = (s16[4,192,128]{2,1,0:T(8,128)(2,1)S(1)}, s16[4,192,128]{2,1,0:T(8,128)(2,1)S(1)}, u32[]{:S(2)}, u32[]{:S(2)}) collective-permute-start(s16[4,192,128]{2,1,0:T(8,128)(2,1)S(1)} %get-tuple-element.49), channel_id=1, source_target_pairs={{0,1},{1,2},{2,3},{3,4},{4,5},{5,6},{6,7},{7,0},{8,9},{9,10},{10,1... | collective-permute-start | bytes 589832 | tf_op jit(solution)/shard_map/ppermute | solution.py:368
  26.2 1.4 %matter.7 = (f32[16,128,128]{2,1,0:T(8,128)S(1)}, f32[3,16,128,128]{3,2,1,0:T(8,128)S(1)}, f32[16,128,128]{2,1,0:T(8,128)S(1)}) custom-call(f32[5,16,128,128]{3,2,1,0:T(8,128)S(1)} %get-tuple-element.29.field_ref, f32[17,8,128]{2,1,0:T(8,128)S(1)} %get-tuple-element.30.table_ref, f32[2,4,128,128]{3,2,1,0:T(8,128)S(1)} %get-tuple-element.44.after_ref.arrived_ref.own_ref), custom_call_target="tpu_custom_call" | custom-call | flops 100000000 | bytes 1000000 | tf_op jit(solution)/shard_map/matter/pallas_call | solution.py:298
  27.8 1.6 %collective-permute-start.7 = (s16[2,4,128,128]{3,2,1,0:T(8,128)(2,1)S(1)}, s16[2,4,128,128]{3,2,1,0:T(8,128)(2,1)S(1)}, u32[]{:S(2)}, u32[]{:S(2)}) collective-permute-start(s16[2,4,128,128]{3,2,1,0:T(8,128)(2,1)S(1)} %merge.4.after_ref), channel_id=1, source_target_pairs={{0,8},{8,16},{16,24},{24,0},{1,9},{9,17},{17,25},{25,1},{2,10},{10... | collective-permute-start | bytes 786440 | tf_op jit(solution)/shard_map/ppermute | solution.py:368
  29.4 2.6 %prints.9 = (f32[2,4,128,128]{3,2,1,0:T(8,128)S(1)}, s16[4,192,128]{2,1,0:T(8,128)(2,1)S(1)}) custom-call(f32[5,16,128,128]{3,2,1,0:T(8,128)S(1)} %get-tuple-element.29.field_ref, f32[17,8,128]{2,1,0:T(8,128)S(1)} %get-tuple-element.30.table_ref, bf16[16,512]{1,0:T(8,128)(2,1)S(1)} %collective-permute-done.left_ref.after_ref, ...), custom_call_target="tpu_custom_call" | custom-call | flops 100000000 | bytes 1000000 | tf_op jit(solution)/shard_map/prints/pallas_call | solution.py:314
  32.4 0.8 %collective-permute-start.5 = (s16[4,192,128]{2,1,0:T(8,128)(2,1)S(1)}, s16[4,192,128]{2,1,0:T(8,128)(2,1)S(1)}, u32[]{:S(2)}, u32[]{:S(2)}) collective-permute-start(s16[4,192,128]{2,1,0:T(8,128)(2,1)S(1)} %get-tuple-element.51), channel_id=1, source_target_pairs={{0,1},{1,2},{2,3},{3,4},{4,5},{5,6},{6,7},{7,0},{8,9},{9,10},{10,1... | collective-permute-start | bytes 589832 | tf_op jit(solution)/shard_map/ppermute | solution.py:368
  33.1 2.2 %collective-permute-start.8 = (s16[2,4,128,128]{3,2,1,0:T(8,128)(2,1)S(1)}, s16[2,4,128,128]{3,2,1,0:T(8,128)(2,1)S(1)}, u32[]{:S(2)}, u32[]{:S(2)}) collective-permute-start(s16[2,4,128,128]{3,2,1,0:T(8,128)(2,1)S(1)} %get-tuple-element.52), channel_id=1, source_target_pairs={{0,24},{8,0},{16,8},{24,16},{1,25},{9,1},{17,9},{25,17},{2,26},{10... | collective-permute-start | bytes 786440 | tf_op jit(solution)/shard_map/ppermute | solution.py:368
  35.5 3.4 %collective-permute-done.7.refs_1_ = s16[2,4,128,128]{3,2,1,0:T(8,128)(2,1)S(1)} collective-permute-done((s16[2,4,128,128]{3,2,1,0:T(8,128)(2,1)S(1)}, s16[2,4,128,128]{3,2,1,0:T(8,128)(2,1)S(1)}, u32[]{:S(2)}, u32[]{:S(2)}) %collective-permute-start.7) | collective-permute-done | bytes 262176 | tf_op jit(solution)/shard_map/ppermute | solution.py:368
  39.0 1.1 %early.1.mix_ref = f32[2,8,128,128]{3,2,1,0:T(8,128)S(1)} custom-call(s32[2,4]{1,0:T(2,128)S(1)} %copy-done.1, f32[2,4,128,128]{3,2,1,0:T(8,128)S(1)} %get-tuple-element.48.arrived_ref.own_ref, s16[4,192,128]{2,1,0:T(8,128)(2,1)S(1)} %collective-permute-done.5.over_ref, f32[2,4,128,128]{3,2,1,0:T(8,128)S(1)} %opened.1.refs_0_, ...), custom_call_target="tpu_custom_call" | custom-call | flops 100000000 | bytes 1000000 | tf_op jit(solution)/shard_map/early/pallas_call | solution.py:344
  40.0 4.5 %collective-permute-done.8.layer_ref = s16[2,4,128,128]{3,2,1,0:T(8,128)(2,1)S(1)} collective-permute-done((s16[2,4,128,128]{3,2,1,0:T(8,128)(2,1)S(1)}, s16[2,4,128,128]{3,2,1,0:T(8,128)(2,1)S(1)}, u32[]{:S(2)}, u32[]{:S(2)}) %collective-permute-start.8) | collective-permute-done | bytes 262176 | tf_op jit(solution)/shard_map/ppermute | solution.py:368
  44.5 0.3 final.1
  44.9 9.8 %all_to_all.5.blocks_ref = s16[8,2,4,16,128]{4,3,2,1,0:T(8,128)(2,1)S(1)} all-to-all(s16[8,2,4,16,128]{4,3,2,1,0:T(8,128)(2,1)S(1)} %final.1), channel_id=1, replica_groups=mesh['depth'=4,'tile'=8] {'tile'}, dimensions={0} | all-to-all | bytes 524288 | tf_op jit(solution)/shard_map/all_to_all | solution.py:404
  54.7 0.9 %place.1 = f32[2,4,16,1024]{3,2,1,0:T(8,128)} custom-call(s16[8,2,4,16,128]{4,3,2,1,0:T(8,128)(2,1)S(1)} %all_to_all.5.blocks_ref), custom_call_target="tpu_custom_call" | custom-call | tf_op jit(solution)/shard_map/place/pallas_call | solution.py:361
  (22 shorter events, 1.5 us)
Async XLA Ops:
  0.0 8.0 %copy-start.2 = (f32[4]{0:T(128)S(1)}, f32[4]{0:T(128)}, u32[]{:S(2)}) copy-start(f32[4]{0:T(128)} %gain_ref.1) | copy-start | bytes 52
  0.0 8.0 %copy-start.3 = (f32[4]{0:T(128)S(1)}, f32[4]{0:T(128)}, u32[]{:S(2)}) copy-start(f32[4]{0:T(128)} %bias_ref.1) | copy-start | bytes 52
  0.0 8.0 %copy-start = (f32[2,3]{1,0:T(2,128)S(1)}, f32[2,3]{1,0:T(2,128)}, u32[]{:S(2)}) copy-start(f32[2,3]{1,0:T(2,128)} %light_ref.1) | copy-start | bytes 76
  0.0 1.6 %copy-start.4 = (bf16[512,16,128]{2,1,0:T(8,128)(2,1)S(1)}, bf16[512,16,128]{2,1,0:T(8,128)(2,1)}, u32[]{:S(2)}) copy-start(bf16[512,16,128]{2,1,0:T(8,128)(2,1)} %volume_ref.1) | copy-start | bytes 6291460
  3.9 6.1 %collective-permute-start = (bf16[16,512]{1,0:T(8,128)(2,1)S(1)}, bf16[16,512]{1,0:T(8,128)(2,1)S(1)}, u32[]{:S(2)}, u32[]{:S(2)}) collective-permute-start(bf16[16,512]{1,0:T(8,128)(2,1)S(1)} %get-tuple-element.31), channel_id=1, source_target_pairs={{0,1},{1,2},{2,3},{3,4},{4,5},{5,6},{6,7},{7,0},{8,9},{9,10},{10,1... | collective-permute-start | bytes 49160 | tf_op jit(solution)/shard_map/ppermute | solution.py:368
  4.4 5.6 %collective-permute-start.1 = (bf16[16,512]{1,0:T(8,128)(2,1)S(1)}, bf16[16,512]{1,0:T(8,128)(2,1)S(1)}, u32[]{:S(2)}, u32[]{:S(2)}) collective-permute-start(bf16[16,512]{1,0:T(8,128)(2,1)S(1)} %get-tuple-element.32), channel_id=1, source_target_pairs={{0,7},{1,0},{2,1},{3,2},{4,3},{5,4},{6,5},{7,6},{8,15},{9,8},{10,9... | collective-permute-start | bytes 49160 | tf_op jit(solution)/shard_map/ppermute | solution.py:368
  10.9 6.0 %collective-permute-start.3 = (s16[4,192,128]{2,1,0:T(8,128)(2,1)S(1)}, s16[4,192,128]{2,1,0:T(8,128)(2,1)S(1)}, u32[]{:S(2)}, u32[]{:S(2)}) collective-permute-start(s16[4,192,128]{2,1,0:T(8,128)(2,1)S(1)} %prints.5.after_ref), channel_id=1, source_target_pairs={{0,1},{1,2},{2,3},{3,4},{4,5},{5,6},{6,7},{7,0},{8,9},{9,10},{10,1... | collective-permute-start | bytes 589832 | tf_op jit(solution)/shard_map/ppermute | solution.py:368
  17.3 18.1 %collective-permute-start.6 = (s16[2,4,128,128]{3,2,1,0:T(8,128)(2,1)S(1)}, s16[2,4,128,128]{3,2,1,0:T(8,128)(2,1)S(1)}, u32[]{:S(2)}, u32[]{:S(2)}) collective-permute-start(s16[2,4,128,128]{3,2,1,0:T(8,128)(2,1)S(1)} %merge.3.after_ref), channel_id=1, source_target_pairs={{0,16},{8,24},{16,0},{24,8},{1,17},{9,25},{17,1},{25,9},{2,18},{10... | collective-permute-start | bytes 786440 | tf_op jit(solution)/shard_map/ppermute | solution.py:368
  20.6 6.9 %collective-permute-start.2 = (s16[4,192,128]{2,1,0:T(8,128)(2,1)S(1)}, s16[4,192,128]{2,1,0:T(8,128)(2,1)S(1)}, u32[]{:S(2)}, u32[]{:S(2)}) collective-permute-start(s16[4,192,128]{2,1,0:T(8,128)(2,1)S(1)} %get-tuple-element.40), channel_id=1, source_target_pairs={{0,1},{1,2},{2,3},{3,4},{4,5},{5,6},{6,7},{7,0},{8,9},{9,10},{10,1... | collective-permute-start | bytes 589832 | tf_op jit(solution)/shard_map/ppermute | solution.py:368
  24.6 7.5 %collective-permute-start.4 = (s16[4,192,128]{2,1,0:T(8,128)(2,1)S(1)}, s16[4,192,128]{2,1,0:T(8,128)(2,1)S(1)}, u32[]{:S(2)}, u32[]{:S(2)}) collective-permute-start(s16[4,192,128]{2,1,0:T(8,128)(2,1)S(1)} %get-tuple-element.49), channel_id=1, source_target_pairs={{0,1},{1,2},{2,3},{3,4},{4,5},{5,6},{6,7},{7,0},{8,9},{9,10},{10,1... | collective-permute-start | bytes 589832 | tf_op jit(solution)/shard_map/ppermute | solution.py:368
  27.8 11.1 %collective-permute-start.7 = (s16[2,4,128,128]{3,2,1,0:T(8,128)(2,1)S(1)}, s16[2,4,128,128]{3,2,1,0:T(8,128)(2,1)S(1)}, u32[]{:S(2)}, u32[]{:S(2)}) collective-permute-start(s16[2,4,128,128]{3,2,1,0:T(8,128)(2,1)S(1)} %merge.4.after_ref), channel_id=1, source_target_pairs={{0,8},{8,16},{16,24},{24,0},{1,9},{9,17},{17,25},{25,1},{2,10},{10... | collective-permute-start | bytes 786440 | tf_op jit(solution)/shard_map/ppermute | solution.py:368
  32.4 6.6 %collective-permute-start.5 = (s16[4,192,128]{2,1,0:T(8,128)(2,1)S(1)}, s16[4,192,128]{2,1,0:T(8,128)(2,1)S(1)}, u32[]{:S(2)}, u32[]{:S(2)}) collective-permute-start(s16[4,192,128]{2,1,0:T(8,128)(2,1)S(1)} %get-tuple-element.51), channel_id=1, source_target_pairs={{0,1},{1,2},{2,3},{3,4},{4,5},{5,6},{6,7},{7,0},{8,9},{9,10},{10,1... | collective-permute-start | bytes 589832 | tf_op jit(solution)/shard_map/ppermute | solution.py:368
  33.1 5.8 %copy-start.1 = (s32[2,4]{1,0:T(2,128)S(1)}, s32[2,4]{1,0:T(2,128)}, u32[]{:S(2)}) copy-start(s32[2,4]{1,0:T(2,128)} %order_ref.1) | copy-start | bytes 100
  33.1 11.4 %collective-permute-start.8 = (s16[2,4,128,128]{3,2,1,0:T(8,128)(2,1)S(1)}, s16[2,4,128,128]{3,2,1,0:T(8,128)(2,1)S(1)}, u32[]{:S(2)}, u32[]{:S(2)}) collective-permute-start(s16[2,4,128,128]{3,2,1,0:T(8,128)(2,1)S(1)} %get-tuple-element.52), channel_id=1, source_target_pairs={{0,24},{8,0},{16,8},{24,16},{1,25},{9,1},{17,9},{25,17},{2,26},{10... | collective-permute-start | bytes 786440 | tf_op jit(solution)/shard_map/ppermute | solution.py:368

commit v7 on v6

--- a/solution.py
+++ b/solution.py
@@ -30,7 +30,7 @@
     return jnp.where(value == code_none, 0.0, lax.exp2(value * (1.0 / code_step) - code_middle))
 
 
-def turn_kernel(volume_ref, field_ref, low_ref, high_ref, ordered):
+def turn_kernel(volume_ref, field_ref, near_ref, far_ref, ordered):
     rows, slices, columns = volume_ref.shape
     blocks, _, _, width = field_ref.shape
     blocks = blocks - 1
@@ -49,20 +49,23 @@
         return carry
 
     lax.fori_loop(0, slices, turn, 0)
-    for edge_ref, x in ((low_ref, 0), (high_ref, columns - 1)):
-        for block in range(blocks):
-            edge_ref[:, block * width:(block + 1) * width] = field_ref[block, :, x, :].astype(edge_ref.dtype)
+    even = lax.rem(lax.axis_index("tile"), 2) == 0
+    for block in range(blocks):
+        low, high = field_ref[block, :, 0, :], field_ref[block, :, columns - 1, :]
+        along = slice(block * width, (block + 1) * width)
+        near_ref[:, along] = jnp.where(even, high, low).astype(near_ref.dtype)
+        far_ref[:, along] = jnp.where(even, low, high).astype(far_ref.dtype)
 
 
 def make_table(total_z, active_ref, light_ref, gain_ref, bias_ref, table_ref):
-    def spread(value):
-        return jnp.full(table_ref.shape[1:], value, jnp.float32)
+    def wide(ref, k):
+        return jnp.broadcast_to(ref[:, k:k + 1], table_ref.shape[1:])
 
     values = [jnp.broadcast_to(active_ref[...].astype(jnp.float32) * (-2.0 / total_z), table_ref.shape[1:])]
-    values += [spread(0.5 * gain_ref[k]) for k in range(3)] + [spread(gain_ref[3] * (1.0 / LN2))]
-    values += [spread(0.5 * bias_ref[k]) for k in range(3)] + [spread(bias_ref[3] * (1.0 / LN2))]
+    values += [0.5 * wide(gain_ref, k) for k in range(3)] + [wide(gain_ref, 3) * (1.0 / LN2)]
+    values += [0.5 * wide(bias_ref, k) for k in range(3)] + [wide(bias_ref, 3) * (1.0 / LN2)]
     for v in range(light_ref.shape[0]):
-        parts = [spread(light_ref[v, k]) for k in range(3)]
+        parts = [jnp.broadcast_to(light_ref[v:v + 1, k:k + 1], table_ref.shape[1:]) for k in range(3)]
         square = jnp.maximum(parts[0] * parts[0] + parts[1] * parts[1] + parts[2] * parts[2], 1e-30)
         unit = (0.35 * LN2) * lax.rsqrt(square)
         values += [part * unit for part in parts] + [4.0 / square]
@@ -114,7 +117,7 @@
     matter_kernel(shift, field_ref, table_ref, None, *refs)
 
 
-def print_kernel(shift, part, views, field_ref, table_ref, left_ref, right_ref, after_ref, thick_ref, tints_ref, slope_ref,
+def print_kernel(shift, part, views, field_ref, table_ref, near_ref, far_ref, after_ref, thick_ref, tints_ref, slope_ref,
                  *refs):
     blocks, slices, columns, width = field_ref.shape
     group = table_ref.shape[1]
@@ -130,8 +133,11 @@
         total[pl.ds(*used), :] = jnp.zeros((used[1], width), jnp.float32)
     along = pl.ds(pl.multiple_of(block * width, width), width)
     tile = lax.axis_index("tile")
-    left = left_ref[:, along].astype(jnp.float32) * jnp.where(tile > 0, 1.0, 0.0)
-    right = right_ref[:, along].astype(jnp.float32) * jnp.where(tile + 1 < lax.axis_size("tile"), 1.0, 0.0)
+    even = lax.rem(tile, 2) == 0
+    near = near_ref[:, along].astype(jnp.float32)
+    far_edge = far_ref[:, along].astype(jnp.float32)
+    left = jnp.where(even, far_edge, near) * jnp.where(tile > 0, 1.0, 0.0)
+    right = jnp.where(even, near, far_edge) * jnp.where(tile + 1 < lax.axis_size("tile"), 1.0, 0.0)
 
     def wanted(v, j, z):
         first = j * group + z * (v + 1) * quad
@@ -301,11 +307,11 @@
     table = jax.ShapeDtypeStruct((9 + 4 * smalls[1].shape[0], 8, width), jnp.float32)
     return pl.pallas_call(
         functools.partial(first_matter_kernel, shift, slices * (blocks - 1)), out_shape=[table] + outs,
-        in_specs=[vmem] + [smem] * 3 + [vmem], out_specs=[vmem] * 4,
+        in_specs=[vmem] * 5, out_specs=[vmem] * 4,
         cost_estimate=short_cost, compiler_params=params, name="matter")(*smalls, field)
 
 
-def prints_of(field, matter, table, left, right, after, shift, views, part):
+def prints_of(field, matter, table, near, beyond, after, shift, views, part):
     blocks, slices, columns, width = field.shape
     shape = (views, 4, columns, width)
     over_shape = (4, sum(over_rows(views - 1, slices, columns)), width)
@@ -315,7 +321,7 @@
         functools.partial(print_kernel, shift, part, views), out_shape=outs,
         in_specs=[vmem] * 4 + [far] + [vmem] * 3, out_specs=[vmem] * len(outs),
         scratch_shapes=[pltpu.VMEM((2 * columns, width), jnp.float32)] * (4 * views),
-        cost_estimate=short_cost, compiler_params=params, name="prints")(field, table, left, right, after, *matter)
+        cost_estimate=short_cost, compiler_params=params, name="prints")(field, table, near, beyond, after, *matter)
 
 
 def merge_of(own, over, later, arrived, slices, passing):
@@ -366,6 +372,12 @@
 def passed_round(x, axis, by):
     devices = lax.axis_size(axis)
     return lax.ppermute(x, axis, [(i, (i + by) % devices) for i in range(devices)])
+
+
+def swapped(x, axis, by):
+    devices = lax.axis_size(axis)
+    pairs = [(i, (i + by * (1 - 2 * (i % 2))) % devices) for i in range(devices)]
+    return lax.ppermute(x, axis, pairs)
 
 
 def local(volume, active, depth_order, light_vector, class_gain, class_bias):
@@ -373,31 +385,36 @@
     tile_count = lax.axis_size("tile")
     rows, slices, columns = volume.shape
     share = rows // (depth_count * tile_count)
-    field, low, high = turn_volume(volume, depth_count)
-    left = passed_round(high, "tile", 1)
-    right = passed_round(low, "tile", -1)
+    field, to_near, to_beyond = turn_volume(volume, depth_count)
+    beyond = swapped(to_beyond, "tile", -1)
+    near = swapped(to_near, "tile", 1)
     shifts = sorted(range(1, depth_count), key=lambda shift: -min(shift, depth_count - shift)) + [0]
-    smalls = (active, light_vector, class_gain, class_bias)
-    table, ready, waiting, layers = None, left, [], []
+    smalls = (active, light_vector, class_gain[None], class_bias[None])
+    table, ready, waiting, layers = None, near, [], []
     views = light_vector.shape[0]
     for index, shift in enumerate(shifts):
-        last = index + 1 == len(shifts)
-        if index == 0:
+        first, last = index == 0, index + 1 == len(shifts)
+        if first:
             table, *matter = matter_of(field, shift, smalls=smalls)
-            sources = field, matter, table, left, right
-            over, = prints_of(*sources, ready, shift, views, "over")
-            own, = prints_of(*sources, over, shift, views, "own")
         else:
             matter = matter_of(field, shift, table=table, after=ready)
-            if len(waiting) > 1:
-                ready, = merge_of(*waiting.pop(0), matter[0], ready, slices, False)
-                layers.append(passed_round(ready, "depth", shifts[len(layers)]))
-            own, over = prints_of(field, matter, table, left, right, ready, shift, views, "all")
-        ready = own
+        if len(waiting) > 1:
+            ready, = merge_of(*waiting.pop(0), matter[0], ready, slices, False)
+            layers.append(passed_round(ready, "depth", shifts[len(layers)]))
+        sources = field, matter, table, near, beyond
+        if first or last:
+            over, = prints_of(*sources, ready, shift, views, "over")
+            ready = over
+        else:
+            own, over = prints_of(*sources, ready, shift, views, "all")
+            ready = own
         if index == 1 or last and waiting:
-            ready, *passed = merge_of(*waiting.pop(0), over if last else own, ready, slices, last)
+            ready, *passed = merge_of(*waiting.pop(0), over if last else ready, ready, slices, last)
             over = passed[0] if last else over
             layers.append(passed_round(ready, "depth", shifts[len(layers)]))
+        if first or last:
+            own, = prints_of(*sources, ready, shift, views, "own")
+            ready = own if first else ready
         waiting.append((own, passed_round(over, "tile", 1)))
     mix = early_of(depth_order, *waiting[0], [open_of(layers[0])] + layers[1:-1], shifts[:-1], slices)
     blocks = final_of(mix, layers[-1], share)

time: 55.8 us -> 55.5 us (level)
  starting transfers between devices: 13.2 us -> 11.7 us
  waiting for transfers between devices: 8.22 us -> 9.17 us
  blocking collectives: 9.85 us -> 10.7 us
  Pallas kernels: 21.9 us -> 21.3 us
    ppermute x9 -> x7, starting transfers between devices: 13.2 us -> 7.58 us  [passed_round(): lax.ppermute(x, axis, [(i, (i + by) % devices) for i in range(devices)])]
    ppermute x0 -> x2, starting transfers between devices: none -> 4.07 us  [swapped(): return lax.ppermute(x, axis, pairs)]
    ppermute x9 -> x7, waiting for transfers between devices: 8.22 us -> 9.16 us  [passed_round(): lax.ppermute(x, axis, [(i, (i + by) % devices) for i in range(devices)])]
    all_to_all x1, blocking collectives: 9.85 us -> 10.7 us  [local(): lax.all_to_all(blocks, 'tile', split_axis=0, concat_axis=0, tiled=True)]
    pallas_call x5 -> x6, Pallas kernels: 10.3 us -> 10.2 us  [prints_of(): pl.pallas_call(functools.partial(print_kernel, shift, part, views), out_s...]
  transfers between devices with their start and end apart: 9 -> 9, of which waited for: 3 -> 4; matrix products, arithmetic and copies ran while one was open for 0% -> 0% of each run, Pallas kernels for 31% -> 30%
where the time goes in v7:
time: 55.5 us; the launch traced here: 55.3 us
  Pallas kernels  21.3 us (38%)
  starting transfers between devices  11.7 us (21%)
  blocking collectives  10.7 us (19%)
  waiting for transfers between devices  9.17 us (17%)
  local copies, waits for them, and re-layouts  1.65 us (3%)
  between operations  0.84 us (2%)
    all_to_all x1, blocking collectives, local(): lax.all_to_all(blocks, 'tile', split_axis=0, concat_axis=0, tiled=True)  10.7 us
    pallas_call x6, Pallas kernels, prints_of(): pl.pallas_call(functools.partial(print_kernel, shift, part, views), out_s...  10.2 us
    ppermute x7, waiting for transfers between devices, passed_round(): lax.ppermute(x, axis, [(i, (i + by) % devices) for i in range(devices)])  9.16 us
    ppermute x7, starting transfers between devices, passed_round(): lax.ppermute(x, axis, [(i, (i + by) % devices) for i in range(devices)])  7.58 us
    pallas_call x3, Pallas kernels, matter_of(): pl.pallas_call(functools.partial(matter_kernel, shift), out_shape=outs, i...  4.09 us
    ppermute x2, starting transfers between devices, swapped(): return lax.ppermute(x, axis, pairs)  4.07 us
    pallas_call x1, Pallas kernels, turn_volume(): pl.pallas_call(turn_kernel, out_shape=[jax.ShapeDtypeStruct((blocks + 1,...  2.23 us
    unnamed x10, local copies, waits for them, and re-layouts  1.65 us
  transfers between devices with their start and end apart: 9, of which 4 were waited for; matrix products, arithmetic and copies ran while one was open for 0% of the time, Pallas kernels for 30%

profile of v7, /device:TPU:0, one launch (start us, length us, event | category | flops | bytes accessed | tf_op | source)
XLA Modules:
  0.0 55.3 jit_solution(5873717025847706756)
XLA Ops:
  0.0 1.6 %copy-done.4 = bf16[512,16,128]{2,1,0:T(8,128)(2,1)S(1)} copy-done((bf16[512,16,128]{2,1,0:T(8,128)(2,1)S(1)}, bf16[512,16,128]{2,1,0:T(8,128)(2,1)}, u32[]{:S(2)}) %copy-start.4) | copy-done | bytes 2097176
  1.6 2.2 %turn_rows.1 = (f32[5,16,128,128]{3,2,1,0:T(8,128)S(1)}, bf16[16,512]{1,0:T(8,128)(2,1)S(1)}, bf16[16,512]{1,0:T(8,128)(2,1)S(1)}) custom-call(bf16[512,16,128]{2,1,0:T(8,128)(2,1)S(1)} %copy-done.4), custom_call_target="tpu_custom_call" | custom-call | flops 10000000000 | bytes 100000000 | tf_op jit(solution)/shard_map/turn_rows/pallas_call | solution.py:290
  3.9 0.5 collective-permute-start
  4.4 3.6 %collective-permute-start.1 = (bf16[16,512]{1,0:T(8,128)(2,1)S(1)}, bf16[16,512]{1,0:T(8,128)(2,1)S(1)}, u32[]{:S(2)}, u32[]{:S(2)}) collective-permute-start(bf16[16,512]{1,0:T(8,128)(2,1)S(1)} %get-tuple-element.30), channel_id=1, source_target_pairs={{0,7},{1,2},{2,1},{3,4},{4,3},{5,6},{6,5},{7,0},{8,15},{9,10},{10,... | collective-permute-start | bytes 49160 | tf_op jit(solution)/shard_map/ppermute | solution.py:380
  8.6 1.5 %matter.4 = (f32[17,8,128]{2,1,0:T(8,128)S(1)}, f32[16,128,128]{2,1,0:T(8,128)S(1)}, f32[3,16,128,128]{3,2,1,0:T(8,128)S(1)}, f32[16,128,128]{2,1,0:T(8,128)S(1)}) custom-call(s32[1,1]{1,0:T(1,128)S(6)} %copy.7.active_ref, f32[2,3]{1,0:T(2,128)S(1)} %copy-done, f32[1,4]{1,0:T(1,128)S(1)} %bitcast.2, f32[1,4]{1,0:T(1,128)S(1)} %bitcast.3, ...), custom_call_target="tpu_custom_call" | custom-call | flops 100000000 | bytes 1000000 | tf_op jit(solution)/shard_map/matter/pallas_call | solution.py:308
  10.1 0.9 %prints.6.after_ref = s16[4,192,128]{2,1,0:T(8,128)(2,1)S(1)} custom-call(f32[5,16,128,128]{3,2,1,0:T(8,128)S(1)} %get-tuple-element.27.field_ref, f32[17,8,128]{2,1,0:T(8,128)S(1)} %get-tuple-element.28.table_ref, bf16[16,512]{1,0:T(8,128)(2,1)S(1)} %collective-permute-done.near_ref.after_ref, bf16[16,512]{1,0:T(8,128)(2,1)S(1)} %collective-permute-done.1.far_ref, ...), custom_call_target="tpu_custom_call" | custom-call | flops 100000000 | bytes 1000000 | tf_op jit(solution)/shard_map/prints/pallas_call | solution.py:320
  11.1 1.6 %prints.7.after_ref.own_ref = f32[2,4,128,128]{3,2,1,0:T(8,128)S(1)} custom-call(f32[5,16,128,128]{3,2,1,0:T(8,128)S(1)} %get-tuple-element.27.field_ref, f32[17,8,128]{2,1,0:T(8,128)S(1)} %get-tuple-element.28.table_ref, bf16[16,512]{1,0:T(8,128)(2,1)S(1)} %collective-permute-done.near_ref.after_ref, bf16[16,512]{1,0:T(8,128)(2,1)S(1)} %collective-permute-done.1.far_ref, ...), custom_call_target="tpu_custom_call" | custom-call | flops 100000000 | bytes 1000000 | tf_op jit(solution)/shard_map/prints/pallas_call | solution.py:320
  12.7 1.4 %matter.5 = (f32[16,128,128]{2,1,0:T(8,128)S(1)}, f32[3,16,128,128]{3,2,1,0:T(8,128)S(1)}, f32[16,128,128]{2,1,0:T(8,128)S(1)}) custom-call(f32[5,16,128,128]{3,2,1,0:T(8,128)S(1)} %get-tuple-element.27.field_ref, f32[17,8,128]{2,1,0:T(8,128)S(1)} %get-tuple-element.28.table_ref, f32[2,4,128,128]{3,2,1,0:T(8,128)S(1)} %prints.7.after_ref.own_ref), custom_call_target="tpu_custom_call" | custom-call | flops 100000000 | bytes 1000000 | tf_op jit(solution)/shard_map/matter/pallas_call | solution.py:304
  14.1 2.6 %prints.8 = (f32[2,4,128,128]{3,2,1,0:T(8,128)S(1)}, s16[4,192,128]{2,1,0:T(8,128)(2,1)S(1)}) custom-call(f32[5,16,128,128]{3,2,1,0:T(8,128)S(1)} %get-tuple-element.27.field_ref, f32[17,8,128]{2,1,0:T(8,128)S(1)} %get-tuple-element.28.table_ref, bf16[16,512]{1,0:T(8,128)(2,1)S(1)} %collective-permute-done.near_ref.after_ref, ...), custom_call_target="tpu_custom_call" | custom-call | flops 100000000 | bytes 1000000 | tf_op jit(solution)/shard_map/prints/pallas_call | solution.py:320
  17.4 2.7 %collective-permute-start.6 = (s16[2,4,128,128]{3,2,1,0:T(8,128)(2,1)S(1)}, s16[2,4,128,128]{3,2,1,0:T(8,128)(2,1)S(1)}, u32[]{:S(2)}, u32[]{:S(2)}) collective-permute-start(s16[2,4,128,128]{3,2,1,0:T(8,128)(2,1)S(1)} %merge.3.after_ref), channel_id=1, source_target_pairs={{0,16},{8,24},{16,0},{24,8},{1,17},{9,25},{17,1},{25,9},{2,18},{10... | collective-permute-start | bytes 786440 | tf_op jit(solution)/shard_map/ppermute | solution.py:374
  20.1 1.4 %matter.6 = (f32[16,128,128]{2,1,0:T(8,128)S(1)}, f32[3,16,128,128]{3,2,1,0:T(8,128)S(1)}, f32[16,128,128]{2,1,0:T(8,128)S(1)}) custom-call(f32[5,16,128,128]{3,2,1,0:T(8,128)S(1)} %get-tuple-element.27.field_ref, f32[17,8,128]{2,1,0:T(8,128)S(1)} %get-tuple-element.28.table_ref, s16[2,4,128,128]{3,2,1,0:T(8,128)(2,1)S(1)} %merge.3.after_ref), custom_call_target="tpu_custom_call" | custom-call | flops 100000000 | bytes 1000000 | tf_op jit(solution)/shard_map/matter/pallas_call | solution.py:304
  21.4 2.6 %prints.9 = (f32[2,4,128,128]{3,2,1,0:T(8,128)S(1)}, s16[4,192,128]{2,1,0:T(8,128)(2,1)S(1)}) custom-call(f32[5,16,128,128]{3,2,1,0:T(8,128)S(1)} %get-tuple-element.27.field_ref, f32[17,8,128]{2,1,0:T(8,128)S(1)} %get-tuple-element.28.table_ref, bf16[16,512]{1,0:T(8,128)(2,1)S(1)} %collective-permute-done.near_ref.after_ref, ...), custom_call_target="tpu_custom_call" | custom-call | flops 100000000 | bytes 1000000 | tf_op jit(solution)/shard_map/prints/pallas_call | solution.py:320
  24.0 1.1 %collective-permute-start.3 = (s16[4,192,128]{2,1,0:T(8,128)(2,1)S(1)}, s16[4,192,128]{2,1,0:T(8,128)(2,1)S(1)}, u32[]{:S(2)}, u32[]{:S(2)}) collective-permute-start(s16[4,192,128]{2,1,0:T(8,128)(2,1)S(1)} %get-tuple-element.42), channel_id=1, source_target_pairs={{0,1},{1,2},{2,3},{3,4},{4,5},{5,6},{6,7},{7,0},{8,9},{9,10},{10,1... | collective-permute-start | bytes 589832 | tf_op jit(solution)/shard_map/ppermute | solution.py:374
  25.1 1.4 %matter.7 = (f32[16,128,128]{2,1,0:T(8,128)S(1)}, f32[3,16,128,128]{3,2,1,0:T(8,128)S(1)}, f32[16,128,128]{2,1,0:T(8,128)S(1)}) custom-call(f32[5,16,128,128]{3,2,1,0:T(8,128)S(1)} %get-tuple-element.27.field_ref, f32[17,8,128]{2,1,0:T(8,128)S(1)} %get-tuple-element.28.table_ref, f32[2,4,128,128]{3,2,1,0:T(8,128)S(1)} %get-tuple-element.41.after_ref.arrived_ref.own_ref), custom_call_target="tpu_custom_call" | custom-call | flops 100000000 | bytes 1000000 | tf_op jit(solution)/shard_map/matter/pallas_call | solution.py:304
  26.8 1.6 %collective-permute-start.7 = (s16[2,4,128,128]{3,2,1,0:T(8,128)(2,1)S(1)}, s16[2,4,128,128]{3,2,1,0:T(8,128)(2,1)S(1)}, u32[]{:S(2)}, u32[]{:S(2)}) collective-permute-start(s16[2,4,128,128]{3,2,1,0:T(8,128)(2,1)S(1)} %merge.4.after_ref), channel_id=1, source_target_pairs={{0,8},{8,16},{16,24},{24,0},{1,9},{9,17},{17,25},{25,1},{2,10},{10... | collective-permute-start | bytes 786440 | tf_op jit(solution)/shard_map/ppermute | solution.py:374
  28.4 0.9 %prints.10.later_ref.arrived_ref = s16[4,192,128]{2,1,0:T(8,128)(2,1)S(1)} custom-call(f32[5,16,128,128]{3,2,1,0:T(8,128)S(1)} %get-tuple-element.27.field_ref, f32[17,8,128]{2,1,0:T(8,128)S(1)} %get-tuple-element.28.table_ref, bf16[16,512]{1,0:T(8,128)(2,1)S(1)} %collective-permute-done.near_ref.after_ref, ...), custom_call_target="tpu_custom_call" | custom-call | flops 100000000 | bytes 1000000 | tf_op jit(solution)/shard_map/prints/pallas_call | solution.py:320
  29.3 0.8 %collective-permute-done.3.over_ref = s16[4,192,128]{2,1,0:T(8,128)(2,1)S(1)} collective-permute-done((s16[4,192,128]{2,1,0:T(8,128)(2,1)S(1)}, s16[4,192,128]{2,1,0:T(8,128)(2,1)S(1)}, u32[]{:S(2)}, u32[]{:S(2)}) %collective-permute-start.3) | collective-permute-done | bytes 196640 | tf_op jit(solution)/shard_map/ppermute | solution.py:374
  30.4 2.1 %collective-permute-start.8 = (s16[2,4,128,128]{3,2,1,0:T(8,128)(2,1)S(1)}, s16[2,4,128,128]{3,2,1,0:T(8,128)(2,1)S(1)}, u32[]{:S(2)}, u32[]{:S(2)}) collective-permute-start(s16[2,4,128,128]{3,2,1,0:T(8,128)(2,1)S(1)} %get-tuple-element.47.after_ref), channel_id=1, source_target_pairs={{0,24},{8,0},{16,8},{24,16},{1,25},{9,1},{17,9},{25,17},{2,26},{10... | collective-permute-start | bytes 786440 | tf_op jit(solution)/shard_map/ppermute | solution.py:374
  32.5 1.6 %prints.11.own_ref = f32[2,4,128,128]{3,2,1,0:T(8,128)S(1)} custom-call(f32[5,16,128,128]{3,2,1,0:T(8,128)S(1)} %get-tuple-element.27.field_ref, f32[17,8,128]{2,1,0:T(8,128)S(1)} %get-tuple-element.28.table_ref, bf16[16,512]{1,0:T(8,128)(2,1)S(1)} %collective-permute-done.near_ref.after_ref, bf16[16,512]{1,0:T(8,128)(2,1)S(1)} %collective-permute-done.1.far_ref, ...), custom_call_target="tpu_custom_call" | custom-call | flops 100000000 | bytes 1000000 | tf_op jit(solution)/shard_map/prints/pallas_call | solution.py:320
  34.3 3.6 %collective-permute-done.7.refs_1_ = s16[2,4,128,128]{3,2,1,0:T(8,128)(2,1)S(1)} collective-permute-done((s16[2,4,128,128]{3,2,1,0:T(8,128)(2,1)S(1)}, s16[2,4,128,128]{3,2,1,0:T(8,128)(2,1)S(1)}, u32[]{:S(2)}, u32[]{:S(2)}) %collective-permute-start.7) | collective-permute-done | bytes 262176 | tf_op jit(solution)/shard_map/ppermute | solution.py:374
  37.9 1.1 %early.1.mix_ref = f32[2,8,128,128]{3,2,1,0:T(8,128)S(1)} custom-call(s32[2,4]{1,0:T(2,128)S(1)} %copy-done.1, f32[2,4,128,128]{3,2,1,0:T(8,128)S(1)} %prints.11.own_ref, s16[4,192,128]{2,1,0:T(8,128)(2,1)S(1)} %collective-permute-done.5.over_ref, f32[2,4,128,128]{3,2,1,0:T(8,128)S(1)} %opened.1.refs_0_, ...), custom_call_target="tpu_custom_call" | custom-call | flops 100000000 | bytes 1000000 | tf_op jit(solution)/shard_map/early/pallas_call | solution.py:350
  39.0 4.4 %collective-permute-done.8.layer_ref = s16[2,4,128,128]{3,2,1,0:T(8,128)(2,1)S(1)} collective-permute-done((s16[2,4,128,128]{3,2,1,0:T(8,128)(2,1)S(1)}, s16[2,4,128,128]{3,2,1,0:T(8,128)(2,1)S(1)}, u32[]{:S(2)}, u32[]{:S(2)}) %collective-permute-start.8) | collective-permute-done | bytes 262176 | tf_op jit(solution)/shard_map/ppermute | solution.py:374
  43.7 10.7 %all_to_all.5.blocks_ref = s16[8,2,4,16,128]{4,3,2,1,0:T(8,128)(2,1)S(1)} all-to-all(s16[8,2,4,16,128]{4,3,2,1,0:T(8,128)(2,1)S(1)} %final.1), channel_id=1, replica_groups=mesh['depth'=4,'tile'=8] {'tile'}, dimensions={0} | all-to-all | bytes 524288 | tf_op jit(solution)/shard_map/all_to_all | solution.py:421
  54.4 0.9 %place.1 = f32[2,4,16,1024]{3,2,1,0:T(8,128)} custom-call(s16[8,2,4,16,128]{4,3,2,1,0:T(8,128)(2,1)S(1)} %all_to_all.5.blocks_ref), custom_call_target="tpu_custom_call" | custom-call | tf_op jit(solution)/shard_map/place/pallas_call | solution.py:367
  (23 shorter events, 1.9 us)
Async XLA Ops:
  0.0 8.6 %copy-start = (f32[2,3]{1,0:T(2,128)S(1)}, f32[2,3]{1,0:T(2,128)}, u32[]{:S(2)}) copy-start(f32[2,3]{1,0:T(2,128)} %light_ref.1) | copy-start | bytes 76
  0.0 8.6 %copy-start.2 = (f32[4]{0:T(128)S(1)}, f32[4]{0:T(128)}, u32[]{:S(2)}) copy-start(f32[4]{0:T(128)} %param.10) | copy-start | bytes 52
  0.0 8.6 %copy-start.3 = (f32[4]{0:T(128)S(1)}, f32[4]{0:T(128)}, u32[]{:S(2)}) copy-start(f32[4]{0:T(128)} %param.11) | copy-start | bytes 52
  0.0 1.6 %copy-start.4 = (bf16[512,16,128]{2,1,0:T(8,128)(2,1)S(1)}, bf16[512,16,128]{2,1,0:T(8,128)(2,1)}, u32[]{:S(2)}) copy-start(bf16[512,16,128]{2,1,0:T(8,128)(2,1)} %volume_ref.1) | copy-start | bytes 6291460
  3.9 6.2 %collective-permute-start = (bf16[16,512]{1,0:T(8,128)(2,1)S(1)}, bf16[16,512]{1,0:T(8,128)(2,1)S(1)}, u32[]{:S(2)}, u32[]{:S(2)}) collective-permute-start(bf16[16,512]{1,0:T(8,128)(2,1)S(1)} %get-tuple-element.29), channel_id=1, source_target_pairs={{0,1},{1,0},{2,3},{3,2},{4,5},{5,4},{6,7},{7,6},{8,9},{9,8},{10,11... | collective-permute-start | bytes 49160 | tf_op jit(solution)/shard_map/ppermute | solution.py:380
  4.4 5.7 %collective-permute-start.1 = (bf16[16,512]{1,0:T(8,128)(2,1)S(1)}, bf16[16,512]{1,0:T(8,128)(2,1)S(1)}, u32[]{:S(2)}, u32[]{:S(2)}) collective-permute-start(bf16[16,512]{1,0:T(8,128)(2,1)S(1)} %get-tuple-element.30), channel_id=1, source_target_pairs={{0,7},{1,2},{2,1},{3,4},{4,3},{5,6},{6,5},{7,0},{8,15},{9,10},{10,... | collective-permute-start | bytes 49160 | tf_op jit(solution)/shard_map/ppermute | solution.py:380
  11.1 6.0 %collective-permute-start.2 = (s16[4,192,128]{2,1,0:T(8,128)(2,1)S(1)}, s16[4,192,128]{2,1,0:T(8,128)(2,1)S(1)}, u32[]{:S(2)}, u32[]{:S(2)}) collective-permute-start(s16[4,192,128]{2,1,0:T(8,128)(2,1)S(1)} %prints.6.after_ref), channel_id=1, source_target_pairs={{0,1},{1,2},{2,3},{3,4},{4,5},{5,6},{6,7},{7,0},{8,9},{9,10},{10,1... | collective-permute-start | bytes 589832 | tf_op jit(solution)/shard_map/ppermute | solution.py:374
  17.4 16.7 %collective-permute-start.6 = (s16[2,4,128,128]{3,2,1,0:T(8,128)(2,1)S(1)}, s16[2,4,128,128]{3,2,1,0:T(8,128)(2,1)S(1)}, u32[]{:S(2)}, u32[]{:S(2)}) collective-permute-start(s16[2,4,128,128]{3,2,1,0:T(8,128)(2,1)S(1)} %merge.3.after_ref), channel_id=1, source_target_pairs={{0,16},{8,24},{16,0},{24,8},{1,17},{9,25},{17,1},{25,9},{2,18},{10... | collective-permute-start | bytes 786440 | tf_op jit(solution)/shard_map/ppermute | solution.py:374
  20.1 6.4 %collective-permute-start.4 = (s16[4,192,128]{2,1,0:T(8,128)(2,1)S(1)}, s16[4,192,128]{2,1,0:T(8,128)(2,1)S(1)}, u32[]{:S(2)}, u32[]{:S(2)}) collective-permute-start(s16[4,192,128]{2,1,0:T(8,128)(2,1)S(1)} %get-tuple-element.43), channel_id=1, source_target_pairs={{0,1},{1,2},{2,3},{3,4},{4,5},{5,6},{6,7},{7,0},{8,9},{9,10},{10,1... | collective-permute-start | bytes 589832 | tf_op jit(solution)/shard_map/ppermute | solution.py:374
  24.0 6.0 %collective-permute-start.3 = (s16[4,192,128]{2,1,0:T(8,128)(2,1)S(1)}, s16[4,192,128]{2,1,0:T(8,128)(2,1)S(1)}, u32[]{:S(2)}, u32[]{:S(2)}) collective-permute-start(s16[4,192,128]{2,1,0:T(8,128)(2,1)S(1)} %get-tuple-element.42), channel_id=1, source_target_pairs={{0,1},{1,2},{2,3},{3,4},{4,5},{5,6},{6,7},{7,0},{8,9},{9,10},{10,1... | collective-permute-start | bytes 589832 | tf_op jit(solution)/shard_map/ppermute | solution.py:374
  26.8 11.1 %collective-permute-start.7 = (s16[2,4,128,128]{3,2,1,0:T(8,128)(2,1)S(1)}, s16[2,4,128,128]{3,2,1,0:T(8,128)(2,1)S(1)}, u32[]{:S(2)}, u32[]{:S(2)}) collective-permute-start(s16[2,4,128,128]{3,2,1,0:T(8,128)(2,1)S(1)} %merge.4.after_ref), channel_id=1, source_target_pairs={{0,8},{8,16},{16,24},{24,0},{1,9},{9,17},{17,25},{25,1},{2,10},{10... | collective-permute-start | bytes 786440 | tf_op jit(solution)/shard_map/ppermute | solution.py:374
  30.4 7.5 %collective-permute-start.5 = (s16[4,192,128]{2,1,0:T(8,128)(2,1)S(1)}, s16[4,192,128]{2,1,0:T(8,128)(2,1)S(1)}, u32[]{:S(2)}, u32[]{:S(2)}) collective-permute-start(s16[4,192,128]{2,1,0:T(8,128)(2,1)S(1)} %get-tuple-element.48), channel_id=1, source_target_pairs={{0,1},{1,2},{2,3},{3,4},{4,5},{5,6},{6,7},{7,0},{8,9},{9,10},{10,1... | collective-permute-start | bytes 589832 | tf_op jit(solution)/shard_map/ppermute | solution.py:374
  30.4 12.9 %collective-permute-start.8 = (s16[2,4,128,128]{3,2,1,0:T(8,128)(2,1)S(1)}, s16[2,4,128,128]{3,2,1,0:T(8,128)(2,1)S(1)}, u32[]{:S(2)}, u32[]{:S(2)}) collective-permute-start(s16[2,4,128,128]{3,2,1,0:T(8,128)(2,1)S(1)} %get-tuple-element.47.after_ref), channel_id=1, source_target_pairs={{0,24},{8,0},{16,8},{24,16},{1,25},{9,1},{17,9},{25,17},{2,26},{10... | collective-permute-start | bytes 786440 | tf_op jit(solution)/shard_map/ppermute | solution.py:374
  34.1 3.8 %copy-start.1 = (s32[2,4]{1,0:T(2,128)S(1)}, s32[2,4]{1,0:T(2,128)}, u32[]{:S(2)}) copy-start(s32[2,4]{1,0:T(2,128)} %order_ref.1) | copy-start | bytes 100
